TPU v7x, 128 devices: a whole 4x4x4 slice. The times are simulated.
128 devices in a mesh: dp: 8 (over z, core), sec: 2 (over x_hi), vocab: 8 (over x_lo, y).
Axes of the slice: x: 4 (x_hi: 2, x_lo: 2; x = x_hi * 2 + x_lo), y: 4, z: 4, core: 2. Of those that a mesh axis runs over, the one named last changes fastest.
Arguments:
- teacher_hidden: bfloat16 [2, 256, 4608], P(None, 'dp'), may hold values from -410 to 410
- student_hidden: bfloat16 [2, 256, 3584], P(None, 'dp'), may hold values from -410 to 410
- teacher_gain: float32 [4608], replicated, may hold values from 0.5 to 1.5
- student_gain: float32 [3584], replicated, may hold values from 0.5 to 1.5
- teacher_head: bfloat16 [4608, 131072], P(None, ('dp', 'sec', 'vocab')), may hold values from -2 to 2
- student_head: bfloat16 [3584, 131072], P(None, ('dp', 'sec', 'vocab')), may hold values from -2 to 2
- labels: int32 [2, 256], replicated, may hold values from 0 to 131071
Outputs:
- row_loss: float32 [2, 256], P(None, 'dp')
- grad_hidden: bfloat16 [2, 256, 3584], P(None, 'dp')
- grad_head: bfloat16 [3584, 131072], P(None, ('dp', 'sec', 'vocab'))
All inputs are finite; a program needn't handle non-finite values.
Results may differ from a plain program's by a relative error of at most 0.0015.
The roundings to bfloat16 on the way count: a program that leaves them out, or rounds other values in their place, can miss the bound.
Values may be sent and summed in bfloat16 or wider, within the bound.
No kernel may reach another device: no remote copies, remote signals or barrier semaphores. Data moves between devices by JAX's collectives and lax.ppermute only.
A program may use at most 128 MiB of HBM per device.

v0:
```python
import jax
import jax.numpy as jnp
from jax import lax
from jax.sharding import PartitionSpec as P

SOFT_CAP = 30.0
KL_WEIGHT = 0.5
NORM_EPS = 1e-06


def normalize(hidden, gain):
    values = hidden.astype(jnp.float32)
    factor = lax.rsqrt(jnp.mean(values * values, axis=-1, keepdims=True) + NORM_EPS)
    return ((values * factor * gain).astype(jnp.bfloat16), factor)


def capped_logits(normed, head_cols):
    return SOFT_CAP * jnp.tanh(
        jnp.dot(normed, head_cols, preferred_element_type=jnp.float32) / SOFT_CAP
    )


def back_rows(logit_rows, head_cols):
    return lax.dot_general(
        logit_rows, head_cols, (((1,), (1,)), ((), ())), preferred_element_type=jnp.float32
    )


def norm_backward(hidden, factor, gain, upstream):
    values = hidden.astype(jnp.float32)
    scaled = upstream * gain
    inner_sum = jnp.mean(values * scaled, axis=-1, keepdims=True)
    return factor * scaled - values * (factor * factor * factor) * inner_sum


def own_rows(values, own_start, row_count):
    return lax.dynamic_slice_in_dim(values, own_start, row_count, 0)


def body(
    teacher_hidden, student_hidden, teacher_gain, student_gain, teacher_head, student_head, labels
):
    batches = teacher_hidden.shape[0]
    local_rows = student_hidden.shape[1]
    col_count = student_head.shape[1]
    device_place = lax.axis_index(("dp", "sec", "vocab"))
    columns = device_place * col_count + lax.broadcasted_iota(jnp.int32, (1, col_count), 1)
    own_start = lax.axis_index("dp") * local_rows
    head_grad = jnp.zeros(student_head.shape, jnp.float32)
    losses = []
    hidden_grads = []
    for member in range(batches):
        teacher_rows, student_rows = (
            lax.all_gather(teacher_hidden[member], "dp", axis=0, tiled=True),
            lax.all_gather(student_hidden[member], "dp", axis=0, tiled=True),
        )
        teacher_normed, _ = normalize(teacher_rows, teacher_gain)
        student_normed, student_factor = normalize(student_rows, student_gain)
        teacher_cap = capped_logits(teacher_normed, teacher_head)
        student_cap = capped_logits(student_normed, student_head)
        teacher_exp = jnp.exp(teacher_cap)
        student_exp = jnp.exp(student_cap)
        matches = labels[member][:, None] == columns
        teacher_part = jnp.sum(teacher_exp, axis=1)
        student_part = jnp.sum(student_exp, axis=1)
        cross_part = jnp.sum(teacher_exp * (teacher_cap - student_cap), axis=1)
        picked_part = jnp.sum(jnp.where(matches, student_cap, jnp.float32(0.0)), axis=1)
        teacher_total, student_total, cross_total, picked_total = lax.psum(
            (teacher_part, student_part, cross_part, picked_part), ("dp", "sec", "vocab")
        )
        ratio = student_cap / SOFT_CAP
        logit_grad = (
            student_exp / student_total[:, None]
            - KL_WEIGHT * teacher_exp / teacher_total[:, None]
            - (1.0 - KL_WEIGHT) * matches.astype(jnp.float32)
        ) * (1.0 - ratio * ratio)
        logit_grad = logit_grad.astype(jnp.bfloat16)
        summed = lax.psum(back_rows(logit_grad, student_head), ("dp", "sec", "vocab"))
        upstream = own_rows(summed, own_start, local_rows)
        head_grad = head_grad + lax.dot_general(
            student_normed, logit_grad, (((0,), (0,)), ((), ())), preferred_element_type=jnp.float32
        )
        teacher_mine = own_rows(teacher_total, own_start, local_rows)
        student_mine = own_rows(student_total, own_start, local_rows)
        cross_mine = own_rows(cross_total, own_start, local_rows)
        picked_mine = own_rows(picked_total, own_start, local_rows)
        divergence = cross_mine / teacher_mine - jnp.log(teacher_mine) + jnp.log(student_mine)
        label_term = jnp.log(student_mine) - picked_mine
        losses.append(KL_WEIGHT * divergence + (1.0 - KL_WEIGHT) * label_term)
        factor_mine = own_rows(student_factor, own_start, local_rows)
        hidden_grads.append(
            norm_backward(student_hidden[member], factor_mine, student_gain, upstream).astype(
                jnp.bfloat16
            )
        )
    return (jnp.stack(losses), jnp.stack(hidden_grads), head_grad.astype(jnp.bfloat16))


def solution(mesh):
    in_specs = (
        P(None, "dp", None),
        P(None, "dp", None),
        P(),
        P(),
        P(None, ("dp", "sec", "vocab")),
        P(None, ("dp", "sec", "vocab")),
        P(),
    )
    out_specs = (P(None, "dp"), P(None, "dp", None), P(None, ("dp", "sec", "vocab")))
    return jax.shard_map(body, mesh=mesh, in_specs=in_specs, out_specs=out_specs, check_vma=False)
```

profile of v0, /device:TPU:0, one launch (start us, length us, event | category | flops | bytes accessed | tf_op | source)
XLA Modules:
  0.0 381.7 jit_solution(2706245771740958057)
XLA Ops:
  7.2 1.9 fusion.74
  9.9 1.9 fusion.73
  12.5 0.8 fusion.75
  13.3 24.1 %all-gather.15.cloned.1.call-done = bf16[1,256,3584]{2,1,0:T(8,128)(2,1)} async-done(((bf16[1,32,3584]{2,1,0:T(8,128)(2,1)}), bf16[1,256,3584]{2,1,0:T(8,128)(2,1)}) %all-gather.15.cloned.1.call-update) | async-done | bytes 1835024 | tf_op jit(solution)/shard_map/all_gather | solution.py:55
  37.3 1.9 fusion.9
  39.3 25.6 %all-gather.11.cloned.1.call-done = bf16[1,256,3584]{2,1,0:T(8,128)(2,1)} async-done(((bf16[1,32,3584]{2,1,0:T(8,128)(2,1)}), bf16[1,256,3584]{2,1,0:T(8,128)(2,1)}) %all-gather.11.cloned.1.call-update) | async-done | bytes 1835024 | tf_op jit(solution)/shard_map/all_gather | solution.py:55
  64.9 2.1 fusion.6
  67.1 5.9 %fusion.41 = f32[256,1024]{1,0:T(8,128)S(1)} fusion(bf16[3584,1024]{1,0:T(8,128)(2,1)} %param.12, bf16[1,256,3584]{2,1,0:T(8,128)(2,1)} %all-gather.11.cloned.1.call-done, f32[3584]{0:T(1024)S(1)} %copy-done.12, f32[256]{0:T(256)S(1)} %add_rsqrt_fusion.2), kind=kOutput, calls=%fused_computation.38 | convolution fusion | flops 1882980352 | bytes 10238976 | tf_op jit(solution)/shard_map/dot_general | solution.py:19
  73.0 3.2 fusion.40
  76.2 16.4 %all-gather.13.cloned.1.call-done = bf16[1,256,4608]{2,1,0:T(8,128)(2,1)} async-done(((bf16[1,32,4608]{2,1,0:T(8,128)(2,1)}), bf16[1,256,4608]{2,1,0:T(8,128)(2,1)}) %all-gather.13.cloned.1.call-update) | async-done | bytes 2359312 | tf_op jit(solution)/shard_map/all_gather | solution.py:54
  92.6 2.4 fusion.3
  95.0 26.0 %all-gather.9.cloned.1.call-done = bf16[1,256,4608]{2,1,0:T(8,128)(2,1)} async-done(((bf16[1,32,4608]{2,1,0:T(8,128)(2,1)}), bf16[1,256,4608]{2,1,0:T(8,128)(2,1)}) %all-gather.9.cloned.1.call-update) | async-done | bytes 2359312 | tf_op jit(solution)/shard_map/all_gather | solution.py:54
  121.0 2.4 fusion
  123.4 5.4 %fusion.31 = f32[256,1024]{1,0:T(8,128)S(1)} fusion(bf16[4608,1024]{1,0:T(8,128)(2,1)} %param.11, bf16[1,256,4608]{2,1,0:T(8,128)(2,1)S(1)} %copy-done.5, f32[256]{0:T(256)S(1)} %add_rsqrt_fusion.1, f32[4608]{0:T(1024)S(1)} %copy-done.13), kind=kOutput, calls=%fused_computation.32 | convolution fusion | flops 2421161984 | bytes 12864512 | tf_op jit(solution)/shard_map/dot_general | solution.py:19
  129.6 3.8 multiply_reduce_fusion.1
  133.4 65.8 %all-reduce = (f32[256]{0:T(256)S(1)}, f32[256]{0:T(256)S(1)}, f32[256]{0:T(256)S(1)}, f32[256]{0:T(256)S(1)}, f32[256]{0:T(256)S(1)}, /*index=5*/f32[256]{0:T(256)S(1)}, f32[256]{0:T(256)S(1)}, f32[256]{0:T(256)S(1)}) all-reduce(f32[256]{0:T(256)S(1)} %get-tuple-element.34, ...), channel_id=1, replica_groups=mesh['dp'=8,'sec'=2,'vocab'=8] {'dp','sec','vocab'}, use_global_device_ids=true, to_apply=%region_19.20 | all-reduce | flops 2048 | bytes 16384 | tf_op jit(solution)/shard_map/psum | solution.py:68
  199.2 7.8 %fusion.68 = f32[256,3584]{1,0:T(8,128)} fusion(bf16[3584,1024]{1,0:T(8,128)(2,1)} %param.12, f32[256,1024]{1,0:T(8,128)S(1)} %copy-done.8, f32[256,1024]{1,0:T(8,128)} %copy-done.10, f32[256]{0:T(256)S(1)} %get-tuple-element.15, f32[256]{0:T(256)S(1)} %get-tuple-element.14, s32[1024]{0:T(1024)S(1)} %iota_add_fusion, s32[256]{0:T(256)S(1)} %bitcast.76), kind=kOutput, calls=%fused_computation.89 | convolution fusion | flops 1882193920 | bytes 13114368 | tf_op jit(solution)/shard_map/dot_general | solution.py:24
  207.0 7.4 %fusion.71 = f32[256,3584]{1,0:T(8,128)} fusion(bf16[3584,1024]{1,0:T(8,128)(2,1)} %param.12, f32[256,1024]{1,0:T(8,128)S(1)} %fusion.41, f32[256,1024]{1,0:T(8,128)S(1)} %get-tuple-element.39, f32[256]{0:T(256)S(1)} %get-tuple-element.19, f32[256]{0:T(256)S(1)} %get-tuple-element.18, s32[1024]{0:T(1024)S(1)} %iota_add_fusion, s32[256]{0:T(256)S(1)} %bitcast.73), kind=kOutput, calls=%fused_computation.90 | convolution fusion | flops 1882193920 | bytes 13114368 | tf_op jit(solution)/shard_map/dot_general | solution.py:24
  216.0 9.2 %fusion.52 = f32[3584,1024]{1,0:T(8,128)} fusion(bf16[1,256,3584]{2,1,0:T(8,128)(2,1)S(1)} %copy-done, f32[3584]{0:T(1024)S(1)} %copy-done.12, f32[256]{0:T(256)S(1)} %add_rsqrt_fusion.2, f32[256,1024]{1,0:T(8,128)S(1)} %fusion.41, f32[256,1024]{1,0:T(8,128)} %copy-done.6, f32[256]{0:T(256)S(1)} %get-tuple-element.19, f32[256]{0:T(256)S(1)} %get-tuple-element.18, ...), kind=kOutput, calls=%fused_computation.61 | convolution fusion | flops 1885863936 | bytes 18634752 | tf_op jit(solution)/shard_map/dot_general | solution.py:80
  225.2 9.1 %add_convert_fusion = bf16[3584,1024]{1,0:T(8,128)(2,1)} fusion(f32[3584,1024]{1,0:T(8,128)} %fusion.52, bf16[1,256,3584]{2,1,0:T(8,128)(2,1)S(1)} %copy-done.2, f32[256]{0:T(256)S(1)} %add_rsqrt_fusion, f32[3584]{0:T(1024)S(1)} %copy-done.12, f32[256,1024]{1,0:T(8,128)S(1)} %copy-done.9, f32[256,1024]{1,0:T(8,128)S(1)} %copy-done.11, ...), kind=kOutput, calls=%fused_computation | convolution fusion | flops 1893203968 | bytes 25974784 | tf_op jit(solution)/shard_map/dot_general | solution.py:80
  234.3 137.3 %all-reduce.4.cloned.1.call-done = (f32[256,3584]{1,0:T(8,128)}, f32[256,3584]{1,0:T(8,128)}) async-done(((f32[256,3584]{1,0:T(8,128)}, f32[256,3584]{1,0:T(8,128)}), (f32[256,3584]{1,0:T(8,128)}, f32[256,3584]{1,0:T(8,128)})) %all-reduce.4.cloned.1.call-update) | async-done | bytes 7340048 | tf_op jit(solution)/shard_map/psum | solution.py:78
  371.5 1.4 fusion.58
  372.9 1.4 fusion.64
  374.3 0.8 pad_maximum_fusion
  (59 shorter events, 3.8 us)
Async XLA Ops:
  7.2 59.9 %copy-start.12 = (f32[3584]{0:T(1024)S(1)}, f32[3584]{0:T(1024)}, u32[]{:S(2)}) copy-start(f32[3584]{0:T(1024)} %param.10) | copy-start | bytes 43012
  7.2 30.2 %all-gather.15.cloned.1.call-start = ((), (), s32[]{:S(2)}) async-start(), calls=%async_computation.3 | async-start | bytes 2064384 | tf_op jit(solution)/shard_map/all_gather | solution.py:55
  9.1 55.8 %all-gather.11.cloned.1.call-start = ((), (), s32[]{:S(2)}) async-start(), calls=%async_computation.1 | async-start | bytes 2064384 | tf_op jit(solution)/shard_map/all_gather | solution.py:55
  9.9 82.8 %all-gather.13.cloned.1.call-start = ((), (), s32[]{:S(2)}) async-start(), calls=%async_computation.2 | async-start | bytes 2654208 | tf_op jit(solution)/shard_map/all_gather | solution.py:54
  11.8 109.1 %all-gather.9.cloned.1.call-start = ((), (), s32[]{:S(2)}) async-start(), calls=%async_computation | async-start | bytes 2654208 | tf_op jit(solution)/shard_map/all_gather | solution.py:54
  12.4 359.1 %all-reduce.4.cloned.1.call-start = ((), (), s32[]{:S(2)}) async-start(), calls=%async_computation.4 | async-start | bytes 14680064 | tf_op jit(solution)/shard_map/psum | solution.py:78
  64.9 8.1 %slice-start.3 = ((s8[7340032]{0:T(1024)(128)(4,1)}), s8[4194304]{0:T(1024)(128)(4,1)S(1)}, s32[]{:S(2)}) async-start(s8[7340032]{0:T(1024)(128)(4,1)} %bitcast.80), calls=%async_computation.8 | async-start | bytes 8388608
  67.0 6.0 %copy-start.1 = (bf16[1,256,3584]{2,1,0:T(8,128)(2,1)S(1)}, bf16[1,256,3584]{2,1,0:T(8,128)(2,1)}, u32[]{:S(2)}) copy-start(bf16[1,256,3584]{2,1,0:T(8,128)(2,1)} %all-gather.15.cloned.1.call-done) | copy-start | bytes 5505028
  67.0 6.0 %slice-start.4 = ((s8[7340032]{0:T(1024)(128)(4,1)}), s8[3145728]{0:T(1024)(128)(4,1)S(1)}, s32[]{:S(2)}) async-start(s8[7340032]{0:T(1024)(128)(4,1)} %bitcast.80), calls=%async_computation.9 | async-start | bytes 6291456
  76.2 47.2 %copy-start.13 = (f32[4608]{0:T(1024)S(1)}, f32[4608]{0:T(1024)}, u32[]{:S(2)}) copy-start(f32[4608]{0:T(1024)} %param.9) | copy-start | bytes 55300
  92.6 30.7 %copy-start.5 = (bf16[1,256,4608]{2,1,0:T(8,128)(2,1)S(1)}, bf16[1,256,4608]{2,1,0:T(8,128)(2,1)}, u32[]{:S(2)}) copy-start(bf16[1,256,4608]{2,1,0:T(8,128)(2,1)} %all-gather.13.cloned.1.call-done) | copy-start | bytes 7077892
  121.0 7.9 %slice-start = ((s8[9437184]{0:T(1024)(128)(4,1)}), s8[4194304]{0:T(1024)(128)(4,1)S(1)}, s32[]{:S(2)}) async-start(s8[9437184]{0:T(1024)(128)(4,1)} %bitcast.78), calls=%async_computation.5 | async-start | bytes 8388608
  123.4 5.5 %copy-start.4 = (bf16[1,256,4608]{2,1,0:T(8,128)(2,1)S(1)}, bf16[1,256,4608]{2,1,0:T(8,128)(2,1)}, u32[]{:S(2)}) copy-start(bf16[1,256,4608]{2,1,0:T(8,128)(2,1)} %all-gather.9.cloned.1.call-done) | copy-start | bytes 7077892
  123.4 5.5 %copy-start.7 = (f32[256,1024]{1,0:T(8,128)S(1)}, f32[256,1024]{1,0:T(8,128)}, u32[]{:S(2)}) copy-start(f32[256,1024]{1,0:T(8,128)} %fusion.40) | copy-start | bytes 3145732
  123.4 6.0 %slice-start.1 = ((s8[9437184]{0:T(1024)(128)(4,1)}), s8[4194304]{0:T(1024)(128)(4,1)S(1)}, s32[]{:S(2)}) async-start(s8[9437184]{0:T(1024)(128)(4,1)} %bitcast.78), calls=%async_computation.6 | async-start | bytes 8388608
  123.4 6.2 %slice-start.2 = ((s8[9437184]{0:T(1024)(128)(4,1)}), s8[1048576]{0:T(1024)(128)(4,1)S(1)}, s32[]{:S(2)}) async-start(s8[9437184]{0:T(1024)(128)(4,1)} %bitcast.78), calls=%async_computation.7 | async-start | bytes 2097152
  128.8 4.6 %copy-start.10 = (f32[256,1024]{1,0:T(8,128)}, f32[256,1024]{1,0:T(8,128)S(1)}, u32[]{:S(2)}) copy-start(f32[256,1024]{1,0:T(8,128)S(1)} %fusion.31) | copy-start | bytes 3145732
  129.6 69.6 %copy-start.8 = (f32[256,1024]{1,0:T(8,128)S(1)}, f32[256,1024]{1,0:T(8,128)}, u32[]{:S(2)}) copy-start(f32[256,1024]{1,0:T(8,128)} %fusion.40) | copy-start | bytes 3145732
  133.4 73.6 %copy-start.6 = (f32[256,1024]{1,0:T(8,128)}, f32[256,1024]{1,0:T(8,128)S(1)}, u32[]{:S(2)}) copy-start(f32[256,1024]{1,0:T(8,128)S(1)} %get-tuple-element.39) | copy-start | bytes 3145732
  214.5 1.5 copy-start
  216.0 9.2 %copy-start.2 = (bf16[1,256,3584]{2,1,0:T(8,128)(2,1)S(1)}, bf16[1,256,3584]{2,1,0:T(8,128)(2,1)}, u32[]{:S(2)}) copy-start(bf16[1,256,3584]{2,1,0:T(8,128)(2,1)} %all-gather.15.cloned.1.call-done) | copy-start | bytes 5505028
  216.0 9.2 %copy-start.9 = (f32[256,1024]{1,0:T(8,128)S(1)}, f32[256,1024]{1,0:T(8,128)}, u32[]{:S(2)}) copy-start(f32[256,1024]{1,0:T(8,128)} %fusion.40) | copy-start | bytes 3145732
  216.0 9.2 %copy-start.11 = (f32[256,1024]{1,0:T(8,128)S(1)}, f32[256,1024]{1,0:T(8,128)}, u32[]{:S(2)}) copy-start(f32[256,1024]{1,0:T(8,128)} %copy-done.10) | copy-start | bytes 3145732
  225.2 146.4 %copy-start.3 = (bf16[2,32,3584]{2,1,0:T(8,128)(2,1)S(1)}, bf16[2,32,3584]{2,1,0:T(8,128)(2,1)}, u32[]{:S(2)}) copy-start(bf16[2,32,3584]{2,1,0:T(8,128)(2,1)} %param.8) | copy-start | bytes 1376260
Sparse Core Ops, SparseCore 0:
  9.7 27.6 all-gather.14
  39.6 25.2 all-gather.10
  66.6 25.9 all-gather.12
  94.7 26.2 all-gather.8
  214.6 156.8 all-reduce.3
where the time goes:
time: 383 us; the launch traced here: 382 us
  waiting for transfers between devices  231 us (60%)
  blocking collectives  65.8 us (17%)
  matrix products  51.8 us (14%)
  between operations  14 us (4%)
  other arithmetic  13.1 us (3%)
  local copies, waits for them, and re-layouts  6.09 us (2%)
    psum x1, waiting for transfers between devices, body(): lax.psum(back_rows(logit_grad, student_head), ('dp', 'sec', 'vocab'))  137 us
    psum x1, blocking collectives, body(): lax.psum((teacher_part, student_part, cross_part, picked_part), ('dp', 's...  65.8 us
    all_gather x2, waiting for transfers between devices, body(): lax.all_gather(student_hidden[member], 'dp', axis=0, tiled=True)  49.7 us
    all_gather x2, waiting for transfers between devices, body(): lax.all_gather(teacher_hidden[member], 'dp', axis=0, tiled=True)  42.4 us
    dot_general x4, matrix products, capped_logits(): jnp.dot(normed, head_cols, preferred_element_type=jnp.float32) / SOFT_CAP  18.3 us
    dot_general x2, matrix products, body(): lax.dot_general(student_normed, logit_grad, (((0,), (0,)), ((), ())), pre...  18.2 us
    dot_general x2, matrix products, back_rows(): lax.dot_general(logit_rows, head_cols, (((1,), (1,)), ((), ())), preferre...  15.3 us
    reduce_sum x4, other arithmetic, normalize(): jnp.mean(values * values, axis=-1, keepdims=True) + NORM_EPS  8.75 us
  transfers between devices with their start and end apart: 5, of which 5 were waited for; matrix products, arithmetic and copies ran while one was open for 10% of the time, Pallas kernels for 0%

commit v1 on v0

v1 whole, which is shorter than its diff:
```python
import jax
import jax.numpy as jnp
from jax import lax
from jax.sharding import PartitionSpec as P

SOFT_CAP = 30.0
KL_WEIGHT = 0.5
NORM_EPS = 1e-06
AXES = ("dp", "sec", "vocab")
PLANE = ("sec", "vocab")
CHIPS = [[(2 * z + core) * 16 + place for z in range(4) for place in range(16)] for core in range(2)]
SIBLING = [(i, i ^ 1) for i in range(8)]


def row_factor(values):
    return lax.rsqrt(jnp.mean(values * values, axis=-1, keepdims=True) + NORM_EPS)


def capped_logits(normed, head_cols):
    return SOFT_CAP * jnp.tanh(
        jnp.dot(normed, head_cols, preferred_element_type=jnp.float32) / SOFT_CAP
    )


def back_rows(logit_rows, head_cols):
    return lax.dot_general(
        logit_rows, head_cols, (((1,), (1,)), ((), ())), preferred_element_type=jnp.float32
    )


def sum_everywhere(part):
    chip = part + lax.ppermute(part, "dp", SIBLING)
    copies = jnp.broadcast_to(chip.reshape(1, 8, 128), (64, 8, 128))
    got = lax.all_to_all(copies, AXES, 0, 0, tiled=True, axis_index_groups=CHIPS)
    return jnp.sum(got, axis=0).reshape(part.shape)


def body(
    teacher_hidden, student_hidden, teacher_gain, student_gain, teacher_head, student_head, labels
):
    batches, local_rows, d_t = teacher_hidden.shape
    d_s = student_hidden.shape[2]
    col_count = student_head.shape[1]
    device_place = lax.axis_index(AXES)
    columns = device_place * col_count + lax.broadcasted_iota(jnp.int32, (1, col_count), 1)
    dp = lax.axis_index("dp")
    core = dp % 2
    teacher_values = teacher_hidden.astype(jnp.float32)
    student_values = student_hidden.astype(jnp.float32)
    teacher_own = (teacher_values * row_factor(teacher_values) * teacher_gain).astype(jnp.bfloat16)
    student_factor = row_factor(student_values)
    student_own = (student_values * student_factor * student_gain).astype(jnp.bfloat16)
    both_own = jnp.concatenate([teacher_own, student_own], axis=2)
    losses, hidden_grads, normed_parts, grad_parts = [], [], [], []
    for member in range(batches):
        rows = lax.all_gather(both_own[member], "dp", axis=0, tiled=True)
        student_normed = rows[:, d_t:]
        teacher_cap = capped_logits(rows[:, :d_t], teacher_head)
        student_cap = capped_logits(student_normed, student_head)
        teacher_exp = jnp.exp(teacher_cap)
        student_exp = jnp.exp(student_cap)
        matches = labels[member][:, None] == columns
        part = jnp.stack(
            [
                jnp.sum(teacher_exp, axis=1),
                jnp.sum(student_exp, axis=1),
                jnp.sum(teacher_exp * (teacher_cap - student_cap), axis=1),
                jnp.sum(jnp.where(matches, student_cap, jnp.float32(0.0)), axis=1),
            ]
        )
        totals = sum_everywhere(part)
        teacher_total, student_total = totals[0], totals[1]
        ratio = student_cap / SOFT_CAP
        logit_grad = (
            student_exp / student_total[:, None]
            - KL_WEIGHT * teacher_exp / teacher_total[:, None]
            - (1.0 - KL_WEIGHT) * matches.astype(jnp.float32)
        ) * (1.0 - ratio * ratio)
        logit_grad = logit_grad.astype(jnp.bfloat16)
        normed_parts.append(student_normed)
        grad_parts.append(logit_grad)
        by_core = logit_grad.reshape(4, 2, local_rows, col_count)
        theirs = lax.dynamic_index_in_dim(by_core, 1 - core, 1, keepdims=False)
        mine = lax.dynamic_index_in_dim(by_core, core, 1, keepdims=False)
        theirs_up = back_rows(theirs.reshape(4 * local_rows, col_count), student_head)
        chip_up = back_rows(mine.reshape(4 * local_rows, col_count), student_head)
        chip_up = chip_up + lax.ppermute(theirs_up, "dp", SIBLING)
        pieces = chip_up.reshape(4, 4, 8, 4, d_s // 4).transpose(0, 3, 1, 2, 4)
        pieces = pieces.reshape(64, 8, d_s // 4)
        got = lax.all_to_all(pieces, AXES, 0, 0, tiled=True, axis_index_groups=CHIPS)
        piece = jnp.sum(got, axis=0)
        spread = jnp.broadcast_to(piece[None], (16, 8, d_s // 4))
        spread = lax.all_to_all(spread, PLANE, 0, 0, tiled=True)
        upstream = spread.reshape(4, 4, 8, d_s // 4).transpose(1, 2, 0, 3).reshape(local_rows, d_s)
        factor = student_factor[member]
        values = student_values[member]
        scaled = upstream * student_gain
        inner_sum = jnp.mean(values * scaled, axis=-1, keepdims=True)
        hidden_grads.append(
            (factor * scaled - values * (factor * factor * factor) * inner_sum).astype(jnp.bfloat16)
        )
        own = lax.dynamic_slice_in_dim(totals, dp * local_rows, local_rows, 1)
        divergence = own[2] / own[0] - jnp.log(own[0]) + jnp.log(own[1])
        losses.append(KL_WEIGHT * divergence + (1.0 - KL_WEIGHT) * (jnp.log(own[1]) - own[3]))
    head_grad = lax.dot_general(
        jnp.concatenate(normed_parts, axis=0),
        jnp.concatenate(grad_parts, axis=0),
        (((0,), (0,)), ((), ())),
        preferred_element_type=jnp.float32,
    )
    return (jnp.stack(losses), jnp.stack(hidden_grads), head_grad.astype(jnp.bfloat16))


def solution(mesh):
    in_specs = (
        P(None, "dp", None),
        P(None, "dp", None),
        P(),
        P(),
        P(None, AXES),
        P(None, AXES),
        P(),
    )
    out_specs = (P(None, "dp"), P(None, "dp", None), P(None, AXES))
    return jax.shard_map(body, mesh=mesh, in_specs=in_specs, out_specs=out_specs, check_vma=False)
```

time: 383 us -> 243 us (0.63)
  waiting for transfers between devices: 231 us -> 104 us
  blocking collectives: 65.8 us -> 0 us
  starting transfers between devices: 0.2 us -> 41.3 us
  local copies, waits for them, and re-layouts: 6.09 us -> 16.1 us
  matrix products: 51.8 us -> 55.7 us
    psum x1 -> x0, waiting for transfers between devices: 137 us -> none  [body(): lax.psum(back_rows(logit_grad, student_head), ('dp', 'sec', 'vocab'))]
    psum x1 -> x0, blocking collectives: 65.8 us -> none  [body(): lax.psum((teacher_part, student_part, cross_part, picked_part), ('dp', 's...]
    all_to_all x0 -> x6, waiting for transfers between devices: none -> 55.9 us  [the longest x2 37.3 us: body(): lax.all_to_all(pieces, AXES, 0, 0, tiled=True, axis_index_groups=CHIPS)]
    all_gather x4 -> x2, waiting for transfers between devices: 92.1 us -> 45.6 us  [body(): rows = lax.all_gather(both_own[member], 'dp', axis=0, tiled=True)]
    all_to_all x0 -> x6, starting transfers between devices: none -> 40 us  [the longest x2 18 us: sum_everywhere(): lax.all_to_all(copies, AXES, 0, 0, tiled=True, axis_index_groups=CHIPS)]
    dot_general x4, matrix products: 18.3 us -> 28.2 us  [capped_logits(): jnp.dot(normed, head_cols, preferred_element_type=jnp.float32) / SOFT_CAP]
    dot_general x2 -> x1, matrix products: 18.2 us -> 9.21 us  [body(): lax.dot_general(jnp.concatenate(normed_parts, axis=0), jnp.concatenate(gr...]
    reduce_sum x5 -> x7, other arithmetic: 10.1 us -> 4.6 us  [the longest x2 2.48 us: row_factor(): jnp.mean(values * values, axis=-1, keepdims=True) + NORM_EPS]
  transfers between devices with their start and end apart: 5 -> 12, of which waited for: 5 -> 9; matrix products, arithmetic and copies ran while one was open for 10% -> 23% of each run, Pallas kernels for 0% -> 0%
where the time goes in v1:
time: 243 us; the launch traced here: 242 us
  waiting for transfers between devices  104 us (43%)
  matrix products  55.7 us (23%)
  starting transfers between devices  41.3 us (17%)
  local copies, waits for them, and re-layouts  16.1 us (7%)
  between operations  14.5 us (6%)
  other arithmetic  10.5 us (4%)
    all_gather x2, waiting for transfers between devices, body(): rows = lax.all_gather(both_own[member], 'dp', axis=0, tiled=True)  45.6 us
    all_to_all x2, waiting for transfers between devices, body(): lax.all_to_all(pieces, AXES, 0, 0, tiled=True, axis_index_groups=CHIPS)  37.3 us
    dot_general x4, matrix products, capped_logits(): jnp.dot(normed, head_cols, preferred_element_type=jnp.float32) / SOFT_CAP  28.2 us
    dot_general x4, matrix products, back_rows(): lax.dot_general(logit_rows, head_cols, (((1,), (1,)), ((), ())), preferre...  18.3 us
    all_to_all x2, starting transfers between devices, sum_everywhere(): lax.all_to_all(copies, AXES, 0, 0, tiled=True, axis_index_groups=CHIPS)  18 us
    all_to_all x2, starting transfers between devices, body(): spread = lax.all_to_all(spread, PLANE, 0, 0, tiled=True)  11.2 us
    all_to_all x2, waiting for transfers between devices, sum_everywhere(): lax.all_to_all(copies, AXES, 0, 0, tiled=True, axis_index_groups=CHIPS)  10.9 us
    all_to_all x2, starting transfers between devices, body(): lax.all_to_all(pieces, AXES, 0, 0, tiled=True, axis_index_groups=CHIPS)  10.8 us
  transfers between devices with their start and end apart: 12, of which 9 were waited for; matrix products, arithmetic and copies ran while one was open for 23% of the time, Pallas kernels for 0%

profile of v1, /device:TPU:0, one launch (start us, length us, event | category | flops | bytes accessed | tf_op | source)
XLA Modules:
  0.0 242.1 jit_solution(8435654290262367875)
XLA Ops:
  14.1 34.2 %all-gather.5.cloned.1.call-done = bf16[1,256,8192]{2,1,0:T(8,128)(2,1)} async-done(((bf16[1,32,8192]{2,1,0:T(8,128)(2,1)}), bf16[1,256,8192]{2,1,0:T(8,128)(2,1)}) %all-gather.5.cloned.1.call-update) | async-done | bytes 4194320 | tf_op jit(solution)/shard_map/all_gather | solution.py:56
  48.2 5.9 %fusion.26 = f32[256,1024]{1,0:T(8,128)S(1)} fusion(bf16[3584,1024]{1,0:T(8,128)(2,1)} %param.12, bf16[256,8192]{1,0:T(8,128)(2,1)} %bitcast.89), kind=kOutput, calls=%fused_computation.21 | convolution fusion | flops 1879310336 | bytes 10223616 | tf_op jit(solution)/shard_map/dot_general | solution.py:21
  54.1 8.2 %exponential_reduce_fusion.3 = (f32[256]{0:T(256)S(1)}, f32[256]{0:T(256)S(1)}, f32[256]{0:T(256)S(1)}, f32[256]{0:T(256)S(1)}, f32[256,1024]{1,0:T(8,128)}) fusion(f32[256,1024]{1,0:T(8,128)S(1)} %fusion.26, s32[1024]{0:T(1024)S(1)} %iota_add_fusion, s32[256]{0:T(256)S(1)} %bitcast.114, bf16[4608,1024]{1,0:T(8,128)(2,1)} %param.11, ...), kind=kOutput, calls=%fused_computation.47 | convolution fusion | flops 2418801664 | bytes 13902848 | tf_op jit(solution)/shard_map/dot_general | solution.py:21
  64.3 8.8 %all-to-all-start = ((f32[64,8,128]{2,1,0:T(8,128)}), f32[64,8,128]{2,1,0:T(8,128)S(1)}, u32[]{:S(2)}, u32[]{:S(2)}) async-start(f32[64,8,128]{2,1,0:T(8,128)} %broadcast_in_dim.19), calls=%async_computation | async-start | bytes 524288 | tf_op jit(solution)/shard_map/all_to_all | solution.py:34
  73.1 11.5 %all-gather.7.cloned.1.call-done = bf16[1,256,8192]{2,1,0:T(8,128)(2,1)} async-done(((bf16[1,32,8192]{2,1,0:T(8,128)(2,1)}), bf16[1,256,8192]{2,1,0:T(8,128)(2,1)}) %all-gather.7.cloned.1.call-update) | async-done | bytes 4194320 | tf_op jit(solution)/shard_map/all_gather | solution.py:56
  84.6 5.7 %fusion.25 = f32[256,1024]{1,0:T(8,128)S(1)} fusion(bf16[3584,1024]{1,0:T(8,128)(2,1)} %param.12, bf16[256,8192]{1,0:T(8,128)(2,1)} %bitcast.92), kind=kOutput, calls=%fused_computation.19 | convolution fusion | flops 1879310336 | bytes 10223616 | tf_op jit(solution)/shard_map/dot_general | solution.py:21
  90.4 8.4 %exponential_reduce_fusion.2 = (f32[256]{0:T(256)S(1)}, f32[256]{0:T(256)S(1)}, f32[256]{0:T(256)S(1)}, f32[256]{0:T(256)S(1)}, bf16[256,1024]{1,0:T(8,128)(2,1)S(1)}, /*index=5*/f32[256,1024]{1,0:T(8,128)S(1)}) fusion(f32[256,1024]{1,0:T(8,128)S(1)} %fusion.25, s32[1024]{0:T(1024)S(1)} %iota_add_fusion, s32[256]{0:T(256)S(1)} %bitcast.96, ...), kind=kOutput, calls=%fused_computation.46 | convolution fusion | flops 2421947392 | bytes 16527360 | tf_op jit(solution)/shard_map/dot_general | solution.py:21
  100.9 9.1 %all-to-all-start.1 = ((f32[64,8,128]{2,1,0:T(8,128)}), f32[64,8,128]{2,1,0:T(8,128)S(1)}, u32[]{:S(2)}, u32[]{:S(2)}) async-start(f32[64,8,128]{2,1,0:T(8,128)} %broadcast_in_dim.21), calls=%async_computation.1 | async-start | bytes 524288 | tf_op jit(solution)/shard_map/all_to_all | solution.py:34
  110.1 10.9 %all-to-all-done.1 = f32[64,8,128]{2,1,0:T(8,128)S(1)} async-done(((f32[64,8,128]{2,1,0:T(8,128)}), f32[64,8,128]{2,1,0:T(8,128)S(1)}, u32[]{:S(2)}, u32[]{:S(2)}) %all-to-all-start.1) | async-done | bytes 262176 | tf_op jit(solution)/shard_map/all_to_all | solution.py:34
  122.6 5.7 %fusion.52 = f32[128,3584]{1,0:T(8,128)S(1)} fusion(bf16[128,1024]{1,0:T(8,128)(2,1)S(1)} %bitcast.88, bf16[3584,1024]{1,0:T(8,128)(2,1)} %param.12), kind=kOutput, calls=%fused_computation.93 | convolution fusion | flops 939524096 | bytes 9437184 | tf_op jit(solution)/shard_map/dot_general | solution.py:26
  128.5 3.8 %fusion.51 = f32[128,3584]{1,0:T(8,128)} fusion(bf16[128,1024]{1,0:T(8,128)(2,1)S(1)} %bitcast.87, bf16[3584,1024]{1,0:T(8,128)(2,1)S(1)} %bitcast.78), kind=kOutput, calls=%fused_computation.92 | convolution fusion | flops 939524096 | bytes 9437184 | tf_op jit(solution)/shard_map/dot_general | solution.py:26
  132.7 2.5 %convolution_add_fusion = f32[128,3584]{1,0:T(8,128)S(1)} fusion(f32[128,3584]{1,0:T(8,128)S(1)} %collective-permute-done.3, bf16[128,1024]{1,0:T(8,128)(2,1)S(1)} %bitcast.86, bf16[3584,1024]{1,0:T(8,128)(2,1)S(1)} %bitcast.78), kind=kOutput, calls=%fused_computation.1 | convolution fusion | flops 939982848 | bytes 11272192 | tf_op jit(solution)/shard_map/dot_general | solution.py:26
  136.7 4.9 %all-to-all-start.4 = ((f32[64,8,896]{2,1,0:T(8,128)}), f32[64,8,896]{2,1,0:T(8,128)S(1)}, u32[]{:S(2)}, u32[]{:S(2)}) async-start(f32[64,8,896]{2,1,0:T(8,128)} %bitcast.33), calls=%async_computation.4 | async-start | bytes 3670016 | tf_op jit(solution)/shard_map/all_to_all | solution.py:90
  141.6 6.2 %convolution_add_fusion.1 = f32[128,3584]{1,0:T(8,128)S(1)} fusion(f32[128,3584]{1,0:T(8,128)} %collective-permute-done.2, bf16[128,1024]{1,0:T(8,128)(2,1)S(1)} %bitcast.85, bf16[3584,1024]{1,0:T(8,128)(2,1)} %param.12), kind=kOutput, calls=%fused_computation.2 | convolution fusion | flops 939982848 | bytes 11272192 | tf_op jit(solution)/shard_map/dot_general | solution.py:26
  149.3 19.5 %all-to-all-done.4 = f32[64,8,896]{2,1,0:T(8,128)S(1)} async-done(((f32[64,8,896]{2,1,0:T(8,128)}), f32[64,8,896]{2,1,0:T(8,128)S(1)}, u32[]{:S(2)}, u32[]{:S(2)}) %all-to-all-start.4) | async-done | bytes 1835040 | tf_op jit(solution)/shard_map/all_to_all | solution.py:90
  170.0 5.9 %all-to-all-start.2 = ((f32[64,8,896]{2,1,0:T(8,128)}), f32[64,8,896]{2,1,0:T(8,128)S(1)}, u32[]{:S(2)}, u32[]{:S(2)}) async-start(f32[64,8,896]{2,1,0:T(8,128)} %bitcast.20), calls=%async_computation.2 | async-start | bytes 3670016 | tf_op jit(solution)/shard_map/all_to_all | solution.py:90
  176.0 2.9 %slice.109 = bf16[256,3584]{1,0:T(8,128)(2,1)} slice(bf16[256,8192]{1,0:T(8,128)(2,1)} %bitcast.90), slice={[0:256], [4608:8192]} | slice | bytes 3670016 | tf_op jit(solution)/shard_map/slice | solution.py:57
  179.0 2.9 %slice.111 = bf16[256,3584]{1,0:T(8,128)(2,1)} slice(bf16[256,8192]{1,0:T(8,128)(2,1)} %bitcast.94), slice={[0:256], [4608:8192]} | slice | bytes 3670016 | tf_op jit(solution)/shard_map/slice | solution.py:57
  181.9 1.6 reduce_sum.158
  183.5 17.8 %all-to-all-done.2 = f32[64,8,896]{2,1,0:T(8,128)S(1)} async-done(((f32[64,8,896]{2,1,0:T(8,128)}), f32[64,8,896]{2,1,0:T(8,128)S(1)}, u32[]{:S(2)}, u32[]{:S(2)}) %all-to-all-start.2) | async-done | bytes 1835040 | tf_op jit(solution)/shard_map/all_to_all | solution.py:90
  202.1 4.4 %all-to-all-start.5 = ((f32[16,8,896]{2,1,0:T(8,128)}), f32[16,8,896]{2,1,0:T(8,128)}, u32[]{:S(2)}, u32[]{:S(2)}) async-start(f32[16,8,896]{2,1,0:T(8,128)} %broadcast_in_dim.23), calls=%async_computation.5 | async-start | bytes 917504 | tf_op jit(solution)/shard_map/all_to_all | solution.py:93
  206.6 9.2 %convolution_convert_fusion = bf16[3584,1024]{1,0:T(8,128)(2,1)} fusion(bf16[256,3584]{1,0:T(8,128)(2,1)} %slice.111, bf16[256,3584]{1,0:T(8,128)(2,1)} %slice.109, bf16[256,1024]{1,0:T(8,128)(2,1)S(1)} %copy-done.3, bf16[256,1024]{1,0:T(8,128)(2,1)} %copy-done.5), kind=kOutput, calls=%fused_computation | convolution fusion | flops 3771203584 | bytes 12058624 | tf_op jit(solution)/shard_map/dot_general | solution.py:105
  216.9 6.8 %all-to-all-start.3 = ((f32[16,8,896]{2,1,0:T(8,128)}), f32[16,8,896]{2,1,0:T(8,128)S(1)}, u32[]{:S(2)}, u32[]{:S(2)}) async-start(f32[16,8,896]{2,1,0:T(8,128)} %broadcast_in_dim.22), calls=%async_computation.3 | async-start | bytes 917504 | tf_op jit(solution)/shard_map/all_to_all | solution.py:93
  225.9 7.6 %all-to-all-done.3 = f32[16,8,896]{2,1,0:T(8,128)S(1)} async-done(((f32[16,8,896]{2,1,0:T(8,128)}), f32[16,8,896]{2,1,0:T(8,128)S(1)}, u32[]{:S(2)}, u32[]{:S(2)}) %all-to-all-start.3) | async-done | bytes 458784 | tf_op jit(solution)/shard_map/all_to_all | solution.py:93
  (85 shorter events, 23.0 us)
Async XLA Ops:
  7.2 6.9 %copy-start.7 = (s32[2,256]{1,0:T(2,128)S(1)}, s32[2,256]{1,0:T(2,128)}, u32[]{:S(2)}) copy-start(s32[2,256]{1,0:T(2,128)} %param.13) | copy-start | bytes 6148
  7.2 41.1 %all-gather.5.cloned.1.call-start = ((), (), s32[]{:S(2)}) async-start(), calls=%async_computation.6 | async-start | bytes 4718592 | tf_op jit(solution)/shard_map/all_gather | solution.py:56
  13.3 71.3 %all-gather.7.cloned.1.call-start = ((), (), s32[]{:S(2)}) async-start(), calls=%async_computation.7 | async-start | bytes 4718592 | tf_op jit(solution)/shard_map/all_gather | solution.py:56
  48.2 5.9 %copy-start.4 = (bf16[1,256,8192]{2,1,0:T(8,128)(2,1)S(1)}, bf16[1,256,8192]{2,1,0:T(8,128)(2,1)}, u32[]{:S(2)}) copy-start(bf16[1,256,8192]{2,1,0:T(8,128)(2,1)} %all-gather.5.cloned.1.call-done) | copy-start | bytes 12582916
  54.1 8.2 %copy-start.8 = (f32[256,1024]{1,0:T(8,128)}, f32[256,1024]{1,0:T(8,128)S(1)}, u32[]{:S(2)}) copy-start(f32[256,1024]{1,0:T(8,128)S(1)} %fusion.26) | copy-start | bytes 3145732
  62.3 1.2 collective-permute-start
  64.3 26.1 %all-to-all-start = ((f32[64,8,128]{2,1,0:T(8,128)}), f32[64,8,128]{2,1,0:T(8,128)S(1)}, u32[]{:S(2)}, u32[]{:S(2)}) async-start(f32[64,8,128]{2,1,0:T(8,128)} %broadcast_in_dim.19), calls=%async_computation | async-start | bytes 524288 | tf_op jit(solution)/shard_map/all_to_all | solution.py:34
  98.9 29.5 %copy-start.5 = (bf16[256,1024]{1,0:T(8,128)(2,1)}, bf16[256,1024]{1,0:T(8,128)(2,1)S(1)}, u32[]{:S(2)}) copy-start(bf16[256,1024]{1,0:T(8,128)(2,1)S(1)} %get-tuple-element.25) | copy-start | bytes 1572868
  98.9 1.2 collective-permute-start.1
  100.9 20.1 %all-to-all-start.1 = ((f32[64,8,128]{2,1,0:T(8,128)}), f32[64,8,128]{2,1,0:T(8,128)S(1)}, u32[]{:S(2)}, u32[]{:S(2)}) async-start(f32[64,8,128]{2,1,0:T(8,128)} %broadcast_in_dim.21), calls=%async_computation.1 | async-start | bytes 524288 | tf_op jit(solution)/shard_map/all_to_all | solution.py:34
  121.1 7.4 %slice-start = ((s8[7340032]{0:T(1024)(128)(4,1)}), s8[4194304]{0:T(1024)(128)(4,1)S(1)}, s32[]{:S(2)}) async-start(s8[7340032]{0:T(1024)(128)(4,1)} %bitcast.77), calls=%async_computation.8 | async-start | bytes 8388608
  121.7 0.8 copy-start.2
  122.6 5.9 %slice-start.1 = ((s8[7340032]{0:T(1024)(128)(4,1)}), s8[3145728]{0:T(1024)(128)(4,1)S(1)}, s32[]{:S(2)}) async-start(s8[7340032]{0:T(1024)(128)(4,1)} %bitcast.77), calls=%async_computation.9 | async-start | bytes 6291456
  128.3 4.4 %collective-permute-start.3 = (f32[128,3584]{1,0:T(8,128)S(1)}, f32[128,3584]{1,0:T(8,128)S(1)}, u32[]{:S(2)}, u32[]{:S(2)}) collective-permute-start(f32[128,3584]{1,0:T(8,128)S(1)} %fusion.52), channel_id=1, source_target_pairs={{0,16},{16,0},{32,48},{48,32},{64,80},{80,64},{96,112},{112,96},{1... | collective-permute-start | bytes 5505032 | tf_op jit(solution)/shard_map/ppermute | solution.py:87
  132.3 9.4 %collective-permute-start.2 = (f32[128,3584]{1,0:T(8,128)}, f32[128,3584]{1,0:T(8,128)}, u32[]{:S(2)}, u32[]{:S(2)}) collective-permute-start(f32[128,3584]{1,0:T(8,128)} %fusion.51), channel_id=1, source_target_pairs={{0,16},{16,0},{32,48},{48,32},{64,80},{80,64},{96,112},{112,96},{1... | collective-permute-start | bytes 5505032 | tf_op jit(solution)/shard_map/ppermute | solution.py:87
  136.7 32.1 %all-to-all-start.4 = ((f32[64,8,896]{2,1,0:T(8,128)}), f32[64,8,896]{2,1,0:T(8,128)S(1)}, u32[]{:S(2)}, u32[]{:S(2)}) async-start(f32[64,8,896]{2,1,0:T(8,128)} %bitcast.33), calls=%async_computation.4 | async-start | bytes 3670016 | tf_op jit(solution)/shard_map/all_to_all | solution.py:90
  147.8 28.1 %copy-start.1 = (bf16[2,32,3584]{2,1,0:T(8,128)(2,1)S(1)}, bf16[2,32,3584]{2,1,0:T(8,128)(2,1)}, u32[]{:S(2)}) copy-start(bf16[2,32,3584]{2,1,0:T(8,128)(2,1)} %param.8) | copy-start | bytes 1376260
  168.8 1.2 copy-start
  170.0 31.3 %all-to-all-start.2 = ((f32[64,8,896]{2,1,0:T(8,128)}), f32[64,8,896]{2,1,0:T(8,128)S(1)}, u32[]{:S(2)}, u32[]{:S(2)}) async-start(f32[64,8,896]{2,1,0:T(8,128)} %bitcast.20), calls=%async_computation.2 | async-start | bytes 3670016 | tf_op jit(solution)/shard_map/all_to_all | solution.py:90
  179.0 27.6 %copy-start.3 = (bf16[256,1024]{1,0:T(8,128)(2,1)S(1)}, bf16[256,1024]{1,0:T(8,128)(2,1)}, u32[]{:S(2)}) copy-start(bf16[256,1024]{1,0:T(8,128)(2,1)} %copy-done.2) | copy-start | bytes 1572868
  202.1 14.0 %all-to-all-start.5 = ((f32[16,8,896]{2,1,0:T(8,128)}), f32[16,8,896]{2,1,0:T(8,128)}, u32[]{:S(2)}, u32[]{:S(2)}) async-start(f32[16,8,896]{2,1,0:T(8,128)} %broadcast_in_dim.23), calls=%async_computation.5 | async-start | bytes 917504 | tf_op jit(solution)/shard_map/all_to_all | solution.py:93
  216.0 18.0 %copy-start.6 = (f32[3584]{0:T(1024)S(1)}, f32[3584]{0:T(1024)}, u32[]{:S(2)}) copy-start(f32[3584]{0:T(1024)} %param.10) | copy-start | bytes 43012
  216.9 16.5 %all-to-all-start.3 = ((f32[16,8,896]{2,1,0:T(8,128)}), f32[16,8,896]{2,1,0:T(8,128)S(1)}, u32[]{:S(2)}, u32[]{:S(2)}) async-start(f32[16,8,896]{2,1,0:T(8,128)} %broadcast_in_dim.22), calls=%async_computation.3 | async-start | bytes 917504 | tf_op jit(solution)/shard_map/all_to_all | solution.py:93
Sparse Core Ops, SparseCore 0:
  13.4 34.7 all-gather.4
  49.9 34.6 all-gather.6

commit v2 on v0

v2 whole, which is shorter than its diff:
```python
import functools

import jax
import jax.numpy as jnp
from jax import lax
from jax.experimental import pallas as pl
from jax.experimental.pallas import tpu as pltpu
from jax.sharding import PartitionSpec as P

SOFT_CAP = 30.0
KL_WEIGHT = 0.5
NORM_EPS = 1e-06
AXES = ("dp", "sec", "vocab")
D_T, D_S, COLS = 4608, 3584, 1024
D_ALL = D_T + D_S
OWN = 64
ROWS = 8 * OWN
HALF = D_ALL // 2
QUARTER = HALF // 4
LANES = 896
FINISH_COPIES = 4
HEAD_STEPS = 7
MIB = 1024 * 1024


def linear(z, core, x, y):
    return (2 * z + core) * 16 + 4 * x + y


def pairs(move):
    return [
        (linear(z, c, x, y), linear(*move(z, c, x, y)))
        for z in range(4)
        for c in range(2)
        for x in range(4)
        for y in range(4)
    ]


SIBLING = pairs(lambda z, c, x, y: (z, 1 - c, x, y))
ALONG_Z = [pairs(lambda z, c, x, y, d=d: ((z + d) % 4, c, x, y)) for d in range(4)]
ALONG_LINE = [
    pairs(lambda z, c, x, y, e=e: (z, c, x, (y + e) % 4) if c else (z, c, (x + e) % 4, y))
    for e in range(4)
]
CHIPS = [
    [linear(z, c, x, y) for z in range(4) for x in range(4) for y in range(4)] for c in range(2)
]


LINES = [[linear(z, 0, x, y) for x in range(4)] for z in range(4) for y in range(4)] + [
    [linear(z, 1, x, y) for y in range(4)] for z in range(4) for x in range(4)
]
WALLS = [[linear(z, 0, x, y) for z in range(4) for y in range(4)] for x in range(4)] + [
    [linear(z, 1, x, y) for z in range(4) for x in range(4)] for y in range(4)
]
PLANES = [[linear(z, 0, x, y) for x in range(4) for y in range(4)] for z in range(4)] + [
    [linear(z, 1, x, y) for y in range(4) for x in range(4)] for z in range(4)
]


def swap(value):
    return lax.ppermute(value, AXES, SIBLING)


def norm_kernel(place, teacher, student, teacher_gain, student_gain, own, quarter):
    def normed(ref, gain):
        values = ref[...].astype(jnp.float32)
        factor = lax.rsqrt(jnp.mean(values * values, axis=-1, keepdims=True) + NORM_EPS)
        return (values * factor * gain[...][None, :]).astype(jnp.bfloat16)

    own[:, :D_T] = normed(teacher, teacher_gain)
    own[:, D_T:] = normed(student, student_gain)
    start = pl.multiple_of(place[2] * QUARTER, QUARTER)
    quarter[0] = own[:, pl.ds(start, QUARTER)]
    quarter[1] = own[:, pl.ds(HALF + start, QUARTER)]


def collect(place, half, pieces, rows, sems):
    z, core, line, line_s = place[0], place[1], place[2], place[3]
    mine, theirs = pieces[:5], pieces[5:]
    groups = []
    for k, (other, at, (own, near, *lines)) in enumerate(
        ((core, line, mine), (1 - core, line_s, theirs))
    ):

        def block(far):
            return pl.ds(pl.multiple_of((other * 4 + (z + 4 - far) % 4) * OWN, OWN), OWN)

        todo = [(own.at[:, pl.ds(half * HALF, HALF)], rows.at[block(0)])]
        for far in range(1, 4):
            for e in range(4):
                lanes = pl.ds(pl.multiple_of(((at + 4 - e) % 4) * QUARTER, QUARTER), QUARTER)
                source = near.at[half, far - 1] if e == 0 else lines[e - 1].at[far - 1]
                todo.append((source, rows.at[block(far), lanes]))
        groups.append(
            [pltpu.make_async_copy(a, b, sems.at[13 * k + i]) for i, (a, b) in enumerate(todo)]
        )
    return groups


def begin(copies):
    for copy in copies:
        copy.start()


def finish(copies):
    for copy in copies:
        copy.wait()


TILE = 256


def head_tiles(parts, buffers, sems):
    def copies(n):
        out, at = [], 0
        for k, (head, start, count) in enumerate(parts):
            source = head.at[pl.ds(start, count), pl.ds(TILE * n, TILE)]
            target = buffers.at[n % 2, pl.ds(at, count), :]
            out.append(pltpu.make_async_copy(source, target, sems.at[n % 2, k]))
            at += count
        return out

    def start(n):
        if n < COLS // TILE:
            for copy in copies(n):
                copy.start()

    def wait(n):
        for copy in copies(n):
            copy.wait()

    return start, wait


def core_rows(core):
    return pl.ds(pl.multiple_of(core * (ROWS // 2), ROWS // 2), ROWS // 2)


def first_kernel(place, *refs):
    *pieces, teacher_head, teacher_part, rows, heads, sems, head_sems = refs
    start, wait = head_tiles([(teacher_head, 0, HALF)], heads, head_sems)
    groups = collect(place, 0, pieces, rows, sems)
    begin(groups[0])
    start(0)
    begin(groups[1])
    start(1)
    for n in range(COLS // TILE):
        tile = slice(TILE * n, TILE * n + TILE)
        if n == 0:
            finish(groups[0])
            wait(0)
            for k in range(2):
                if k:
                    finish(groups[1])
                at = core_rows(place[1] if k == 0 else 1 - place[1])
                teacher_part[at, tile] = jnp.dot(
                    rows[at, :], heads[0], preferred_element_type=jnp.float32
                )
        else:
            wait(n)
            teacher_part[:, tile] = jnp.dot(
                rows[...], heads[n % 2], preferred_element_type=jnp.float32
            )
        start(n + 2)


def second_kernel(place, *refs):
    *pieces, teacher_part, teacher_head, student_head, labels = refs[:14]
    teacher_out, student_out, sums = refs[14:17]
    rows, heads, teacher_exp, student_cap, acc, sems, head_sems, out_sems = refs[17:]
    rest = D_T - HALF
    start, wait = head_tiles(
        [(teacher_head, HALF, rest), (student_head, 0, D_S)], heads, head_sems
    )
    groups = collect(place, 1, pieces, rows, sems)
    begin(groups[0])
    start(0)
    begin(groups[1])
    start(1)
    acc[...] = jnp.zeros_like(acc)

    def fold(value):
        return sum(value[:, 128 * i : 128 * i + 128] for i in range(TILE // 128))

    def dots(n, at):
        tile = slice(TILE * n, TILE * n + TILE)
        teacher_exp[n, at, :] = teacher_part[at, tile] + jnp.dot(
            rows[at, :rest], heads[n % 2, :rest, :], preferred_element_type=jnp.float32
        )
        student_cap[n, at, :] = jnp.dot(
            rows[at, rest:], heads[n % 2, rest:, :], preferred_element_type=jnp.float32
        )

    out_copies = []

    def caps(n):
        columns = place[4] + TILE * n + lax.broadcasted_iota(jnp.int32, (1, TILE), 1)
        chunk = 32
        for i in range(ROWS // chunk):
            at = slice(chunk * i, chunk * i + chunk)
            t_cap = SOFT_CAP * jnp.tanh(teacher_exp[n, at, :] * (1.0 / SOFT_CAP))
            s_cap = SOFT_CAP * jnp.tanh(student_cap[n, at, :] * (1.0 / SOFT_CAP))
            t_exp = jnp.exp(t_cap)
            teacher_exp[n, at, :] = t_exp
            student_cap[n, at, :] = s_cap
            picked = jnp.where(labels[at, :] == columns, s_cap, jnp.float32(0.0))
            acc[0, at, :] += fold(t_exp)
            acc[1, at, :] += fold(jnp.exp(s_cap))
            acc[2, at, :] += fold(t_exp * (t_cap - s_cap))
            acc[3, at, :] += fold(picked)
        for k, (source, out) in enumerate(((teacher_exp, teacher_out), (student_cap, student_out))):
            copy = pltpu.make_async_copy(
                source.at[n], out.at[:, pl.ds(TILE * n, TILE)], out_sems.at[2 * n + k]
            )
            copy.start()
            out_copies.append(copy)

    for n in range(COLS // TILE):
        if n == 0:
            finish(groups[0])
            wait(0)
            dots(0, core_rows(place[1]))
            finish(groups[1])
            dots(0, core_rows(1 - place[1]))
        else:
            wait(n)
            dots(n, slice(0, ROWS))
            caps(n - 1)
        start(n + 2)
    caps(COLS // TILE - 1)
    for kind in range(4):
        for i in range(4):
            block = acc[kind, 128 * i : 128 * i + 128, :]
            at = 4 * kind + i
            sums[at : at + 1, :] = jnp.sum(block.T, axis=0, keepdims=True)
    finish(out_copies)


def grad_kernel(
    place, teacher_in, student_in, totals, labels, logit_grad, teacher_exp, student_cap, sems
):
    copies = []
    for i in range(4):
        at = pl.ds(128 * i, 128)
        copies.append(
            [
                pltpu.make_async_copy(teacher_in.at[at, :], teacher_exp.at[at, :], sems.at[i, 0]),
                pltpu.make_async_copy(student_in.at[at, :], student_cap.at[at, :], sems.at[i, 1]),
            ]
        )
        for copy in copies[-1]:
            copy.start()
    columns = place[4] + lax.broadcasted_iota(jnp.int32, (1, COLS), 1)
    for i in range(4):

        def column(kind):
            at = 4 * kind + i
            return jnp.broadcast_to(totals[at : at + 1, :], (128, 128)).T

        teacher_scale = KL_WEIGHT / column(0)
        student_scale = 1.0 / column(1)
        block = slice(128 * i, 128 * i + 128)
        label = labels[block, :]
        for copy in copies[i]:
            copy.wait()
        for j in range(COLS // 128):
            lanes = slice(128 * j, 128 * j + 128)
            s_cap = student_cap[block, lanes]
            ratio = s_cap * (1.0 / SOFT_CAP)
            matches = (label == columns[:, lanes]).astype(jnp.float32)
            grad = (
                jnp.exp(s_cap) * student_scale
                - teacher_exp[block, lanes] * teacher_scale
                - (1.0 - KL_WEIGHT) * matches
            ) * (1.0 - ratio * ratio)
            logit_grad[2 * i, :, lanes] = grad[:OWN].astype(jnp.bfloat16)
            logit_grad[2 * i + 1, :, lanes] = grad[OWN:].astype(jnp.bfloat16)


def back_dot(logit_grad, core, head, part, n):
    rows = logit_grad[pl.ds(4 * core, 4)].reshape(4 * OWN, COLS)
    start = part * (D_S // 2) + n * LANES
    return lax.dot_general(
        rows,
        head[start : start + LANES, :],
        (((1,), (1,)), ((), ())),
        preferred_element_type=jnp.float32,
    )


def head_grad_kernel(place, *refs):
    *pieces, logit_grad, out, rows, buffers, sems, out_sems = refs
    groups = collect(place, 1, pieces, rows, sems)
    for group in groups:
        begin(group)
    for group in groups:
        finish(group)
    step = D_S // HEAD_STEPS

    def copy_out(n):
        return pltpu.make_async_copy(
            buffers.at[n % 2], out.at[pl.ds(step * n, step), :], out_sems.at[n % 2]
        )

    for n in range(HEAD_STEPS):
        lanes = slice(D_T - HALF + step * n, D_T - HALF + step * n + step)
        value = lax.dot_general(
            rows[:, lanes],
            logit_grad[...].reshape(ROWS, COLS),
            (((0,), (0,)), ((), ())),
            preferred_element_type=jnp.float32,
        )
        if n >= 2:
            copy_out(n - 2).wait()
        buffers[n % 2] = value.astype(jnp.bfloat16)
        copy_out(n).start()
    for n in range(HEAD_STEPS - 2, HEAD_STEPS):
        copy_out(n).wait()


def theirs_kernel(part, place, logit_grad, head, out):
    for n in range(D_S // 2 // LANES):
        out[:, n * LANES : n * LANES + LANES] = back_dot(logit_grad, 1 - place[1], head, part, n)


def mine_kernel(part, place, logit_grad, head, received, *rest):
    out = rest[-1]
    for n in range(D_S // 2 // LANES):
        lanes = slice(n * LANES, n * LANES + LANES)
        value = back_dot(logit_grad, place[1], head, part, n) + received[:, lanes]
        start = part * (D_S // 2) + n * LANES
        for i in range(64):
            to = (i // 4 % 4) * 16 + (i // 16) * 4 + i % 4
            out[to, :, start : start + LANES] = value[4 * i : 4 * i + 4, :]


def line_sum_kernel(got, out, parts, total, sems, out_sems):
    def copy_in(i, source):
        at = pl.ds(16 * source + 4 * i, 4)
        return pltpu.make_async_copy(got.at[at], parts.at[at], sems.at[i, source])

    def copy_out(i):
        at = pl.ds(4 * i, 4)
        return pltpu.make_async_copy(total.at[at], out.at[at], out_sems.at[i])

    for i in range(4):
        for source in range(4):
            copy_in(i, source).start()
    for i in range(4):
        for source in range(4):
            copy_in(i, source).wait()
        for k in range(4 * i, 4 * i + 4):
            total[k] = (parts[k] + parts[16 + k]) + (parts[32 + k] + parts[48 + k])
        copy_out(i).start()
    for i in range(4):
        copy_out(i).wait()


def finish_kernel(got, hidden, gain, out, parts, sems):
    chunk = 16 // FINISH_COPIES
    copies = [
        pltpu.make_async_copy(got.at[pl.ds(chunk * i, chunk)], parts.at[i], sems.at[i])
        for i in range(FINISH_COPIES)
    ]
    for copy in copies:
        copy.start()
    total = None
    for i in range(FINISH_COPIES):
        copies[i].wait()
        for k in range(chunk):
            part = parts[i, k]
            total = part if total is None else total + part
    values = hidden[...].astype(jnp.float32)
    factor = lax.rsqrt(jnp.mean(values * values, axis=-1, keepdims=True) + NORM_EPS)
    scaled = total * gain[...][None, :]
    inner_sum = jnp.mean(values * scaled, axis=-1, keepdims=True)
    grad = factor * scaled - values * (factor * factor * factor) * inner_sum
    out[...] = jnp.broadcast_to(grad.astype(jnp.bfloat16)[None], out.shape)


def limit(mib):
    return pltpu.CompilerParams(vmem_limit_bytes=mib * MIB)


def in_hbm(value):
    return pltpu.with_memory_space_constraint(value, pltpu.HBM)


def sum_everywhere(part):
    chip = part + swap(part)
    copies = jnp.broadcast_to(chip[None], (64, 16, 128))
    got = lax.all_to_all(copies, AXES, 0, 0, tiled=True, axis_index_groups=CHIPS)
    return jnp.sum(got, axis=0)


def body(
    teacher_hidden, student_hidden, teacher_gain, student_gain, teacher_head, student_head, labels
):
    dp, sec, vocab = (lax.axis_index(a) for a in AXES)
    z, core = dp // 2, dp % 2
    x, y = sec * 2 + vocab // 4, vocab % 4
    line = jnp.where(core == 0, x, y)
    line_s = other = jnp.where(core == 0, y, x)
    device_place = lax.axis_index(AXES)
    place = jnp.stack([z, core, line, line_s, device_place * COLS, 1 - core]).astype(jnp.int32)
    labels_here = labels.reshape(2, 4, 2, 32).transpose(2, 1, 0, 3).reshape(ROWS, 1)

    smem = pl.BlockSpec(memory_space=pltpu.SMEM)
    vmem = pl.BlockSpec(memory_space=pltpu.VMEM)
    any_space = pl.BlockSpec(memory_space=pltpu.HBM)
    own, quarter = pl.pallas_call(
        norm_kernel,
        out_shape=[
            jax.ShapeDtypeStruct((OWN, D_ALL), jnp.bfloat16),
            jax.ShapeDtypeStruct((2, OWN, QUARTER), jnp.bfloat16),
        ],
        in_specs=[smem] + [vmem] * 4,
        out_specs=[vmem] * 2,
        compiler_params=limit(56),
    )(
        place,
        teacher_hidden.reshape(OWN, D_T),
        student_hidden.reshape(OWN, D_S),
        teacher_gain,
        student_gain,
    )

    own_s = swap(own)

    near = jnp.stack([lax.ppermute(quarter, AXES, ALONG_Z[d]) for d in (1, 2, 3)], axis=1)
    near, own_s = lax.optimization_barrier((near, own_s))
    lines_1, lines_2 = (
        [lax.ppermute(near[half], AXES, ALONG_LINE[e]) for e in (1, 2, 3)] for half in range(2)
    )
    near_s, lines_1[0] = lax.optimization_barrier((near, lines_1[0]))
    near_s = swap(near_s)
    pieces_1 = [own, near, *lines_1, own_s, near_s, *(swap(v) for v in lines_1)]
    teacher_part = pl.pallas_call(
        first_kernel,
        out_shape=jax.ShapeDtypeStruct((ROWS, COLS), jnp.float32),
        in_specs=[smem] + [any_space] * 11,
        out_specs=vmem,
        scratch_shapes=[
            pltpu.VMEM((ROWS, HALF), jnp.bfloat16),
            pltpu.VMEM((2, HALF, TILE), jnp.bfloat16),
            pltpu.SemaphoreType.DMA((26,)),
            pltpu.SemaphoreType.DMA((2, 1)),
        ],
        compiler_params=limit(24),
        cost_estimate=pl.CostEstimate(
            flops=2 * ROWS * HALF * COLS, bytes_accessed=14 * MIB, transcendentals=0
        ),
    )(place, *map(in_hbm, pieces_1), in_hbm(teacher_head))
    *lines_2, teacher_part = lax.optimization_barrier((*lines_2, teacher_part))
    pieces_2 = [own, near, *lines_2, own_s, near_s, *(swap(v) for v in lines_2)]
    teacher_exp, student_cap, sums = pl.pallas_call(
        second_kernel,
        out_shape=[
            pltpu.HBM((ROWS, COLS), jnp.float32),
            pltpu.HBM((ROWS, COLS), jnp.float32),
            jax.ShapeDtypeStruct((16, 128), jnp.float32),
        ],
        in_specs=[smem] + [any_space] * 10 + [vmem] + [any_space] * 2 + [vmem],
        out_specs=[any_space] * 2 + [vmem],
        scratch_shapes=[
            pltpu.VMEM((ROWS, HALF), jnp.bfloat16),
            pltpu.VMEM((2, HALF, TILE), jnp.bfloat16),
            pltpu.VMEM((COLS // TILE, ROWS, TILE), jnp.float32),
            pltpu.VMEM((COLS // TILE, ROWS, TILE), jnp.float32),
            pltpu.VMEM((4, ROWS, 128), jnp.float32),
            pltpu.SemaphoreType.DMA((26,)),
            pltpu.SemaphoreType.DMA((2, 2)),
            pltpu.SemaphoreType.DMA((8,)),
        ],
        compiler_params=limit(28),
        cost_estimate=pl.CostEstimate(
            flops=2 * ROWS * HALF * COLS, bytes_accessed=24 * MIB, transcendentals=4 * ROWS * COLS
        ),
    )(
        place,
        *map(in_hbm, pieces_2),
        teacher_part,
        in_hbm(teacher_head),
        in_hbm(student_head),
        labels_here,
    )

    totals = sum_everywhere(sums)

    logit_grad = pl.pallas_call(
        grad_kernel,
        out_shape=jax.ShapeDtypeStruct((8, OWN, COLS), jnp.bfloat16),
        in_specs=[smem] + [any_space] * 2 + [vmem] * 2,
        out_specs=vmem,
        scratch_shapes=[
            pltpu.VMEM((ROWS, COLS), jnp.float32),
            pltpu.VMEM((ROWS, COLS), jnp.float32),
            pltpu.SemaphoreType.DMA((4, 2)),
        ],
        compiler_params=limit(10),
        cost_estimate=pl.CostEstimate(
            flops=8 * ROWS * COLS, bytes_accessed=5 * MIB, transcendentals=ROWS * COLS
        ),
    )(
        place, in_hbm(teacher_exp), in_hbm(student_cap), totals, labels_here
    )

    back_cost = pl.CostEstimate(
        flops=4 * OWN * COLS * D_S, bytes_accessed=6 * MIB, transcendentals=0
    )
    theirs = [
        swap(
            pl.pallas_call(
                functools.partial(theirs_kernel, part),
                out_shape=jax.ShapeDtypeStruct((4 * OWN, D_S // 2), jnp.float32),
                in_specs=[smem, vmem, vmem],
                out_specs=vmem,
                compiler_params=limit(6),
                cost_estimate=back_cost,
            )(place, logit_grad, student_head)
        )
        for part in range(2)
    ]
    pieces = ()
    for part in range(2):
        pieces = pl.pallas_call(
            functools.partial(mine_kernel, part),
            out_shape=[jax.ShapeDtypeStruct((64, 4, D_S), jnp.float32)],
            in_specs=[smem, vmem, vmem, vmem] + [vmem] * part,
            out_specs=[vmem],
            input_output_aliases={4: 0} if part else {},
            compiler_params=limit(8),
            cost_estimate=back_cost,
        )(place, logit_grad, student_head, theirs[part], *pieces)
    got = lax.all_to_all(pieces[0], AXES, 0, 0, tiled=True, axis_index_groups=LINES)
    head_grad = pl.pallas_call(
        head_grad_kernel,
        out_shape=pltpu.HBM((D_S, COLS), jnp.bfloat16),
        in_specs=[smem] + [any_space] * 10 + [vmem],
        out_specs=any_space,
        scratch_shapes=[
            pltpu.VMEM((ROWS, HALF), jnp.bfloat16),
            pltpu.VMEM((2, D_S // HEAD_STEPS, COLS), jnp.bfloat16),
            pltpu.SemaphoreType.DMA((26,)),
            pltpu.SemaphoreType.DMA((2,)),
        ],
        compiler_params=limit(20),
        cost_estimate=pl.CostEstimate(
            flops=2 * ROWS * D_S * COLS, bytes_accessed=13 * MIB, transcendentals=0
        ),
    )(place, *map(in_hbm, pieces_2), logit_grad)
    got, head_grad = lax.optimization_barrier((got, head_grad))
    got = pl.pallas_call(
        line_sum_kernel,
        out_shape=pltpu.HBM((16, 4, D_S), jnp.float32),
        in_specs=[any_space],
        out_specs=any_space,
        scratch_shapes=[
            pltpu.VMEM((64, 4, D_S), jnp.float32),
            pltpu.VMEM((16, 4, D_S), jnp.float32),
            pltpu.SemaphoreType.DMA((4, 4)),
            pltpu.SemaphoreType.DMA((4,)),
        ],
        compiler_params=limit(12),
    )(in_hbm(got))
    got = lax.all_to_all(got, AXES, 0, 0, tiled=True, axis_index_groups=WALLS)
    hidden = student_hidden.reshape(16, 4, D_S)
    hidden = lax.dynamic_index_in_dim(hidden, 4 * line + other, 0, keepdims=False)
    hidden_grad = pl.pallas_call(
        finish_kernel,
        out_shape=jax.ShapeDtypeStruct((16, 4, D_S), jnp.bfloat16),
        in_specs=[any_space, vmem, vmem],
        out_specs=vmem,
        scratch_shapes=[
            pltpu.VMEM((FINISH_COPIES, 16 // FINISH_COPIES, 4, D_S), jnp.float32),
            pltpu.SemaphoreType.DMA((FINISH_COPIES,)),
        ],
        compiler_params=limit(8),
    )(in_hbm(got), hidden, student_gain)
    hidden_grad = lax.all_to_all(hidden_grad, AXES, 0, 0, tiled=True, axis_index_groups=PLANES)

    mine = lax.dynamic_slice_in_dim(totals.reshape(4, ROWS), (4 * core + z) * OWN, OWN, 1)
    divergence = mine[2] / mine[0] - jnp.log(mine[0]) + jnp.log(mine[1])
    loss = KL_WEIGHT * divergence + (1.0 - KL_WEIGHT) * (jnp.log(mine[1]) - mine[3])
    return (loss.reshape(2, 32), hidden_grad.reshape(2, 32, D_S), head_grad)


def solution(mesh):
    in_specs = (
        P(None, "dp", None),
        P(None, "dp", None),
        P(),
        P(),
        P(None, AXES),
        P(None, AXES),
        P(),
    )
    out_specs = (P(None, "dp"), P(None, "dp", None), P(None, AXES))
    return jax.shard_map(body, mesh=mesh, in_specs=in_specs, out_specs=out_specs, check_vma=False)
```

time: 383 us -> 184 us (0.48)
  waiting for transfers between devices: 231 us -> 66.2 us
  Pallas kernels: 0 us -> 53.7 us
  matrix products: 51.8 us -> 0 us
  blocking collectives: 65.8 us -> 19.4 us
  starting transfers between devices: 0.2 us -> 32.1 us
  other arithmetic: 13.1 us -> 0.19 us
  between operations: 14 us -> 1.1 us
  local copies, waits for them, and re-layouts: 6.09 us -> 10.3 us
    psum x1 -> x0, waiting for transfers between devices: 137 us -> none  [body(): lax.psum(back_rows(logit_grad, student_head), ('dp', 'sec', 'vocab'))]
    all_gather x4 -> x0, waiting for transfers between devices: 92.1 us -> none  [the longest x2 49.7 us: body(): lax.all_gather(student_hidden[member], 'dp', axis=0, tiled=True)]
    psum x1 -> x0, blocking collectives: 65.8 us -> none  [body(): lax.psum((teacher_part, student_part, cross_part, picked_part), ('dp', 's...]
    pallas_call x0 -> x11, Pallas kernels: none -> 53.7 us  [the longest x1 13.7 us: body(): pl.pallas_call(second_kernel, out_shape=[pltpu.HBM((ROWS, COLS), jnp.floa...]
    dot_general x8 -> x0, matrix products: 51.8 us -> none  [the longest x4 18.3 us: capped_logits(): jnp.dot(normed, head_cols, preferred_element_type=jnp.float32) / SOFT_CAP]
    all_to_all x0 -> x3, waiting for transfers between devices: none -> 39.6 us  [the longest x1 15.5 us: body(): lax.all_to_all(pieces[0], AXES, 0, 0, tiled=True, axis_index_groups=LINES)]
    ppermute x0 -> x20, waiting for transfers between devices: none -> 26.6 us  [the longest x3 13.6 us: body(): lax.ppermute(quarter, AXES, ALONG_Z[d])]
    ppermute x0 -> x20, starting transfers between devices: none -> 19.6 us  [the longest x6 10.8 us: body(): lax.ppermute(near[half], AXES, ALONG_LINE[e])]
  transfers between devices with their start and end apart: 5 -> 23, of which waited for: 5 -> 13; matrix products, arithmetic and copies ran while one was open for 10% -> 1% of each run, Pallas kernels for 0% -> 14%
where the time goes in v2:
time: 184 us; the launch traced here: 183 us
  waiting for transfers between devices  66.2 us (36%)
  Pallas kernels  53.7 us (29%)
  starting transfers between devices  32.1 us (17%)
  blocking collectives  19.4 us (11%)
  local copies, waits for them, and re-layouts  10.3 us (6%)
    all_to_all x1, blocking collectives, sum_everywhere(): lax.all_to_all(copies, AXES, 0, 0, tiled=True, axis_index_groups=CHIPS)  19.4 us
    all_to_all x1, waiting for transfers between devices, body(): lax.all_to_all(pieces[0], AXES, 0, 0, tiled=True, axis_index_groups=LINES)  15.5 us
    all_to_all x1, waiting for transfers between devices, body(): got = lax.all_to_all(got, AXES, 0, 0, tiled=True, axis_index_groups=WALLS)  13.9 us
    pallas_call x1, Pallas kernels, body(): pl.pallas_call(second_kernel, out_shape=[pltpu.HBM((ROWS, COLS), jnp.floa...  13.7 us
    ppermute x3, waiting for transfers between devices, body(): lax.ppermute(quarter, AXES, ALONG_Z[d])  13.6 us
    pallas_call x1, Pallas kernels, body(): pl.pallas_call(first_kernel, out_shape=jax.ShapeDtypeStruct((ROWS, COLS),...  12 us
    ppermute x6, starting transfers between devices, body(): lax.ppermute(near[half], AXES, ALONG_LINE[e])  10.8 us
    all_to_all x1, waiting for transfers between devices, body(): lax.all_to_all(hidden_grad, AXES, 0, 0, tiled=True, axis_index_groups=PLA...  10.2 us
  transfers between devices with their start and end apart: 23, of which 13 were waited for; matrix products, arithmetic and copies ran while one was open for 1% of the time, Pallas kernels for 14%

profile of v2, /device:TPU:0, one launch (start us, length us, event | category | flops | bytes accessed | tf_op | source)
XLA Modules:
  0.0 183.0 jit_solution(14555211937074150193)
XLA Ops:
  1.4 2.8 %shard_map.94 = (bf16[64,8192]{1,0:T(8,128)(2,1)}, bf16[2,64,1024]{2,1,0:T(8,128)(2,1)}) custom-call(s32[6]{0:T(128)} %stack.39.place, bf16[64,4608]{1,0:T(8,128)(2,1)} %bitcast.23, bf16[64,3584]{1,0:T(8,128)(2,1)} %bitcast.22, f32[4608]{0:T(1024)} %teacher_gain.1, f32[3584]{0:T(1024)} %gain.1), custom_call_target="tpu_custom_call" | custom-call | tf_op jit(solution)/shard_map/pallas_call | solution.py:413
  4.2 4.1 %collective-permute-start.2 = (bf16[2,64,1024]{2,1,0:T(8,128)(2,1)}, bf16[2,64,1024]{2,1,0:T(8,128)(2,1)S(1)}, u32[]{:S(2)}, u32[]{:S(2)}) collective-permute-start(bf16[2,64,1024]{2,1,0:T(8,128)(2,1)} %get-tuple-element.19), channel_id=1, source_target_pairs={{0,96},{1,97},{2,98},{3,99},{4,100},{5,101},{6,102},{7,103},{8,104... | collective-permute-start | bytes 786440 | tf_op jit(solution)/shard_map/ppermute | solution.py:432
  8.3 1.9 %collective-permute-start.1 = (bf16[2,64,1024]{2,1,0:T(8,128)(2,1)}, bf16[2,64,1024]{2,1,0:T(8,128)(2,1)S(1)}, u32[]{:S(2)}, u32[]{:S(2)}) collective-permute-start(bf16[2,64,1024]{2,1,0:T(8,128)(2,1)} %get-tuple-element.19), channel_id=1, source_target_pairs={{0,64},{1,65},{2,66},{3,67},{4,68},{5,69},{6,70},{7,71},{8,72},{9,... | collective-permute-start | bytes 786440 | tf_op jit(solution)/shard_map/ppermute | solution.py:432
  10.2 10.3 %collective-permute-done.2 = bf16[2,64,1024]{2,1,0:T(8,128)(2,1)S(1)} collective-permute-done((bf16[2,64,1024]{2,1,0:T(8,128)(2,1)}, bf16[2,64,1024]{2,1,0:T(8,128)(2,1)S(1)}, u32[]{:S(2)}, u32[]{:S(2)}) %collective-permute-start.2) | collective-permute-done | bytes 262176 | tf_op jit(solution)/shard_map/ppermute | solution.py:432
  20.5 3.3 %collective-permute-done = bf16[2,64,1024]{2,1,0:T(8,128)(2,1)S(1)} collective-permute-done((bf16[2,64,1024]{2,1,0:T(8,128)(2,1)}, bf16[2,64,1024]{2,1,0:T(8,128)(2,1)S(1)}, u32[]{:S(2)}, u32[]{:S(2)}) %collective-permute-start) | collective-permute-done | bytes 262176 | tf_op jit(solution)/shard_map/ppermute | solution.py:432
  25.6 2.7 %collective-permute-start.8 = (bf16[3,64,1024]{2,1,0:T(8,128)(2,1)S(1)}, bf16[3,64,1024]{2,1,0:T(8,128)(2,1)S(1)}, u32[]{:S(2)}, u32[]{:S(2)}) collective-permute-start(bf16[3,64,1024]{2,1,0:T(8,128)(2,1)S(1)} %get-tuple-element.33), channel_id=1, source_target_pairs={{0,8},{1,9},{2,10},{3,11},{4,12},{5,13},{6,14},{7,15},{8,0},{9,1},... | collective-permute-start | bytes 1179656 | tf_op jit(solution)/shard_map/ppermute | solution.py:435
  29.7 3.3 %collective-permute-done.7.refs_2_ = bf16[3,64,1024]{2,1,0:T(8,128)(2,1)S(1)} collective-permute-done((bf16[3,64,1024]{2,1,0:T(8,128)(2,1)S(1)}, bf16[3,64,1024]{2,1,0:T(8,128)(2,1)S(1)}, u32[]{:S(2)}, u32[]{:S(2)}) %collective-permute-start.7) | collective-permute-done | bytes 393248 | tf_op jit(solution)/shard_map/ppermute | solution.py:435
  33.6 4.7 %collective-permute-done.8.refs_3_ = bf16[3,64,1024]{2,1,0:T(8,128)(2,1)S(1)} collective-permute-done((bf16[3,64,1024]{2,1,0:T(8,128)(2,1)S(1)}, bf16[3,64,1024]{2,1,0:T(8,128)(2,1)S(1)}, u32[]{:S(2)}, u32[]{:S(2)}) %collective-permute-start.8) | collective-permute-done | bytes 393248 | tf_op jit(solution)/shard_map/ppermute | solution.py:435
  40.2 2.1 %collective-permute-start.5 = (bf16[3,64,1024]{2,1,0:T(8,128)(2,1)S(1)}, bf16[3,64,1024]{2,1,0:T(8,128)(2,1)S(1)}, u32[]{:S(2)}, u32[]{:S(2)}) collective-permute-start(bf16[3,64,1024]{2,1,0:T(8,128)(2,1)S(1)} %get-tuple-element.34), channel_id=1, source_target_pairs={{0,8},{1,9},{2,10},{3,11},{4,12},{5,13},{6,14},{7,15},{8,0},{9,1},... | collective-permute-start | bytes 1179656 | tf_op jit(solution)/shard_map/ppermute | solution.py:435
  45.6 12.0 %shard_map.95.refs_10_ = f32[512,1024]{1,0:T(8,128)S(1)} custom-call(s32[6]{0:T(128)S(1)} %copy-done.3, bf16[64,8192]{1,0:T(8,128)(2,1)} %get-tuple-element.18.refs_0_, bf16[2,3,64,1024]{3,2,1,0:T(8,128)(2,1)} %copy-done.4, bf16[3,64,1024]{2,1,0:T(8,128)(2,1)} %copy-done.12, bf16[3,64,1024]{2,1,0:T(8,128)(2,1)} %copy-done.13, ...), custom_call_target="tpu_custom_call" | custom-call | flops 4294967296 | bytes 14680064 | tf_op jit(solution)/shard_map/pallas_call | solution.py:440
  60.8 13.7 %shard_map.96 = (f32[512,1024]{1,0:T(8,128)}, f32[512,1024]{1,0:T(8,128)}, f32[16,128]{1,0:T(8,128)S(1)}) custom-call(s32[6]{0:T(128)S(1)} %copy-done.3, bf16[64,8192]{1,0:T(8,128)(2,1)} %get-tuple-element.18.refs_0_, bf16[2,3,64,1024]{3,2,1,0:T(8,128)(2,1)} %copy-done.4, bf16[3,64,1024]{2,1,0:T(8,128)(2,1)} %copy-done.9, bf16[3,64,1024]{2,1,0:T(8,128)(2,1)} %copy-done.10, ...), custom_call_target="tpu_custom_call" | custom-call | flops 4294967296 | bytes 25165824 | tf_op jit(solution)/shard_map/pallas_call | solution.py:458
  75.8 19.4 %all_to_all.20 = f32[64,16,128]{2,1,0:T(8,128)S(1)} all-to-all(f32[64,16,128]{2,1,0:T(8,128)S(1)} %broadcast_in_dim.2), channel_id=1, replica_groups={{0,1,2,3,4,5,6,7,8,9,10,11,12,13,14,15,32,33,34,35,36,37,38,39,40,41,42..., dimensions={0} | all-to-all | bytes 1048576 | tf_op jit(solution)/shard_map/all_to_all | solution.py:394
  95.3 3.0 %shard_map.97.logit_grad.refs_10_ = bf16[8,64,1024]{2,1,0:T(8,128)(2,1)S(1)} custom-call(s32[6]{0:T(128)S(1)} %copy-done.3, f32[512,1024]{1,0:T(8,128)} %get-tuple-element.29.teacher_in, f32[512,1024]{1,0:T(8,128)} %get-tuple-element.30.student_in, f32[16,128]{1,0:T(8,128)S(1)} %reduce_sum.9.totals, s32[512,1]{1,0:T(8,128)S(1)} %reshape.49.refs_13_.labels), custom_call_target="tpu_custom_call" | custom-call | flops 4194304 | bytes 5242880 | tf_op jit(solution)/shard_map/pallas_call | solution.py:492
  98.3 3.1 %copy-done = bf16[3584,1024]{1,0:T(8,128)(2,1)S(1)} copy-done((bf16[3584,1024]{1,0:T(8,128)(2,1)S(1)}, bf16[3584,1024]{1,0:T(8,128)(2,1)}, u32[]{:S(2)}) %copy-start) | copy-done | bytes 7340056
  109.7 1.8 shard_map.101
  113.3 4.7 %all-to-all-start.1 = ((f32[64,4,3584]{2,1,0:T(4,128)}), f32[64,4,3584]{2,1,0:T(4,128)}, u32[]{:S(2)}, u32[]{:S(2)}) async-start(f32[64,4,3584]{2,1,0:T(4,128)} %copy-done.1), calls=%async_computation.1 | async-start | bytes 7340032 | tf_op jit(solution)/shard_map/all_to_all | solution.py:537
  118.1 9.5 %shard_map.102 = bf16[3584,1024]{1,0:T(8,128)(2,1)} custom-call(s32[6]{0:T(128)S(1)} %copy-done.3, bf16[64,8192]{1,0:T(8,128)(2,1)} %get-tuple-element.18.refs_0_, bf16[2,3,64,1024]{3,2,1,0:T(8,128)(2,1)} %copy-done.4, bf16[3,64,1024]{2,1,0:T(8,128)(2,1)} %copy-done.9, bf16[3,64,1024]{2,1,0:T(8,128)(2,1)} %copy-done.10, bf16[3,64,1024]{2,1,0:T(8,128)(2,1)} %copy-done.11, ...), custom_call_target="tpu_custom_call" | custom-call | flops 3758096384 | bytes 13631488 | tf_op jit(solution)/shard_map/pallas_call | solution.py:538
  127.6 15.5 %all-to-all-done.1.got = f32[64,4,3584]{2,1,0:T(4,128)} async-done(((f32[64,4,3584]{2,1,0:T(4,128)}), f32[64,4,3584]{2,1,0:T(4,128)}, u32[]{:S(2)}, u32[]{:S(2)}) %all-to-all-start.1) | async-done | bytes 3670048 | tf_op jit(solution)/shard_map/all_to_all | solution.py:537
  143.1 3.0 %shard_map.103 = f32[16,4,3584]{2,1,0:T(4,128)} custom-call(f32[64,4,3584]{2,1,0:T(4,128)} %all-to-all-done.1.got), custom_call_target="tpu_custom_call" | custom-call | tf_op jit(solution)/shard_map/pallas_call | solution.py:555
  146.1 3.6 %all-to-all-start.2 = ((f32[16,4,3584]{2,1,0:T(4,128)}), f32[16,4,3584]{2,1,0:T(4,128)S(1)}, u32[]{:S(2)}, u32[]{:S(2)}) async-start(f32[16,4,3584]{2,1,0:T(4,128)} %shard_map.103), calls=%async_computation.2 | async-start | bytes 1835008 | tf_op jit(solution)/shard_map/all_to_all | solution.py:568
  149.9 13.9 %all-to-all-done.2.got = f32[16,4,3584]{2,1,0:T(4,128)S(1)} async-done(((f32[16,4,3584]{2,1,0:T(4,128)}), f32[16,4,3584]{2,1,0:T(4,128)S(1)}, u32[]{:S(2)}, u32[]{:S(2)}) %all-to-all-start.2) | async-done | bytes 917536 | tf_op jit(solution)/shard_map/all_to_all | solution.py:568
  164.8 2.3 %shard_map.104 = bf16[16,4,3584]{2,1,0:T(4,128)(2,1)} custom-call(f32[16,4,3584]{2,1,0:T(4,128)} %copy-done.7, bf16[4,3584]{1,0:T(4,128)(2,1)S(1)} %dynamic-slice_bitcast_fusion.hidden, f32[3584]{0:T(1024)S(1)} %copy-done.2), custom_call_target="tpu_custom_call" | custom-call | tf_op jit(solution)/shard_map/pallas_call | solution.py:571
  167.0 4.2 %all-to-all-start.3 = ((bf16[16,4,3584]{2,1,0:T(4,128)(2,1)}), bf16[16,4,3584]{2,1,0:T(4,128)(2,1)S(1)}, u32[]{:S(2)}, u32[]{:S(2)}) async-start(bf16[16,4,3584]{2,1,0:T(4,128)(2,1)} %shard_map.104), calls=%async_computation.3 | async-start | bytes 917504 | tf_op jit(solution)/shard_map/all_to_all | solution.py:582
  172.0 10.2 %all-to-all-done.3 = bf16[16,4,3584]{2,1,0:T(4,128)(2,1)S(1)} async-done(((bf16[16,4,3584]{2,1,0:T(4,128)(2,1)}), bf16[16,4,3584]{2,1,0:T(4,128)(2,1)S(1)}, u32[]{:S(2)}, u32[]{:S(2)}) %all-to-all-start.3) | async-done | bytes 458784 | tf_op jit(solution)/shard_map/all_to_all | solution.py:582
  (93 shorter events, 26.7 us)
Async XLA Ops:
  1.4 44.2 %copy-start.3 = (s32[6]{0:T(128)S(1)}, s32[6]{0:T(128)}, u32[]{:S(2)}) copy-start(s32[6]{0:T(128)} %stack.39.place) | copy-start | bytes 76
  4.2 19.7 %collective-permute-start.3 = (bf16[64,8192]{1,0:T(8,128)(2,1)}, bf16[64,8192]{1,0:T(8,128)(2,1)S(1)}, u32[]{:S(2)}, u32[]{:S(2)}) collective-permute-start(bf16[64,8192]{1,0:T(8,128)(2,1)} %get-tuple-element.18.refs_0_), channel_id=1, source_target_pairs={{0,16},{1,17},{2,18},{3,19},{4,20},{5,21},{6,22},{7,23},{8,24},{9,... | collective-permute-start | bytes 3145736 | tf_op jit(solution)/shard_map/ppermute | solution.py:63
  4.2 16.3 %collective-permute-start.2 = (bf16[2,64,1024]{2,1,0:T(8,128)(2,1)}, bf16[2,64,1024]{2,1,0:T(8,128)(2,1)S(1)}, u32[]{:S(2)}, u32[]{:S(2)}) collective-permute-start(bf16[2,64,1024]{2,1,0:T(8,128)(2,1)} %get-tuple-element.19), channel_id=1, source_target_pairs={{0,96},{1,97},{2,98},{3,99},{4,100},{5,101},{6,102},{7,103},{8,104... | collective-permute-start | bytes 786440 | tf_op jit(solution)/shard_map/ppermute | solution.py:432
  8.3 15.5 %collective-permute-start = (bf16[2,64,1024]{2,1,0:T(8,128)(2,1)}, bf16[2,64,1024]{2,1,0:T(8,128)(2,1)S(1)}, u32[]{:S(2)}, u32[]{:S(2)}) collective-permute-start(bf16[2,64,1024]{2,1,0:T(8,128)(2,1)} %get-tuple-element.19), channel_id=1, source_target_pairs={{0,32},{1,33},{2,34},{3,35},{4,36},{5,37},{6,38},{7,39},{8,40},{9,... | collective-permute-start | bytes 786440 | tf_op jit(solution)/shard_map/ppermute | solution.py:432
  8.3 15.5 %collective-permute-start.1 = (bf16[2,64,1024]{2,1,0:T(8,128)(2,1)}, bf16[2,64,1024]{2,1,0:T(8,128)(2,1)S(1)}, u32[]{:S(2)}, u32[]{:S(2)}) collective-permute-start(bf16[2,64,1024]{2,1,0:T(8,128)(2,1)} %get-tuple-element.19), channel_id=1, source_target_pairs={{0,64},{1,65},{2,66},{3,67},{4,68},{5,69},{6,70},{7,71},{8,72},{9,... | collective-permute-start | bytes 786440 | tf_op jit(solution)/shard_map/ppermute | solution.py:432
  24.0 9.1 %collective-permute-start.7 = (bf16[3,64,1024]{2,1,0:T(8,128)(2,1)S(1)}, bf16[3,64,1024]{2,1,0:T(8,128)(2,1)S(1)}, u32[]{:S(2)}, u32[]{:S(2)}) collective-permute-start(bf16[3,64,1024]{2,1,0:T(8,128)(2,1)S(1)} %get-tuple-element.33), channel_id=1, source_target_pairs={{0,4},{1,5},{2,6},{3,7},{4,8},{5,9},{6,10},{7,11},{8,12},{9,13},{1... | collective-permute-start | bytes 1179656 | tf_op jit(solution)/shard_map/ppermute | solution.py:435
  25.6 12.7 %collective-permute-start.8 = (bf16[3,64,1024]{2,1,0:T(8,128)(2,1)S(1)}, bf16[3,64,1024]{2,1,0:T(8,128)(2,1)S(1)}, u32[]{:S(2)}, u32[]{:S(2)}) collective-permute-start(bf16[3,64,1024]{2,1,0:T(8,128)(2,1)S(1)} %get-tuple-element.33), channel_id=1, source_target_pairs={{0,8},{1,9},{2,10},{3,11},{4,12},{5,13},{6,14},{7,15},{8,0},{9,1},... | collective-permute-start | bytes 1179656 | tf_op jit(solution)/shard_map/ppermute | solution.py:435
  28.3 10.0 %collective-permute-start.9 = (bf16[3,64,1024]{2,1,0:T(8,128)(2,1)S(1)}, bf16[3,64,1024]{2,1,0:T(8,128)(2,1)S(1)}, u32[]{:S(2)}, u32[]{:S(2)}) collective-permute-start(bf16[3,64,1024]{2,1,0:T(8,128)(2,1)S(1)} %get-tuple-element.33), channel_id=1, source_target_pairs={{0,12},{1,13},{2,14},{3,15},{4,0},{5,1},{6,2},{7,3},{8,4},{9,5},{1... | collective-permute-start | bytes 1179656 | tf_op jit(solution)/shard_map/ppermute | solution.py:435
  33.1 10.9 %collective-permute-start.10 = (bf16[2,3,64,1024]{3,2,1,0:T(8,128)(2,1)S(1)}, bf16[2,3,64,1024]{3,2,1,0:T(8,128)(2,1)S(1)}, u32[]{:S(2)}, u32[]{:S(2)}) collective-permute-start(bf16[2,3,64,1024]{3,2,1,0:T(8,128)(2,1)S(1)} %pad_maximum_fusion.refs_1_), channel_id=1, source_target_pairs={{0,16},{1,17},{2,18},{3,19},{4,20},{5,21},{6,22},{7,23},{8,24},{9,... | collective-permute-start | bytes 2359304 | tf_op jit(solution)/shard_map/ppermute | solution.py:63
  33.1 7.2 %collective-permute-start.11 = (bf16[3,64,1024]{2,1,0:T(8,128)(2,1)S(1)}, bf16[3,64,1024]{2,1,0:T(8,128)(2,1)S(1)}, u32[]{:S(2)}, u32[]{:S(2)}) collective-permute-start(bf16[3,64,1024]{2,1,0:T(8,128)(2,1)S(1)} %collective-permute-done.7.refs_2_), channel_id=1, source_target_pairs={{0,16},{1,17},{2,18},{3,19},{4,20},{5,21},{6,22},{7,23},{8,24},{9,... | collective-permute-start | bytes 1179656 | tf_op jit(solution)/shard_map/ppermute | solution.py:63
  38.3 4.1 %collective-permute-start.12 = (bf16[3,64,1024]{2,1,0:T(8,128)(2,1)S(1)}, bf16[3,64,1024]{2,1,0:T(8,128)(2,1)S(1)}, u32[]{:S(2)}, u32[]{:S(2)}) collective-permute-start(bf16[3,64,1024]{2,1,0:T(8,128)(2,1)S(1)} %collective-permute-done.8.refs_3_), channel_id=1, source_target_pairs={{0,16},{1,17},{2,18},{3,19},{4,20},{5,21},{6,22},{7,23},{8,24},{9,... | collective-permute-start | bytes 1179656 | tf_op jit(solution)/shard_map/ppermute | solution.py:63
  38.3 5.6 %collective-permute-start.13 = (bf16[3,64,1024]{2,1,0:T(8,128)(2,1)S(1)}, bf16[3,64,1024]{2,1,0:T(8,128)(2,1)S(1)}, u32[]{:S(2)}, u32[]{:S(2)}) collective-permute-start(bf16[3,64,1024]{2,1,0:T(8,128)(2,1)S(1)} %collective-permute-done.9.refs_4_), channel_id=1, source_target_pairs={{0,16},{1,17},{2,18},{3,19},{4,20},{5,21},{6,22},{7,23},{8,24},{9,... | collective-permute-start | bytes 1179656 | tf_op jit(solution)/shard_map/ppermute | solution.py:63
  38.8 18.9 %collective-permute-start.4 = (bf16[3,64,1024]{2,1,0:T(8,128)(2,1)S(1)}, bf16[3,64,1024]{2,1,0:T(8,128)(2,1)S(1)}, u32[]{:S(2)}, u32[]{:S(2)}) collective-permute-start(bf16[3,64,1024]{2,1,0:T(8,128)(2,1)S(1)} %get-tuple-element.34), channel_id=1, source_target_pairs={{0,4},{1,5},{2,6},{3,7},{4,8},{5,9},{6,10},{7,11},{8,12},{9,13},{1... | collective-permute-start | bytes 1179656 | tf_op jit(solution)/shard_map/ppermute | solution.py:435
  40.2 17.4 %collective-permute-start.5 = (bf16[3,64,1024]{2,1,0:T(8,128)(2,1)S(1)}, bf16[3,64,1024]{2,1,0:T(8,128)(2,1)S(1)}, u32[]{:S(2)}, u32[]{:S(2)}) collective-permute-start(bf16[3,64,1024]{2,1,0:T(8,128)(2,1)S(1)} %get-tuple-element.34), channel_id=1, source_target_pairs={{0,8},{1,9},{2,10},{3,11},{4,12},{5,13},{6,14},{7,15},{8,0},{9,1},... | collective-permute-start | bytes 1179656 | tf_op jit(solution)/shard_map/ppermute | solution.py:435
  42.4 15.3 %collective-permute-start.6 = (bf16[3,64,1024]{2,1,0:T(8,128)(2,1)S(1)}, bf16[3,64,1024]{2,1,0:T(8,128)(2,1)S(1)}, u32[]{:S(2)}, u32[]{:S(2)}) collective-permute-start(bf16[3,64,1024]{2,1,0:T(8,128)(2,1)S(1)} %get-tuple-element.34), channel_id=1, source_target_pairs={{0,12},{1,13},{2,14},{3,15},{4,0},{5,1},{6,2},{7,3},{8,4},{9,5},{1... | collective-permute-start | bytes 1179656 | tf_op jit(solution)/shard_map/ppermute | solution.py:435
  57.7 1.9 %collective-permute-start.14 = (bf16[3,64,1024]{2,1,0:T(8,128)(2,1)S(1)}, bf16[3,64,1024]{2,1,0:T(8,128)(2,1)}, u32[]{:S(2)}, u32[]{:S(2)}) collective-permute-start(bf16[3,64,1024]{2,1,0:T(8,128)(2,1)S(1)} %collective-permute-done.4.refs_2_), channel_id=1, source_target_pairs={{0,16},{1,17},{2,18},{3,19},{4,20},{5,21},{6,22},{7,23},{8,24},{9,... | collective-permute-start | bytes 1179656 | tf_op jit(solution)/shard_map/ppermute | solution.py:63
  57.8 2.4 %collective-permute-start.15 = (bf16[3,64,1024]{2,1,0:T(8,128)(2,1)S(1)}, bf16[3,64,1024]{2,1,0:T(8,128)(2,1)}, u32[]{:S(2)}, u32[]{:S(2)}) collective-permute-start(bf16[3,64,1024]{2,1,0:T(8,128)(2,1)S(1)} %collective-permute-done.5.refs_3_), channel_id=1, source_target_pairs={{0,16},{1,17},{2,18},{3,19},{4,20},{5,21},{6,22},{7,23},{8,24},{9,... | collective-permute-start | bytes 1179656 | tf_op jit(solution)/shard_map/ppermute | solution.py:63
  58.3 2.5 %collective-permute-start.16 = (bf16[3,64,1024]{2,1,0:T(8,128)(2,1)S(1)}, bf16[3,64,1024]{2,1,0:T(8,128)(2,1)}, u32[]{:S(2)}, u32[]{:S(2)}) collective-permute-start(bf16[3,64,1024]{2,1,0:T(8,128)(2,1)S(1)} %collective-permute-done.6.refs_4_), channel_id=1, source_target_pairs={{0,16},{1,17},{2,18},{3,19},{4,20},{5,21},{6,22},{7,23},{8,24},{9,... | collective-permute-start | bytes 1179656 | tf_op jit(solution)/shard_map/ppermute | solution.py:63
  74.5 1.3 collective-permute-start.17
  103.2 3.9 %collective-permute-start.19 = (f32[256,1792]{1,0:T(8,128)S(1)}, f32[256,1792]{1,0:T(8,128)S(1)}, u32[]{:S(2)}, u32[]{:S(2)}) collective-permute-start(f32[256,1792]{1,0:T(8,128)S(1)} %shard_map.99), channel_id=1, source_target_pairs={{0,16},{1,17},{2,18},{3,19},{4,20},{5,21},{6,22},{7,23},{8,24},{9,... | collective-permute-start | bytes 5505032 | tf_op jit(solution)/shard_map/ppermute | solution.py:63
  105.1 4.6 %collective-permute-start.18 = (f32[256,1792]{1,0:T(8,128)S(1)}, f32[256,1792]{1,0:T(8,128)S(1)}, u32[]{:S(2)}, u32[]{:S(2)}) collective-permute-start(f32[256,1792]{1,0:T(8,128)S(1)} %shard_map.98), channel_id=1, source_target_pairs={{0,16},{1,17},{2,18},{3,19},{4,20},{5,21},{6,22},{7,23},{8,24},{9,... | collective-permute-start | bytes 5505032 | tf_op jit(solution)/shard_map/ppermute | solution.py:63
  113.3 29.7 %all-to-all-start.1 = ((f32[64,4,3584]{2,1,0:T(4,128)}), f32[64,4,3584]{2,1,0:T(4,128)}, u32[]{:S(2)}, u32[]{:S(2)}) async-start(f32[64,4,3584]{2,1,0:T(4,128)} %copy-done.1), calls=%async_computation.1 | async-start | bytes 7340032 | tf_op jit(solution)/shard_map/all_to_all | solution.py:537
  146.1 17.7 %all-to-all-start.2 = ((f32[16,4,3584]{2,1,0:T(4,128)}), f32[16,4,3584]{2,1,0:T(4,128)S(1)}, u32[]{:S(2)}, u32[]{:S(2)}) async-start(f32[16,4,3584]{2,1,0:T(4,128)} %shard_map.103), calls=%async_computation.2 | async-start | bytes 1835008 | tf_op jit(solution)/shard_map/all_to_all | solution.py:568
  167.0 15.2 %all-to-all-start.3 = ((bf16[16,4,3584]{2,1,0:T(4,128)(2,1)}), bf16[16,4,3584]{2,1,0:T(4,128)(2,1)S(1)}, u32[]{:S(2)}, u32[]{:S(2)}) async-start(bf16[16,4,3584]{2,1,0:T(4,128)(2,1)} %shard_map.104), calls=%async_computation.3 | async-start | bytes 917504 | tf_op jit(solution)/shard_map/all_to_all | solution.py:582
  (20 other events, 154.6 us)

commit v3 on v2

v3 whole, which is shorter than its diff:
```python
import functools

import jax
import jax.numpy as jnp
from jax import lax
from jax.experimental import pallas as pl
from jax.experimental.pallas import tpu as pltpu
from jax.sharding import PartitionSpec as P

SOFT_CAP = 30.0
KL_WEIGHT = 0.5
NORM_EPS = 1e-06
AXES = ("dp", "sec", "vocab")
D_T, D_S, COLS = 4608, 3584, 1024
D_ALL = D_T + D_S
OWN = 64
ROWS = 8 * OWN
QUARTER = D_ALL // 4
NEAR, FAR = (0, 1, 3), (2,)
FARS = NEAR + FAR
LANES = 896
HEAD_STEPS = 7
MIB = 1024 * 1024


def linear(z, core, x, y):
    return (2 * z + core) * 16 + 4 * x + y


def pairs(move):
    return [
        (linear(z, c, x, y), linear(*move(z, c, x, y)))
        for z in range(4)
        for c in range(2)
        for x in range(4)
        for y in range(4)
    ]


SIBLING = pairs(lambda z, c, x, y: (z, 1 - c, x, y))
ALONG_Z = [pairs(lambda z, c, x, y, d=d: ((z + d) % 4, c, x, y)) for d in range(4)]
ALONG_LINE = [
    pairs(lambda z, c, x, y, e=e: (z, c, x, (y + e) % 4) if c else (z, c, (x + e) % 4, y))
    for e in range(4)
]
CHIPS = [
    [linear(z, c, x, y) for z in range(4) for x in range(4) for y in range(4)] for c in range(2)
]


WALLS = [[linear(z, 0, x, y) for z in range(4) for y in range(4)] for x in range(4)] + [
    [linear(z, 1, x, y) for z in range(4) for x in range(4)] for y in range(4)
]
PLANES = [[linear(z, 0, x, y) for x in range(4) for y in range(4)] for z in range(4)] + [
    [linear(z, 1, x, y) for y in range(4) for x in range(4)] for z in range(4)
]


def swap(value):
    return lax.ppermute(value, AXES, SIBLING)


def norm_kernel(*refs):
    inputs, (own, quarter), buffers, sems = refs[:4], refs[4:6], refs[6:10], refs[10]
    copies = [pltpu.make_async_copy(a, b, sems.at[i]) for i, (a, b) in enumerate(zip(inputs, buffers))]
    begin(copies)
    teacher, student, teacher_gain, student_gain = buffers

    def normed(ref, gain):
        values = ref[...].astype(jnp.float32)
        factor = lax.rsqrt(jnp.mean(values * values, axis=-1, keepdims=True) + NORM_EPS)
        return (values * factor * gain[...][None, :]).astype(jnp.bfloat16)

    finish([copies[1], copies[3]])
    own[:, D_T:] = normed(student, student_gain)
    finish([copies[0], copies[2]])
    own[:, :D_T] = normed(teacher, teacher_gain)
    dp, sec, vocab = (lax.axis_index(a) for a in AXES)
    line = jnp.where(dp % 2 == 0, sec * 2 + vocab // 4, vocab % 4)
    quarter[...] = own[:, pl.ds(pl.multiple_of(line * QUARTER, QUARTER), QUARTER)]


def row_start(place, k, far):
    other = place[1] if k == 0 else 1 - place[1]
    return pl.multiple_of((other * 4 + (place[0] + 4 - far) % 4) * OWN, OWN)


def collect(place, pieces, rows, start_of, sems):
    groups, used = ([], []), 0
    for k, far, sources in pieces:
        block = pl.ds(start_of(k, far), OWN)
        for e, source in enumerate(sources):
            target = rows.at[block]
            if len(sources) > 1:
                lanes = pl.multiple_of(((place[2 + k] + 4 - e) % 4) * QUARTER, QUARTER)
                target = rows.at[block, pl.ds(lanes, QUARTER)]
            groups[k].append(pltpu.make_async_copy(source, target, sems.at[used]))
            used += 1
    return groups


def pieces_of(fars, refs):
    out, per_core = [], len(refs) // 2
    for k in range(2):
        own, lines = refs[k * per_core], refs[(k + 1) * per_core - 4 : (k + 1) * per_core]
        others = [far for far in fars if far]
        for far in fars:
            if far == 0:
                out.append((k, far, [own]))
            else:
                out.append((k, far, [line.at[others.index(far)] for line in lines]))
    return out


def begin(copies):
    for copy in copies:
        copy.start()


def finish(copies):
    for copy in copies:
        copy.wait()


CHUNK = 1024
BUFFERS = 3


def head_chunks(parts, buffers, sems):
    def copy(n):
        head, start, count = parts[n]
        target = buffers.at[n % BUFFERS, pl.ds(0, count), :]
        return pltpu.make_async_copy(head.at[pl.ds(start, count), :], target, sems.at[n % BUFFERS])

    def start(n):
        if n < len(parts):
            copy(n).start()

    return start, lambda n: copy(n).wait()


def all_pieces(refs):
    return pieces_of(NEAR, refs[:10]) + pieces_of(FAR, refs[10:18])


def forward_kernel(place, *refs):
    received, refs = refs[:18], refs[18:]
    teacher_head, student_head, labels = refs[:3]
    teacher_out, student_out, sums = refs[3:6]
    rows, heads, teacher_cap, teacher_exp, student_cap, acc, sems, head_sems, out_sems = refs[6:]
    side = len(FARS) * OWN
    parts = [(teacher_head, at, min(CHUNK, D_T - at)) for at in range(0, D_T, CHUNK)]
    teacher_parts = len(parts)
    parts += [(student_head, at, min(CHUNK, D_S - at)) for at in range(0, D_S, CHUNK)]
    start, wait = head_chunks(parts, heads, head_sems)
    groups = collect(
        place, all_pieces(received), rows, lambda k, far: k * side + FARS.index(far) * OWN, sems
    )
    begin(groups[0])
    start(0)
    begin(groups[1])
    start(1)
    start(2)

    def fold(value):
        return sum(value[:, 128 * i : 128 * i + 128] for i in range(COLS // 128))

    blocks = [(k, far) for k in range(2) for far in FARS]

    def out_copy(source, out, k, b):
        there = pl.ds(row_start(place, *blocks[b]), OWN)
        return pltpu.make_async_copy(source.at[pl.ds(OWN * b, OWN), :], out.at[there, :], out_sems.at[k, b])

    step = 16
    columns = place[4] + lax.broadcasted_iota(jnp.int32, (1, COLS), 1)

    def steps_of(b):
        first = row_start(place, *blocks[b])
        for i in range(OWN // step):
            at = OWN * b + step * i
            yield slice(at, at + step), pl.ds(pl.multiple_of(first + step * i, step), step)

    def teacher_block(b):
        for at, there in steps_of(b):
            t_cap = SOFT_CAP * jnp.tanh(teacher_cap[at, :] * (1.0 / SOFT_CAP))
            t_exp = jnp.exp(t_cap)
            teacher_cap[at, :] = t_cap
            teacher_exp[at, :] = t_exp
            acc[0, there, :] = fold(t_exp)
        out_copy(teacher_exp, teacher_out, 0, b).start()

    def student_block(b):
        for at, there in steps_of(b):
            s_cap = SOFT_CAP * jnp.tanh(student_cap[at, :] * (1.0 / SOFT_CAP))
            student_cap[at, :] = s_cap
            picked = jnp.where(labels[there, :] == columns, s_cap, jnp.float32(0.0))
            acc[1, there, :] = fold(jnp.exp(s_cap))
            acc[2, there, :] = fold(teacher_exp[at, :] * (teacher_cap[at, :] - s_cap))
            acc[3, there, :] = fold(picked)
        out_copy(student_cap, student_out, 1, b).start()

    lane, done = 0, 0
    for n, (_, _, count) in enumerate(parts):
        lanes = slice(lane, lane + count)
        lane += count
        total = teacher_cap if n < teacher_parts else student_cap
        if n == 0:
            for k in range(2):
                finish(groups[k])
                if k == 0:
                    wait(0)
                at = slice(k * side, k * side + side)
                total[at, :] = jnp.dot(
                    rows[at, lanes], heads[0, :count, :], preferred_element_type=jnp.float32
                )
        else:
            wait(n)
            value = jnp.dot(
                rows[:, lanes], heads[n % BUFFERS, :count, :], preferred_element_type=jnp.float32
            )
            total[...] = value if n == teacher_parts else total[...] + value
        if n >= teacher_parts:
            until = len(blocks) * (n + 1 - teacher_parts) // (len(parts) - teacher_parts)
            for b in range(done, until):
                teacher_block(b)
            done = until
        start(n + BUFFERS)
    for b in range(len(blocks)):
        student_block(b)
    for kind in range(4):
        for i in range(4):
            block = acc[kind, 128 * i : 128 * i + 128, :]
            at = 4 * kind + i
            sums[at : at + 1, :] = jnp.sum(block.T, axis=0, keepdims=True)
    for b in range(len(blocks)):
        out_copy(teacher_exp, teacher_out, 0, b).wait()
        out_copy(student_cap, student_out, 1, b).wait()


def grad_kernel(
    place, teacher_in, student_in, totals, labels, head, logit_grad, head_here,
    teacher_exp, student_cap, sems, head_sem,
):
    copies = []
    for i in range(4):
        at = pl.ds(128 * i, 128)
        copies.append(
            [
                pltpu.make_async_copy(teacher_in.at[at, :], teacher_exp.at[at, :], sems.at[i, 0]),
                pltpu.make_async_copy(student_in.at[at, :], student_cap.at[at, :], sems.at[i, 1]),
            ]
        )
        begin(copies[-1])
    head_copy = pltpu.make_async_copy(head, head_here, head_sem)
    head_copy.start()
    columns = place[4] + lax.broadcasted_iota(jnp.int32, (1, COLS), 1)
    for i in range(4):

        def column(kind):
            at = 4 * kind + i
            return jnp.broadcast_to(totals[at : at + 1, :], (128, 128)).T

        teacher_scale = KL_WEIGHT / column(0)
        student_scale = 1.0 / column(1)
        block = slice(128 * i, 128 * i + 128)
        label = labels[block, :]
        finish(copies[i])
        for j in range(COLS // 128):
            lanes = slice(128 * j, 128 * j + 128)
            s_cap = student_cap[block, lanes]
            ratio = s_cap * (1.0 / SOFT_CAP)
            matches = (label == columns[:, lanes]).astype(jnp.float32)
            grad = (
                jnp.exp(s_cap) * student_scale
                - teacher_exp[block, lanes] * teacher_scale
                - (1.0 - KL_WEIGHT) * matches
            ) * (1.0 - ratio * ratio)
            logit_grad[2 * i, :, lanes] = grad[:OWN].astype(jnp.bfloat16)
            logit_grad[2 * i + 1, :, lanes] = grad[OWN:].astype(jnp.bfloat16)
    head_copy.wait()


def back_dot(logit_grad, core, head, part, n):
    rows = logit_grad[pl.ds(4 * core, 4)].reshape(4 * OWN, COLS)
    start = part * (D_S // 2) + n * LANES
    return lax.dot_general(
        rows,
        head[start : start + LANES, :],
        (((1,), (1,)), ((), ())),
        preferred_element_type=jnp.float32,
    )


def head_grad_kernel(place, *refs):
    received = refs[:18]
    logit_grad, out, rows, buffers, sems, out_sems = refs[18:]
    groups = collect(place, all_pieces(received), rows, functools.partial(row_start, place), sems)
    for group in groups:
        begin(group)
    for group in groups:
        finish(group)
    step = D_S // HEAD_STEPS

    def copy_out(n):
        return pltpu.make_async_copy(
            buffers.at[n % 2], out.at[pl.ds(step * n, step), :], out_sems.at[n % 2]
        )

    for n in range(HEAD_STEPS):
        lanes = slice(D_T + step * n, D_T + step * n + step)
        value = lax.dot_general(
            rows[:, lanes],
            logit_grad[...].reshape(ROWS, COLS),
            (((0,), (0,)), ((), ())),
            preferred_element_type=jnp.float32,
        )
        if n >= 2:
            copy_out(n - 2).wait()
        buffers[n % 2] = value.astype(jnp.bfloat16)
        copy_out(n).start()
    for n in range(HEAD_STEPS - 2, HEAD_STEPS):
        copy_out(n).wait()


def theirs_kernel(part, place, logit_grad, head, out):
    for n in range(D_S // 2 // LANES):
        out[:, n * LANES : n * LANES + LANES] = back_dot(logit_grad, 1 - place[1], head, part, n)


def mine_kernel(part, place, logit_grad, head, received, *rest):
    *outs, value = rest
    for n in range(D_S // 2 // LANES):
        lanes = slice(n * LANES, n * LANES + LANES)
        value[...] = back_dot(logit_grad, place[1], head, part, n) + received[:, lanes]
        for e, out in enumerate(outs):
            for z in range(4):
                at = pl.multiple_of(z * OWN + ((place[2] + e) % 4) * 16, 16)
                block = value[pl.ds(at, 16), :]
                for other in range(4):
                    out[4 * z + other, :, lanes] = block[4 * other : 4 * other + 4]


def line_sum_kernel(*refs):
    slabs, (out, total, sems) = refs[:8], refs[8:]

    def copy_out(i):
        at = pl.ds(4 * i, 4)
        return pltpu.make_async_copy(total.at[at], out.at[at], sems.at[i])

    for i in range(4):
        for part in range(2):
            a, b, c, d = slabs[4 * part : 4 * part + 4]
            lanes = slice(part * (D_S // 2), (part + 1) * (D_S // 2))
            for at in range(4 * i, 4 * i + 4):
                total[at, :, lanes] = (a[at] + b[at]) + (c[at] + d[at])
        copy_out(i).start()
    for i in range(4):
        copy_out(i).wait()


def finish_kernel(got, hidden, gain, out):
    total = got[0]
    for k in range(1, 16):
        total = total + got[k]
    values = hidden[...].astype(jnp.float32)
    factor = lax.rsqrt(jnp.mean(values * values, axis=-1, keepdims=True) + NORM_EPS)
    scaled = total * gain[...][None, :]
    inner_sum = jnp.mean(values * scaled, axis=-1, keepdims=True)
    grad = factor * scaled - values * (factor * factor * factor) * inner_sum
    out[...] = jnp.broadcast_to(grad.astype(jnp.bfloat16)[None], out.shape)


def limit(mib):
    return pltpu.CompilerParams(vmem_limit_bytes=mib * MIB)


def in_hbm(value):
    return pltpu.with_memory_space_constraint(value, pltpu.HBM)


def sum_everywhere(part):
    chip = part + swap(part)
    copies = jnp.broadcast_to(chip[None], (64, 16, 128))
    got = lax.all_to_all(copies, AXES, 0, 0, tiled=True, axis_index_groups=CHIPS)
    return jnp.sum(got, axis=0)


def body(
    teacher_hidden, student_hidden, teacher_gain, student_gain, teacher_head, student_head, labels
):
    dp, sec, vocab = (lax.axis_index(a) for a in AXES)
    z, core = dp // 2, dp % 2
    x, y = sec * 2 + vocab // 4, vocab % 4
    line = jnp.where(core == 0, x, y)
    line_s = other = jnp.where(core == 0, y, x)
    device_place = lax.axis_index(AXES)
    place = jnp.stack([z, core, line, line_s, device_place * COLS, 1 - core]).astype(jnp.int32)
    labels_here = labels.reshape(2, 4, 2, 32).transpose(2, 1, 0, 3).reshape(ROWS, 1)

    smem = pl.BlockSpec(memory_space=pltpu.SMEM)
    vmem = pl.BlockSpec(memory_space=pltpu.VMEM)
    any_space = pl.BlockSpec(memory_space=pltpu.HBM)
    own, quarter = pl.pallas_call(
        norm_kernel,
        out_shape=[
            jax.ShapeDtypeStruct((OWN, D_ALL), jnp.bfloat16),
            jax.ShapeDtypeStruct((OWN, QUARTER), jnp.bfloat16),
        ],
        in_specs=[any_space] * 4,
        out_specs=[vmem] * 2,
        scratch_shapes=[
            pltpu.VMEM((OWN, D_T), jnp.bfloat16),
            pltpu.VMEM((OWN, D_S), jnp.bfloat16),
            pltpu.VMEM((D_T,), jnp.float32),
            pltpu.VMEM((D_S,), jnp.float32),
            pltpu.SemaphoreType.DMA((4,)),
        ],
        compiler_params=limit(10),
    )(
        in_hbm(teacher_hidden.reshape(OWN, D_T)),
        in_hbm(student_hidden.reshape(OWN, D_S)),
        in_hbm(teacher_gain),
        in_hbm(student_gain),
    )

    own_s = swap(own)

    next_1, next_3, opposite = (lax.ppermute(quarter, AXES, ALONG_Z[d]) for d in (1, 3, 2))
    near, own_s = lax.optimization_barrier((jnp.stack([next_1, next_3]), own_s))

    def along_line(value):
        return [value] + [lax.ppermute(value, AXES, ALONG_LINE[e]) for e in (1, 2, 3)]

    near_lines = along_line(near)
    far_lines = along_line(opposite[None])
    pieces = [own, *near_lines, own_s, *map(swap, near_lines), *far_lines, *map(swap, far_lines)]
    teacher_exp, student_cap, sums = pl.pallas_call(
        forward_kernel,
        out_shape=[
            pltpu.HBM((ROWS, COLS), jnp.float32),
            pltpu.HBM((ROWS, COLS), jnp.float32),
            jax.ShapeDtypeStruct((16, 128), jnp.float32),
        ],
        in_specs=[smem] + [any_space] * 20 + [vmem],
        out_specs=[any_space] * 2 + [vmem],
        scratch_shapes=[
            pltpu.VMEM((ROWS, D_ALL), jnp.bfloat16),
            pltpu.VMEM((BUFFERS, CHUNK, COLS), jnp.bfloat16),
            pltpu.VMEM((ROWS, COLS), jnp.float32),
            pltpu.VMEM((ROWS, COLS), jnp.float32),
            pltpu.VMEM((ROWS, COLS), jnp.float32),
            pltpu.VMEM((4, ROWS, 128), jnp.float32),
            pltpu.SemaphoreType.DMA((26,)),
            pltpu.SemaphoreType.DMA((BUFFERS,)),
            pltpu.SemaphoreType.DMA((2, 8)),
        ],
        compiler_params=limit(32),
        cost_estimate=pl.CostEstimate(
            flops=2 * ROWS * D_ALL * COLS, bytes_accessed=30 * MIB, transcendentals=4 * ROWS * COLS
        ),
    )(
        place,
        *map(in_hbm, pieces),
        in_hbm(teacher_head),
        in_hbm(student_head),
        labels_here,
    )

    totals = sum_everywhere(sums)

    logit_grad, head_here = pl.pallas_call(
        grad_kernel,
        out_shape=[
            jax.ShapeDtypeStruct((8, OWN, COLS), jnp.bfloat16),
            jax.ShapeDtypeStruct((D_S, COLS), jnp.bfloat16),
        ],
        in_specs=[smem] + [any_space] * 2 + [vmem] * 2 + [any_space],
        out_specs=[vmem] * 2,
        scratch_shapes=[
            pltpu.VMEM((ROWS, COLS), jnp.float32),
            pltpu.VMEM((ROWS, COLS), jnp.float32),
            pltpu.SemaphoreType.DMA((4, 2)),
            pltpu.SemaphoreType.DMA,
        ],
        compiler_params=limit(10),
        cost_estimate=pl.CostEstimate(
            flops=8 * ROWS * COLS, bytes_accessed=5 * MIB, transcendentals=ROWS * COLS
        ),
    )(
        place, in_hbm(teacher_exp), in_hbm(student_cap), totals, labels_here,
        in_hbm(student_head),
    )

    back_cost = pl.CostEstimate(
        flops=4 * OWN * COLS * D_S, bytes_accessed=6 * MIB, transcendentals=0
    )
    theirs = [
        swap(
            pl.pallas_call(
                functools.partial(theirs_kernel, part),
                out_shape=jax.ShapeDtypeStruct((4 * OWN, D_S // 2), jnp.float32),
                in_specs=[smem, vmem, vmem],
                out_specs=vmem,
                compiler_params=limit(6),
                cost_estimate=back_cost,
            )(place, logit_grad, head_here)
        )
        for part in range(2)
    ]
    slabs = []
    for part in range(2):
        mine = pl.pallas_call(
            functools.partial(mine_kernel, part),
            out_shape=[jax.ShapeDtypeStruct((16, 4, D_S // 2), jnp.float32)] * 4,
            in_specs=[smem, vmem, vmem, vmem],
            out_specs=[vmem] * 4,
            scratch_shapes=[pltpu.VMEM((4 * OWN, LANES), jnp.float32)],
            compiler_params=limit(8),
            cost_estimate=back_cost,
        )(place, logit_grad, head_here, theirs[part])
        slabs += [mine[0]] + [lax.ppermute(mine[e], AXES, ALONG_LINE[e]) for e in (1, 2, 3)]
    head_grad = pl.pallas_call(
        head_grad_kernel,
        out_shape=pltpu.HBM((D_S, COLS), jnp.bfloat16),
        in_specs=[smem] + [any_space] * 18 + [vmem],
        out_specs=any_space,
        scratch_shapes=[
            pltpu.VMEM((ROWS, D_ALL), jnp.bfloat16),
            pltpu.VMEM((2, D_S // HEAD_STEPS, COLS), jnp.bfloat16),
            pltpu.SemaphoreType.DMA((26,)),
            pltpu.SemaphoreType.DMA((2,)),
        ],
        compiler_params=limit(20),
        cost_estimate=pl.CostEstimate(
            flops=2 * ROWS * D_S * COLS, bytes_accessed=13 * MIB, transcendentals=0
        ),
    )(place, *map(in_hbm, pieces), logit_grad)
    *slabs, head_grad = lax.optimization_barrier((*slabs, head_grad))
    got = pl.pallas_call(
        line_sum_kernel,
        out_shape=pltpu.HBM((16, 4, D_S), jnp.float32),
        in_specs=[vmem] * 8,
        out_specs=any_space,
        scratch_shapes=[
            pltpu.VMEM((16, 4, D_S), jnp.float32),
            pltpu.SemaphoreType.DMA((4,)),
        ],
        compiler_params=limit(6),
    )(*slabs)
    got = lax.all_to_all(got, AXES, 0, 0, tiled=True, axis_index_groups=WALLS)
    hidden = student_hidden.reshape(16, 4, D_S)
    hidden = lax.dynamic_index_in_dim(hidden, 4 * line + other, 0, keepdims=False)
    hidden_grad = pl.pallas_call(
        finish_kernel,
        out_shape=jax.ShapeDtypeStruct((16, 4, D_S), jnp.bfloat16),
        in_specs=[vmem] * 3,
        out_specs=vmem,
        compiler_params=limit(4),
    )(got, hidden, student_gain)
    hidden_grad = lax.all_to_all(hidden_grad, AXES, 0, 0, tiled=True, axis_index_groups=PLANES)

    mine = lax.dynamic_slice_in_dim(totals.reshape(4, ROWS), (4 * core + z) * OWN, OWN, 1)
    divergence = mine[2] / mine[0] - jnp.log(mine[0]) + jnp.log(mine[1])
    loss = KL_WEIGHT * divergence + (1.0 - KL_WEIGHT) * (jnp.log(mine[1]) - mine[3])
    return (loss.reshape(2, 32), hidden_grad.reshape(2, 32, D_S), head_grad)


def solution(mesh):
    in_specs = (
        P(None, "dp", None),
        P(None, "dp", None),
        P(),
        P(),
        P(None, AXES),
        P(None, AXES),
        P(),
    )
    out_specs = (P(None, "dp"), P(None, "dp", None), P(None, AXES))
    return jax.shard_map(body, mesh=mesh, in_specs=in_specs, out_specs=out_specs, check_vma=False)
```

time: 184 us -> 159 us (0.86)
  waiting for transfers between devices: 66.2 us -> 55.3 us
  Pallas kernels: 53.7 us -> 43.6 us
  local copies, waits for them, and re-layouts: 10.3 us -> 2.27 us
  blocking collectives: 19.4 us -> 22.4 us
    all_to_all x1 -> x0, waiting for transfers between devices: 15.5 us -> none  [body(): lax.all_to_all(pieces[0], AXES, 0, 0, tiled=True, axis_index_groups=LINES)]
    ppermute x6 -> x12, waiting for transfers between devices: 8.03 us -> 17.7 us  [the longest x6 11.3 us: along_line(): lax.ppermute(value, AXES, ALONG_LINE[e])]
    unnamed x42 -> x26, local copies, waits for them, and re-layouts: 7.45 us -> 0.05 us
    pallas_call x3 -> x2, Pallas kernels: 28.8 us -> 21.6 us  [the longest x1 16.6 us: body(): pl.pallas_call(forward_kernel, out_shape=[pltpu.HBM((ROWS, COLS), jnp.flo...]
    ppermute x3, waiting for transfers between devices: 13.6 us -> 7.05 us  [body(): lax.ppermute(quarter, AXES, ALONG_Z[d])]
    ppermute x6 -> x12, starting transfers between devices: 10.8 us -> 16.9 us  [the longest x6 10.5 us: along_line(): lax.ppermute(value, AXES, ALONG_LINE[e])]
    all_to_all x1 -> x0, starting transfers between devices: 4.74 us -> none  [body(): lax.all_to_all(pieces[0], AXES, 0, 0, tiled=True, axis_index_groups=LINES)]
    all_to_all x1, blocking collectives: 19.4 us -> 22.4 us  [sum_everywhere(): lax.all_to_all(copies, AXES, 0, 0, tiled=True, axis_index_groups=CHIPS)]
  transfers between devices with their start and end apart: 23 -> 29, of which waited for: 13 -> 14; matrix products, arithmetic and copies ran while one was open for 1% -> 1% of each run, Pallas kernels for 14% -> 10%
where the time goes in v3:
time: 159 us; the launch traced here: 158 us
  waiting for transfers between devices  55.3 us (35%)
  Pallas kernels  43.6 us (27%)
  starting transfers between devices  33.7 us (21%)
  blocking collectives  22.4 us (14%)
  local copies, waits for them, and re-layouts  2.27 us (1%)
    all_to_all x1, blocking collectives, sum_everywhere(): lax.all_to_all(copies, AXES, 0, 0, tiled=True, axis_index_groups=CHIPS)  22.4 us
    pallas_call x1, Pallas kernels, body(): pl.pallas_call(forward_kernel, out_shape=[pltpu.HBM((ROWS, COLS), jnp.flo...  16.6 us
    all_to_all x1, waiting for transfers between devices, body(): got = lax.all_to_all(got, AXES, 0, 0, tiled=True, axis_index_groups=WALLS)  14.8 us
    ppermute x6, waiting for transfers between devices, along_line(): lax.ppermute(value, AXES, ALONG_LINE[e])  11.3 us
    pallas_call x1, Pallas kernels, body(): pl.pallas_call(head_grad_kernel, out_shape=pltpu.HBM((D_S, COLS), jnp.bfl...  10.7 us
    ppermute x6, starting transfers between devices, along_line(): lax.ppermute(value, AXES, ALONG_LINE[e])  10.5 us
    all_to_all x1, waiting for transfers between devices, body(): lax.all_to_all(hidden_grad, AXES, 0, 0, tiled=True, axis_index_groups=PLA...  10.3 us
    ppermute x3, waiting for transfers between devices, body(): lax.ppermute(quarter, AXES, ALONG_Z[d])  7.05 us
  transfers between devices with their start and end apart: 29, of which 14 were waited for; matrix products, arithmetic and copies ran while one was open for 1% of the time, Pallas kernels for 10%

profile of v3, /device:TPU:0, one launch (start us, length us, event | category | flops | bytes accessed | tf_op | source)
XLA Modules:
  0.0 158.4 jit_solution(11133142605768988429)
XLA Ops:
  0.6 1.8 %shard_map.94 = (bf16[64,8192]{1,0:T(8,128)(2,1)S(1)}, bf16[64,2048]{1,0:T(8,128)(2,1)S(1)}) custom-call(bf16[64,4608]{1,0:T(8,128)(2,1)} %bitcast.17, bf16[64,3584]{1,0:T(8,128)(2,1)} %bitcast.16, f32[4608]{0:T(1024)} %refs_2_.1, f32[3584]{0:T(1024)} %gain.1), custom_call_target="tpu_custom_call" | custom-call | tf_op jit(solution)/shard_map/pallas_call | solution.py:403
  2.5 4.0 %collective-permute-start.10 = (bf16[64,2048]{1,0:T(8,128)(2,1)S(1)}, bf16[64,2048]{1,0:T(8,128)(2,1)S(1)}, u32[]{:S(2)}, u32[]{:S(2)}) collective-permute-start(bf16[64,2048]{1,0:T(8,128)(2,1)S(1)} %get-tuple-element.30), channel_id=1, source_target_pairs={{0,64},{1,65},{2,66},{3,67},{4,68},{5,69},{6,70},{7,71},{8,72},{9,... | collective-permute-start | bytes 786440 | tf_op jit(solution)/shard_map/ppermute | solution.py:428
  8.6 5.2 %collective-permute-done.10 = bf16[64,2048]{1,0:T(8,128)(2,1)S(1)} collective-permute-done((bf16[64,2048]{1,0:T(8,128)(2,1)S(1)}, bf16[64,2048]{1,0:T(8,128)(2,1)S(1)}, u32[]{:S(2)}, u32[]{:S(2)}) %collective-permute-start.10) | collective-permute-done | bytes 262176 | tf_op jit(solution)/shard_map/ppermute | solution.py:428
  15.3 2.7 %collective-permute-start.12 = (bf16[1,64,2048]{2,1,0:T(8,128)(2,1)S(1)}, bf16[1,64,2048]{2,1,0:T(8,128)(2,1)S(1)}, u32[]{:S(2)}, u32[]{:S(2)}) collective-permute-start(bf16[1,64,2048]{2,1,0:T(8,128)(2,1)S(1)} %bitcast.19), channel_id=1, source_target_pairs={{0,8},{1,9},{2,10},{3,11},{4,12},{5,13},{6,14},{7,15},{8,0},{9,1},... | collective-permute-start | bytes 786440 | tf_op jit(solution)/shard_map/ppermute | solution.py:432
  18.0 1.9 %collective-permute-done.1 = bf16[64,2048]{1,0:T(8,128)(2,1)S(1)} collective-permute-done((bf16[64,2048]{1,0:T(8,128)(2,1)S(1)}, bf16[64,2048]{1,0:T(8,128)(2,1)S(1)}, u32[]{:S(2)}, u32[]{:S(2)}) %collective-permute-start.1) | collective-permute-done | bytes 262176 | tf_op jit(solution)/shard_map/ppermute | solution.py:428
  19.9 2.8 %collective-permute-start.13 = (bf16[1,64,2048]{2,1,0:T(8,128)(2,1)S(1)}, bf16[1,64,2048]{2,1,0:T(8,128)(2,1)}, u32[]{:S(2)}, u32[]{:S(2)}) collective-permute-start(bf16[1,64,2048]{2,1,0:T(8,128)(2,1)S(1)} %bitcast.20), channel_id=1, source_target_pairs={{0,12},{1,13},{2,14},{3,15},{4,0},{5,1},{6,2},{7,3},{8,4},{9,5},{1... | collective-permute-start | bytes 786440 | tf_op jit(solution)/shard_map/ppermute | solution.py:432
  22.8 2.3 %collective-permute-start.4 = (bf16[2,64,2048]{2,1,0:T(8,128)(2,1)S(1)}, bf16[2,64,2048]{2,1,0:T(8,128)(2,1)}, u32[]{:S(2)}, u32[]{:S(2)}) collective-permute-start(bf16[2,64,2048]{2,1,0:T(8,128)(2,1)S(1)} %pad_maximum_fusion.refs_1_), channel_id=1, source_target_pairs={{0,8},{1,9},{2,10},{3,11},{4,12},{5,13},{6,14},{7,15},{8,0},{9,1},... | collective-permute-start | bytes 1572872 | tf_op jit(solution)/shard_map/ppermute | solution.py:432
  28.3 10.5 %collective-permute-done.3.refs_2_ = bf16[2,64,2048]{2,1,0:T(8,128)(2,1)S(1)} collective-permute-done((bf16[2,64,2048]{2,1,0:T(8,128)(2,1)S(1)}, bf16[2,64,2048]{2,1,0:T(8,128)(2,1)S(1)}, u32[]{:S(2)}, u32[]{:S(2)}) %collective-permute-start.3) | collective-permute-done | bytes 524320 | tf_op jit(solution)/shard_map/ppermute | solution.py:432
  41.1 1.9 %collective-permute-done.17.refs_17_ = bf16[1,64,2048]{2,1,0:T(8,128)(2,1)} collective-permute-done((bf16[1,64,2048]{2,1,0:T(8,128)(2,1)}, bf16[1,64,2048]{2,1,0:T(8,128)(2,1)}, u32[]{:S(2)}, u32[]{:S(2)}) %collective-permute-start.17) | collective-permute-done | bytes 262176 | tf_op jit(solution)/shard_map/ppermute | solution.py:60
  43.0 16.6 %shard_map.95 = (f32[512,1024]{1,0:T(8,128)}, f32[512,1024]{1,0:T(8,128)}, f32[16,128]{1,0:T(8,128)S(1)}) custom-call(s32[6]{0:T(128)S(1)} %stack.36.place, bf16[64,8192]{1,0:T(8,128)(2,1)} %copy-done, bf16[2,64,2048]{2,1,0:T(8,128)(2,1)} %copy-done.2, bf16[2,64,2048]{2,1,0:T(8,128)(2,1)} %copy-done.5, bf16[2,64,2048]{2,1,0:T(8,128)(2,1)} %collective-permute-done.4.refs_3_, ...), custom_call_target="tpu_custom_call" | custom-call | flops 8589934592 | bytes 31457280 | tf_op jit(solution)/shard_map/pallas_call | solution.py:437
  60.9 22.4 %all_to_all.15 = f32[64,16,128]{2,1,0:T(8,128)S(1)} all-to-all(f32[64,16,128]{2,1,0:T(8,128)S(1)} %broadcast_in_dim.10), channel_id=1, replica_groups={{0,1,2,3,4,5,6,7,8,9,10,11,12,13,14,15,32,33,34,35,36,37,38,39,40,41,42..., dimensions={0} | all-to-all | bytes 1048576 | tf_op jit(solution)/shard_map/all_to_all | solution.py:384
  83.4 5.0 %shard_map.96 = (bf16[8,64,1024]{2,1,0:T(8,128)(2,1)S(1)}, bf16[3584,1024]{1,0:T(8,128)(2,1)S(1)}) custom-call(s32[6]{0:T(128)S(1)} %stack.36.place, f32[512,1024]{1,0:T(8,128)} %get-tuple-element.34.teacher_in, f32[512,1024]{1,0:T(8,128)} %get-tuple-element.35.student_in, f32[16,128]{1,0:T(8,128)S(1)} %reduce_sum.9.totals, ...), custom_call_target="tpu_custom_call" | custom-call | flops 4194304 | bytes 5242880 | tf_op jit(solution)/shard_map/pallas_call | solution.py:471
  88.4 1.8 %shard_map.97 = f32[256,1792]{1,0:T(8,128)S(1)} custom-call(s32[6]{0:T(128)S(1)} %stack.36.place, bf16[8,64,1024]{2,1,0:T(8,128)(2,1)S(1)} %get-tuple-element.36.logit_grad.refs_18_, bf16[3584,1024]{1,0:T(8,128)(2,1)S(1)} %get-tuple-element.37.head), custom_call_target="tpu_custom_call" | custom-call | flops 939524096 | bytes 6291456 | tf_op jit(solution)/shard_map/pallas_call | solution.py:499
  90.5 1.8 %shard_map.99 = f32[256,1792]{1,0:T(8,128)S(1)} custom-call(s32[6]{0:T(128)S(1)} %stack.36.place, bf16[8,64,1024]{2,1,0:T(8,128)(2,1)S(1)} %get-tuple-element.36.logit_grad.refs_18_, bf16[3584,1024]{1,0:T(8,128)(2,1)S(1)} %get-tuple-element.37.head), custom_call_target="tpu_custom_call" | custom-call | flops 939524096 | bytes 6291456 | tf_op jit(solution)/shard_map/pallas_call | solution.py:499
  94.3 2.0 %shard_map.98 = (f32[16,4,1792]{2,1,0:T(4,128)S(1)}, f32[16,4,1792]{2,1,0:T(4,128)S(1)}, f32[16,4,1792]{2,1,0:T(4,128)S(1)}, f32[16,4,1792]{2,1,0:T(4,128)S(1)}) custom-call(s32[6]{0:T(128)S(1)} %stack.36.place, bf16[8,64,1024]{2,1,0:T(8,128)(2,1)S(1)} %get-tuple-element.36.logit_grad.refs_18_, bf16[3584,1024]{1,0:T(8,128)(2,1)S(1)} %get-tuple-element.37.head, ...), custom_call_target="tpu_custom_call" | custom-call | flops 939524096 | bytes 6291456 | tf_op jit(solution)/shard_map/pallas_call | solution.py:512
  98.2 1.5 collective-permute-start.22
  99.7 2.0 %shard_map.100 = (f32[16,4,1792]{2,1,0:T(4,128)S(1)}, f32[16,4,1792]{2,1,0:T(4,128)S(1)}, f32[16,4,1792]{2,1,0:T(4,128)S(1)}, f32[16,4,1792]{2,1,0:T(4,128)S(1)}) custom-call(s32[6]{0:T(128)S(1)} %stack.36.place, bf16[8,64,1024]{2,1,0:T(8,128)(2,1)S(1)} %get-tuple-element.36.logit_grad.refs_18_, bf16[3584,1024]{1,0:T(8,128)(2,1)S(1)} %get-tuple-element.37.head, ...), custom_call_target="tpu_custom_call" | custom-call | flops 939524096 | bytes 6291456 | tf_op jit(solution)/shard_map/pallas_call | solution.py:512
  102.5 2.2 %collective-permute-start.25 = (f32[16,4,1792]{2,1,0:T(4,128)S(1)}, f32[16,4,1792]{2,1,0:T(4,128)S(1)}, u32[]{:S(2)}, u32[]{:S(2)}) collective-permute-start(f32[16,4,1792]{2,1,0:T(4,128)S(1)} %get-tuple-element.44), channel_id=1, source_target_pairs={{0,8},{1,9},{2,10},{3,11},{4,12},{5,13},{6,14},{7,15},{8,0},{9,1},... | collective-permute-start | bytes 1376264 | tf_op jit(solution)/shard_map/ppermute | solution.py:521
  104.7 6.3 %collective-permute-done.20.refs_1_ = f32[16,4,1792]{2,1,0:T(4,128)S(1)} collective-permute-done((f32[16,4,1792]{2,1,0:T(4,128)S(1)}, f32[16,4,1792]{2,1,0:T(4,128)S(1)}, u32[]{:S(2)}, u32[]{:S(2)}) %collective-permute-start.20) | collective-permute-done | bytes 458784 | tf_op jit(solution)/shard_map/ppermute | solution.py:521
  111.0 10.7 %shard_map.101 = bf16[3584,1024]{1,0:T(8,128)(2,1)} custom-call(s32[6]{0:T(128)S(1)} %stack.36.place, bf16[64,8192]{1,0:T(8,128)(2,1)} %copy-done, bf16[2,64,2048]{2,1,0:T(8,128)(2,1)} %copy-done.2, bf16[2,64,2048]{2,1,0:T(8,128)(2,1)} %copy-done.5, bf16[2,64,2048]{2,1,0:T(8,128)(2,1)} %collective-permute-done.4.refs_3_, ...), custom_call_target="tpu_custom_call" | custom-call | flops 3758096384 | bytes 13631488 | tf_op jit(solution)/shard_map/pallas_call | solution.py:522
  122.8 3.6 %all-to-all-start.1 = ((f32[16,4,3584]{2,1,0:T(4,128)}), f32[16,4,3584]{2,1,0:T(4,128)S(1)}, u32[]{:S(2)}, u32[]{:S(2)}) async-start(f32[16,4,3584]{2,1,0:T(4,128)} %shard_map.102), calls=%async_computation.1 | async-start | bytes 1835008 | tf_op jit(solution)/shard_map/all_to_all | solution.py:550
  126.6 14.8 %all-to-all-done.1.got = f32[16,4,3584]{2,1,0:T(4,128)S(1)} async-done(((f32[16,4,3584]{2,1,0:T(4,128)}), f32[16,4,3584]{2,1,0:T(4,128)S(1)}, u32[]{:S(2)}, u32[]{:S(2)}) %all-to-all-start.1) | async-done | bytes 917536 | tf_op jit(solution)/shard_map/all_to_all | solution.py:550
  142.4 4.1 %all-to-all-start.2 = ((bf16[16,4,3584]{2,1,0:T(4,128)(2,1)}), bf16[16,4,3584]{2,1,0:T(4,128)(2,1)S(1)}, u32[]{:S(2)}, u32[]{:S(2)}) async-start(bf16[16,4,3584]{2,1,0:T(4,128)(2,1)} %shard_map.103), calls=%async_computation.2 | async-start | bytes 917504 | tf_op jit(solution)/shard_map/all_to_all | solution.py:560
  147.3 10.3 %all-to-all-done.2 = bf16[16,4,3584]{2,1,0:T(4,128)(2,1)S(1)} async-done(((bf16[16,4,3584]{2,1,0:T(4,128)(2,1)}), bf16[16,4,3584]{2,1,0:T(4,128)(2,1)S(1)}, u32[]{:S(2)}, u32[]{:S(2)}) %all-to-all-start.2) | async-done | bytes 458784 | tf_op jit(solution)/shard_map/all_to_all | solution.py:560
  (86 shorter events, 19.4 us)
Async XLA Ops:
  2.4 20.3 %collective-permute-start.2 = (bf16[64,8192]{1,0:T(8,128)(2,1)S(1)}, bf16[64,8192]{1,0:T(8,128)(2,1)S(1)}, u32[]{:S(2)}, u32[]{:S(2)}) collective-permute-start(bf16[64,8192]{1,0:T(8,128)(2,1)S(1)} %get-tuple-element.29.refs_0_), channel_id=1, source_target_pairs={{0,16},{1,17},{2,18},{3,19},{4,20},{5,21},{6,22},{7,23},{8,24},{9,... | collective-permute-start | bytes 3145736 | tf_op jit(solution)/shard_map/ppermute | solution.py:60
  2.5 11.2 %collective-permute-start.10 = (bf16[64,2048]{1,0:T(8,128)(2,1)S(1)}, bf16[64,2048]{1,0:T(8,128)(2,1)S(1)}, u32[]{:S(2)}, u32[]{:S(2)}) collective-permute-start(bf16[64,2048]{1,0:T(8,128)(2,1)S(1)} %get-tuple-element.30), channel_id=1, source_target_pairs={{0,64},{1,65},{2,66},{3,67},{4,68},{5,69},{6,70},{7,71},{8,72},{9,... | collective-permute-start | bytes 786440 | tf_op jit(solution)/shard_map/ppermute | solution.py:428
  6.6 13.3 %collective-permute-start.1 = (bf16[64,2048]{1,0:T(8,128)(2,1)S(1)}, bf16[64,2048]{1,0:T(8,128)(2,1)S(1)}, u32[]{:S(2)}, u32[]{:S(2)}) collective-permute-start(bf16[64,2048]{1,0:T(8,128)(2,1)S(1)} %get-tuple-element.30), channel_id=1, source_target_pairs={{0,96},{1,97},{2,98},{3,99},{4,100},{5,101},{6,102},{7,103},{8,104... | collective-permute-start | bytes 786440 | tf_op jit(solution)/shard_map/ppermute | solution.py:428
  7.3 15.3 %collective-permute-start = (bf16[64,2048]{1,0:T(8,128)(2,1)S(1)}, bf16[64,2048]{1,0:T(8,128)(2,1)S(1)}, u32[]{:S(2)}, u32[]{:S(2)}) collective-permute-start(bf16[64,2048]{1,0:T(8,128)(2,1)S(1)} %get-tuple-element.30), channel_id=1, source_target_pairs={{0,32},{1,33},{2,34},{3,35},{4,36},{5,37},{6,38},{7,39},{8,40},{9,... | collective-permute-start | bytes 786440 | tf_op jit(solution)/shard_map/ppermute | solution.py:428
  13.8 11.3 %collective-permute-start.11 = (bf16[1,64,2048]{2,1,0:T(8,128)(2,1)S(1)}, bf16[1,64,2048]{2,1,0:T(8,128)(2,1)S(1)}, u32[]{:S(2)}, u32[]{:S(2)}) collective-permute-start(bf16[1,64,2048]{2,1,0:T(8,128)(2,1)S(1)} %bitcast.18), channel_id=1, source_target_pairs={{0,4},{1,5},{2,6},{3,7},{4,8},{5,9},{6,10},{7,11},{8,12},{9,13},{1... | collective-permute-start | bytes 786440 | tf_op jit(solution)/shard_map/ppermute | solution.py:432
  15.3 11.0 %collective-permute-start.12 = (bf16[1,64,2048]{2,1,0:T(8,128)(2,1)S(1)}, bf16[1,64,2048]{2,1,0:T(8,128)(2,1)S(1)}, u32[]{:S(2)}, u32[]{:S(2)}) collective-permute-start(bf16[1,64,2048]{2,1,0:T(8,128)(2,1)S(1)} %bitcast.19), channel_id=1, source_target_pairs={{0,8},{1,9},{2,10},{3,11},{4,12},{5,13},{6,14},{7,15},{8,0},{9,1},... | collective-permute-start | bytes 786440 | tf_op jit(solution)/shard_map/ppermute | solution.py:432
  19.9 6.6 %collective-permute-start.13 = (bf16[1,64,2048]{2,1,0:T(8,128)(2,1)S(1)}, bf16[1,64,2048]{2,1,0:T(8,128)(2,1)}, u32[]{:S(2)}, u32[]{:S(2)}) collective-permute-start(bf16[1,64,2048]{2,1,0:T(8,128)(2,1)S(1)} %bitcast.20), channel_id=1, source_target_pairs={{0,12},{1,13},{2,14},{3,15},{4,0},{5,1},{6,2},{7,3},{8,4},{9,5},{1... | collective-permute-start | bytes 786440 | tf_op jit(solution)/shard_map/ppermute | solution.py:432
  22.7 16.1 %collective-permute-start.3 = (bf16[2,64,2048]{2,1,0:T(8,128)(2,1)S(1)}, bf16[2,64,2048]{2,1,0:T(8,128)(2,1)S(1)}, u32[]{:S(2)}, u32[]{:S(2)}) collective-permute-start(bf16[2,64,2048]{2,1,0:T(8,128)(2,1)S(1)} %pad_maximum_fusion.refs_1_), channel_id=1, source_target_pairs={{0,4},{1,5},{2,6},{3,7},{4,8},{5,9},{6,10},{7,11},{8,12},{9,13},{1... | collective-permute-start | bytes 1572872 | tf_op jit(solution)/shard_map/ppermute | solution.py:432
  22.8 16.0 %collective-permute-start.4 = (bf16[2,64,2048]{2,1,0:T(8,128)(2,1)S(1)}, bf16[2,64,2048]{2,1,0:T(8,128)(2,1)}, u32[]{:S(2)}, u32[]{:S(2)}) collective-permute-start(bf16[2,64,2048]{2,1,0:T(8,128)(2,1)S(1)} %pad_maximum_fusion.refs_1_), channel_id=1, source_target_pairs={{0,8},{1,9},{2,10},{3,11},{4,12},{5,13},{6,14},{7,15},{8,0},{9,1},... | collective-permute-start | bytes 1572872 | tf_op jit(solution)/shard_map/ppermute | solution.py:432
  25.1 14.7 %collective-permute-start.5 = (bf16[2,64,2048]{2,1,0:T(8,128)(2,1)S(1)}, bf16[2,64,2048]{2,1,0:T(8,128)(2,1)}, u32[]{:S(2)}, u32[]{:S(2)}) collective-permute-start(bf16[2,64,2048]{2,1,0:T(8,128)(2,1)S(1)} %pad_maximum_fusion.refs_1_), channel_id=1, source_target_pairs={{0,12},{1,13},{2,14},{3,15},{4,0},{5,1},{6,2},{7,3},{8,4},{9,5},{1... | collective-permute-start | bytes 1572872 | tf_op jit(solution)/shard_map/ppermute | solution.py:432
  27.8 12.0 %collective-permute-start.16 = (bf16[1,64,2048]{2,1,0:T(8,128)(2,1)S(1)}, bf16[1,64,2048]{2,1,0:T(8,128)(2,1)S(1)}, u32[]{:S(2)}, u32[]{:S(2)}) collective-permute-start(bf16[1,64,2048]{2,1,0:T(8,128)(2,1)S(1)} %collective-permute-done.12.refs_12_), channel_id=1, source_target_pairs={{0,16},{1,17},{2,18},{3,19},{4,20},{5,21},{6,22},{7,23},{8,24},{9,... | collective-permute-start | bytes 786440 | tf_op jit(solution)/shard_map/ppermute | solution.py:60
  28.1 14.8 %collective-permute-start.6 = (bf16[2,64,2048]{2,1,0:T(8,128)(2,1)S(1)}, bf16[2,64,2048]{2,1,0:T(8,128)(2,1)}, u32[]{:S(2)}, u32[]{:S(2)}) collective-permute-start(bf16[2,64,2048]{2,1,0:T(8,128)(2,1)S(1)} %pad_maximum_fusion.refs_1_), channel_id=1, source_target_pairs={{0,16},{1,17},{2,18},{3,19},{4,20},{5,21},{6,22},{7,23},{8,24},{9,... | collective-permute-start | bytes 1572872 | tf_op jit(solution)/shard_map/ppermute | solution.py:60
  38.8 4.1 %collective-permute-start.7 = (bf16[2,64,2048]{2,1,0:T(8,128)(2,1)S(1)}, bf16[2,64,2048]{2,1,0:T(8,128)(2,1)}, u32[]{:S(2)}, u32[]{:S(2)}) collective-permute-start(bf16[2,64,2048]{2,1,0:T(8,128)(2,1)S(1)} %collective-permute-done.3.refs_2_), channel_id=1, source_target_pairs={{0,16},{1,17},{2,18},{3,19},{4,20},{5,21},{6,22},{7,23},{8,24},{9,... | collective-permute-start | bytes 1572872 | tf_op jit(solution)/shard_map/ppermute | solution.py:60
  38.8 4.1 %collective-permute-start.8 = (bf16[2,64,2048]{2,1,0:T(8,128)(2,1)}, bf16[2,64,2048]{2,1,0:T(8,128)(2,1)}, u32[]{:S(2)}, u32[]{:S(2)}) collective-permute-start(bf16[2,64,2048]{2,1,0:T(8,128)(2,1)} %collective-permute-done.4.refs_3_), channel_id=1, source_target_pairs={{0,16},{1,17},{2,18},{3,19},{4,20},{5,21},{6,22},{7,23},{8,24},{9,... | collective-permute-start | bytes 1572872 | tf_op jit(solution)/shard_map/ppermute | solution.py:60
  90.2 4.1 %collective-permute-start.19 = (f32[256,1792]{1,0:T(8,128)S(1)}, f32[256,1792]{1,0:T(8,128)S(1)}, u32[]{:S(2)}, u32[]{:S(2)}) collective-permute-start(f32[256,1792]{1,0:T(8,128)S(1)} %shard_map.97), channel_id=1, source_target_pairs={{0,16},{1,17},{2,18},{3,19},{4,20},{5,21},{6,22},{7,23},{8,24},{9,... | collective-permute-start | bytes 5505032 | tf_op jit(solution)/shard_map/ppermute | solution.py:60
  92.4 7.4 %collective-permute-start.23 = (f32[256,1792]{1,0:T(8,128)S(1)}, f32[256,1792]{1,0:T(8,128)S(1)}, u32[]{:S(2)}, u32[]{:S(2)}) collective-permute-start(f32[256,1792]{1,0:T(8,128)S(1)} %shard_map.99), channel_id=1, source_target_pairs={{0,16},{1,17},{2,18},{3,19},{4,20},{5,21},{6,22},{7,23},{8,24},{9,... | collective-permute-start | bytes 5505032 | tf_op jit(solution)/shard_map/ppermute | solution.py:60
  96.3 14.7 %collective-permute-start.20 = (f32[16,4,1792]{2,1,0:T(4,128)S(1)}, f32[16,4,1792]{2,1,0:T(4,128)S(1)}, u32[]{:S(2)}, u32[]{:S(2)}) collective-permute-start(f32[16,4,1792]{2,1,0:T(4,128)S(1)} %get-tuple-element.39), channel_id=1, source_target_pairs={{0,4},{1,5},{2,6},{3,7},{4,8},{5,9},{6,10},{7,11},{8,12},{9,13},{1... | collective-permute-start | bytes 1376264 | tf_op jit(solution)/shard_map/ppermute | solution.py:521
  97.0 24.7 %collective-permute-start.21 = (f32[16,4,1792]{2,1,0:T(4,128)S(1)}, f32[16,4,1792]{2,1,0:T(4,128)S(1)}, u32[]{:S(2)}, u32[]{:S(2)}) collective-permute-start(f32[16,4,1792]{2,1,0:T(4,128)S(1)} %get-tuple-element.40), channel_id=1, source_target_pairs={{0,8},{1,9},{2,10},{3,11},{4,12},{5,13},{6,14},{7,15},{8,0},{9,1},... | collective-permute-start | bytes 1376264 | tf_op jit(solution)/shard_map/ppermute | solution.py:521
  98.2 23.4 %collective-permute-start.22 = (f32[16,4,1792]{2,1,0:T(4,128)S(1)}, f32[16,4,1792]{2,1,0:T(4,128)S(1)}, u32[]{:S(2)}, u32[]{:S(2)}) collective-permute-start(f32[16,4,1792]{2,1,0:T(4,128)S(1)} %get-tuple-element.41), channel_id=1, source_target_pairs={{0,12},{1,13},{2,14},{3,15},{4,0},{5,1},{6,2},{7,3},{8,4},{9,5},{1... | collective-permute-start | bytes 1376264 | tf_op jit(solution)/shard_map/ppermute | solution.py:521
  101.7 19.9 %collective-permute-start.24 = (f32[16,4,1792]{2,1,0:T(4,128)S(1)}, f32[16,4,1792]{2,1,0:T(4,128)S(1)}, u32[]{:S(2)}, u32[]{:S(2)}) collective-permute-start(f32[16,4,1792]{2,1,0:T(4,128)S(1)} %get-tuple-element.43), channel_id=1, source_target_pairs={{0,4},{1,5},{2,6},{3,7},{4,8},{5,9},{6,10},{7,11},{8,12},{9,13},{1... | collective-permute-start | bytes 1376264 | tf_op jit(solution)/shard_map/ppermute | solution.py:521
  102.5 19.1 %collective-permute-start.25 = (f32[16,4,1792]{2,1,0:T(4,128)S(1)}, f32[16,4,1792]{2,1,0:T(4,128)S(1)}, u32[]{:S(2)}, u32[]{:S(2)}) collective-permute-start(f32[16,4,1792]{2,1,0:T(4,128)S(1)} %get-tuple-element.44), channel_id=1, source_target_pairs={{0,8},{1,9},{2,10},{3,11},{4,12},{5,13},{6,14},{7,15},{8,0},{9,1},... | collective-permute-start | bytes 1376264 | tf_op jit(solution)/shard_map/ppermute | solution.py:521
  111.0 10.8 %collective-permute-start.26 = (f32[16,4,1792]{2,1,0:T(4,128)S(1)}, f32[16,4,1792]{2,1,0:T(4,128)S(1)}, u32[]{:S(2)}, u32[]{:S(2)}) collective-permute-start(f32[16,4,1792]{2,1,0:T(4,128)S(1)} %get-tuple-element.45), channel_id=1, source_target_pairs={{0,12},{1,13},{2,14},{3,15},{4,0},{5,1},{6,2},{7,3},{8,4},{9,5},{1... | collective-permute-start | bytes 1376264 | tf_op jit(solution)/shard_map/ppermute | solution.py:521
  122.8 18.6 %all-to-all-start.1 = ((f32[16,4,3584]{2,1,0:T(4,128)}), f32[16,4,3584]{2,1,0:T(4,128)S(1)}, u32[]{:S(2)}, u32[]{:S(2)}) async-start(f32[16,4,3584]{2,1,0:T(4,128)} %shard_map.102), calls=%async_computation.1 | async-start | bytes 1835008 | tf_op jit(solution)/shard_map/all_to_all | solution.py:550
  142.4 15.2 %all-to-all-start.2 = ((bf16[16,4,3584]{2,1,0:T(4,128)(2,1)}), bf16[16,4,3584]{2,1,0:T(4,128)(2,1)S(1)}, u32[]{:S(2)}, u32[]{:S(2)}) async-start(bf16[16,4,3584]{2,1,0:T(4,128)(2,1)} %shard_map.103), calls=%async_computation.2 | async-start | bytes 917504 | tf_op jit(solution)/shard_map/all_to_all | solution.py:560
  (18 other events, 239.6 us)

commit v4 on v3

--- a/solution.py
+++ b/solution.py
@@ -237,33 +237,57 @@
         out_copy(student_cap, student_out, 1, b).wait()
 
 
-def grad_kernel(
-    place, teacher_in, student_in, totals, labels, head, logit_grad, head_here,
-    teacher_exp, student_cap, sems, head_sem,
-):
+def back_dot(logit_grad, head, n):
+    return lax.dot_general(
+        logit_grad[...].reshape(4 * OWN, COLS),
+        head[n * LANES : n * LANES + LANES, :],
+        (((1,), (1,)), ((), ())),
+        preferred_element_type=jnp.float32,
+    )
+
+
+def grad_kernel(part, place, teacher_in, student_in, totals, labels, head, *refs):
+    logit_grad, head_here, out, teacher_exp, student_cap, sems, head_sem = refs[part:]
+    other = place[1] if part else 1 - place[1]
+    first = pl.multiple_of(other * (ROWS // 2), ROWS // 2)
     copies = []
-    for i in range(4):
-        at = pl.ds(128 * i, 128)
+    for i in range(2):
+        at, here = pl.ds(pl.multiple_of(first + 128 * i, 128), 128), pl.ds(128 * i, 128)
         copies.append(
             [
-                pltpu.make_async_copy(teacher_in.at[at, :], teacher_exp.at[at, :], sems.at[i, 0]),
-                pltpu.make_async_copy(student_in.at[at, :], student_cap.at[at, :], sems.at[i, 1]),
+                pltpu.make_async_copy(teacher_in.at[at, :], teacher_exp.at[here, :], sems.at[i, 0]),
+                pltpu.make_async_copy(student_in.at[at, :], student_cap.at[here, :], sems.at[i, 1]),
             ]
         )
-        begin(copies[-1])
-    head_copy = pltpu.make_async_copy(head, head_here, head_sem)
-    head_copy.start()
+    head_copy = pltpu.make_async_copy(
+        head.at[pl.ds(part * (D_S // 2), D_S // 2), :], head_here, head_sem
+    )
+
+    def upstream(rows):
+        head_copy.wait()
+        for n in range(D_S // 2 // LANES):
+            out[:, n * LANES : n * LANES + LANES] = back_dot(rows, head_here, n)
+
+    if part:
+        head_copy.start()
+        for group in copies:
+            begin(group)
+        upstream(refs[0])
+    else:
+        for group in copies:
+            begin(group)
+        head_copy.start()
     columns = place[4] + lax.broadcasted_iota(jnp.int32, (1, COLS), 1)
-    for i in range(4):
+    for i in range(2):
 
         def column(kind):
-            at = 4 * kind + i
-            return jnp.broadcast_to(totals[at : at + 1, :], (128, 128)).T
+            row = totals[pl.ds(4 * kind + 2 * other + i, 1), :]
+            return jnp.broadcast_to(row, (128, 128)).T
 
         teacher_scale = KL_WEIGHT / column(0)
         student_scale = 1.0 / column(1)
         block = slice(128 * i, 128 * i + 128)
-        label = labels[block, :]
+        label = labels[pl.ds(pl.multiple_of(first + 128 * i, 128), 128), :]
         finish(copies[i])
         for j in range(COLS // 128):
             lanes = slice(128 * j, 128 * j + 128)
@@ -277,26 +301,25 @@
             ) * (1.0 - ratio * ratio)
             logit_grad[2 * i, :, lanes] = grad[:OWN].astype(jnp.bfloat16)
             logit_grad[2 * i + 1, :, lanes] = grad[OWN:].astype(jnp.bfloat16)
-    head_copy.wait()
-
-
-def back_dot(logit_grad, core, head, part, n):
-    rows = logit_grad[pl.ds(4 * core, 4)].reshape(4 * OWN, COLS)
-    start = part * (D_S // 2) + n * LANES
-    return lax.dot_general(
-        rows,
-        head[start : start + LANES, :],
-        (((1,), (1,)), ((), ())),
-        preferred_element_type=jnp.float32,
-    )
+    if not part:
+        upstream(logit_grad)
 
 
 def head_grad_kernel(place, *refs):
     received = refs[:18]
-    logit_grad, out, rows, buffers, sems, out_sems = refs[18:]
-    groups = collect(place, all_pieces(received), rows, functools.partial(row_start, place), sems)
+    mine, theirs, out, rows, logit_grad, buffers, sems, out_sems = refs[18:]
+    side = len(FARS) * OWN
+    groups = collect(
+        place,
+        all_pieces(received),
+        rows,
+        lambda k, far: k * side + pl.multiple_of((place[0] + 4 - far) % 4 * OWN, OWN),
+        sems,
+    )
     for group in groups:
         begin(group)
+    logit_grad[:side, :] = mine[...].reshape(side, COLS)
+    logit_grad[side:, :] = theirs[...].reshape(side, COLS)
     for group in groups:
         finish(group)
     step = D_S // HEAD_STEPS
@@ -310,7 +333,7 @@
         lanes = slice(D_T + step * n, D_T + step * n + step)
         value = lax.dot_general(
             rows[:, lanes],
-            logit_grad[...].reshape(ROWS, COLS),
+            logit_grad[...],
             (((0,), (0,)), ((), ())),
             preferred_element_type=jnp.float32,
         )
@@ -322,16 +345,11 @@
         copy_out(n).wait()
 
 
-def theirs_kernel(part, place, logit_grad, head, out):
-    for n in range(D_S // 2 // LANES):
-        out[:, n * LANES : n * LANES + LANES] = back_dot(logit_grad, 1 - place[1], head, part, n)
-
-
-def mine_kernel(part, place, logit_grad, head, received, *rest):
+def mine_kernel(place, logit_grad, head, received, *rest):
     *outs, value = rest
     for n in range(D_S // 2 // LANES):
         lanes = slice(n * LANES, n * LANES + LANES)
-        value[...] = back_dot(logit_grad, place[1], head, part, n) + received[:, lanes]
+        value[...] = back_dot(logit_grad, head, n) + received[:, lanes]
         for e, out in enumerate(outs):
             for z in range(4):
                 at = pl.multiple_of(z * OWN + ((place[2] + e) % 4) * 16, 16)
@@ -468,64 +486,55 @@
 
     totals = sum_everywhere(sums)
 
-    logit_grad, head_here = pl.pallas_call(
-        grad_kernel,
-        out_shape=[
-            jax.ShapeDtypeStruct((8, OWN, COLS), jnp.bfloat16),
-            jax.ShapeDtypeStruct((D_S, COLS), jnp.bfloat16),
-        ],
-        in_specs=[smem] + [any_space] * 2 + [vmem] * 2 + [any_space],
-        out_specs=[vmem] * 2,
-        scratch_shapes=[
-            pltpu.VMEM((ROWS, COLS), jnp.float32),
-            pltpu.VMEM((ROWS, COLS), jnp.float32),
-            pltpu.SemaphoreType.DMA((4, 2)),
-            pltpu.SemaphoreType.DMA,
-        ],
-        compiler_params=limit(10),
-        cost_estimate=pl.CostEstimate(
-            flops=8 * ROWS * COLS, bytes_accessed=5 * MIB, transcendentals=ROWS * COLS
-        ),
-    )(
-        place, in_hbm(teacher_exp), in_hbm(student_cap), totals, labels_here,
-        in_hbm(student_head),
-    )
-
     back_cost = pl.CostEstimate(
-        flops=4 * OWN * COLS * D_S, bytes_accessed=6 * MIB, transcendentals=0
-    )
-    theirs = [
-        swap(
-            pl.pallas_call(
-                functools.partial(theirs_kernel, part),
-                out_shape=jax.ShapeDtypeStruct((4 * OWN, D_S // 2), jnp.float32),
-                in_specs=[smem, vmem, vmem],
-                out_specs=vmem,
-                compiler_params=limit(6),
-                cost_estimate=back_cost,
-            )(place, logit_grad, head_here)
+        flops=4 * OWN * COLS * D_S, bytes_accessed=6 * MIB, transcendentals=ROWS * COLS // 2
+    )
+    grads, heads_here, theirs = [], [], []
+    for part in range(2):
+        grad, head_here, out = pl.pallas_call(
+            functools.partial(grad_kernel, part),
+            out_shape=[
+                jax.ShapeDtypeStruct((4, OWN, COLS), jnp.bfloat16),
+                jax.ShapeDtypeStruct((D_S // 2, COLS), jnp.bfloat16),
+                jax.ShapeDtypeStruct((4 * OWN, D_S // 2), jnp.float32),
+            ],
+            in_specs=[smem] + [any_space] * 2 + [vmem] * 2 + [any_space] + [vmem] * part,
+            out_specs=[vmem] * 3,
+            scratch_shapes=[
+                pltpu.VMEM((ROWS // 2, COLS), jnp.float32),
+                pltpu.VMEM((ROWS // 2, COLS), jnp.float32),
+                pltpu.SemaphoreType.DMA((2, 2)),
+                pltpu.SemaphoreType.DMA,
+            ],
+            compiler_params=limit(10),
+            cost_estimate=back_cost,
+        )(
+            place, in_hbm(teacher_exp), in_hbm(student_cap), totals, labels_here,
+            in_hbm(student_head), *grads,
         )
-        for part in range(2)
-    ]
+        grads.append(grad)
+        heads_here.append(head_here)
+        theirs.append(swap(out))
     slabs = []
     for part in range(2):
         mine = pl.pallas_call(
-            functools.partial(mine_kernel, part),
+            mine_kernel,
             out_shape=[jax.ShapeDtypeStruct((16, 4, D_S // 2), jnp.float32)] * 4,
             in_specs=[smem, vmem, vmem, vmem],
             out_specs=[vmem] * 4,
             scratch_shapes=[pltpu.VMEM((4 * OWN, LANES), jnp.float32)],
             compiler_params=limit(8),
             cost_estimate=back_cost,
-        )(place, logit_grad, head_here, theirs[part])
+        )(place, grads[1], heads_here[part], theirs[part])
         slabs += [mine[0]] + [lax.ppermute(mine[e], AXES, ALONG_LINE[e]) for e in (1, 2, 3)]
     head_grad = pl.pallas_call(
         head_grad_kernel,
         out_shape=pltpu.HBM((D_S, COLS), jnp.bfloat16),
-        in_specs=[smem] + [any_space] * 18 + [vmem],
+        in_specs=[smem] + [any_space] * 18 + [vmem] * 2,
         out_specs=any_space,
         scratch_shapes=[
             pltpu.VMEM((ROWS, D_ALL), jnp.bfloat16),
+            pltpu.VMEM((ROWS, COLS), jnp.bfloat16),
             pltpu.VMEM((2, D_S // HEAD_STEPS, COLS), jnp.bfloat16),
             pltpu.SemaphoreType.DMA((26,)),
             pltpu.SemaphoreType.DMA((2,)),
@@ -534,7 +543,7 @@
         cost_estimate=pl.CostEstimate(
             flops=2 * ROWS * D_S * COLS, bytes_accessed=13 * MIB, transcendentals=0
         ),
-    )(place, *map(in_hbm, pieces), logit_grad)
+    )(place, *map(in_hbm, pieces), grads[1], grads[0])
     *slabs, head_grad = lax.optimization_barrier((*slabs, head_grad))
     got = pl.pallas_call(
         line_sum_kernel,

time: 159 us -> 158 us (level)
    pallas_call x5 -> x4, Pallas kernels: 12.6 us -> 13 us  [the longest x2 9.04 us: body(): pl.pallas_call(functools.partial(grad_kernel, part), out_shape=[jax.Shape...]
  transfers between devices with their start and end apart: 29 -> 29, of which waited for: 14 -> 13; matrix products, arithmetic and copies ran while one was open for 1% -> 1% of each run, Pallas kernels for 10% -> 12%
where the time goes in v4:
time: 158 us; the launch traced here: 157 us
  waiting for transfers between devices  53.8 us (34%)
  Pallas kernels  44 us (28%)
  starting transfers between devices  33.7 us (21%)
  blocking collectives  22.5 us (14%)
  local copies, waits for them, and re-layouts  2.27 us (1%)
    all_to_all x1, blocking collectives, sum_everywhere(): lax.all_to_all(copies, AXES, 0, 0, tiled=True, axis_index_groups=CHIPS)  22.5 us
    pallas_call x1, Pallas kernels, body(): pl.pallas_call(forward_kernel, out_shape=[pltpu.HBM((ROWS, COLS), jnp.flo...  16.6 us
    all_to_all x1, waiting for transfers between devices, body(): got = lax.all_to_all(got, AXES, 0, 0, tiled=True, axis_index_groups=WALLS)  14.7 us
    ppermute x6, waiting for transfers between devices, along_line(): lax.ppermute(value, AXES, ALONG_LINE[e])  11.3 us
    pallas_call x1, Pallas kernels, body(): pl.pallas_call(head_grad_kernel, out_shape=pltpu.HBM((D_S, COLS), jnp.bfl...  10.6 us
    ppermute x6, starting transfers between devices, along_line(): lax.ppermute(value, AXES, ALONG_LINE[e])  10.5 us
    all_to_all x1, waiting for transfers between devices, body(): lax.all_to_all(hidden_grad, AXES, 0, 0, tiled=True, axis_index_groups=PLA...  10.3 us
    pallas_call x2, Pallas kernels, body(): pl.pallas_call(functools.partial(grad_kernel, part), out_shape=[jax.Shape...  9.04 us
  transfers between devices with their start and end apart: 29, of which 13 were waited for; matrix products, arithmetic and copies ran while one was open for 1% of the time, Pallas kernels for 12%

profile of v4, /device:TPU:0, one launch (start us, length us, event | category | flops | bytes accessed | tf_op | source)
XLA Modules:
  0.0 157.4 jit_solution(5178450214581044523)
XLA Ops:
  0.6 1.8 %shard_map.94 = (bf16[64,8192]{1,0:T(8,128)(2,1)S(1)}, bf16[64,2048]{1,0:T(8,128)(2,1)S(1)}) custom-call(bf16[64,4608]{1,0:T(8,128)(2,1)} %bitcast.17, bf16[64,3584]{1,0:T(8,128)(2,1)} %bitcast.16, f32[4608]{0:T(1024)} %refs_2_.1, f32[3584]{0:T(1024)} %gain.1), custom_call_target="tpu_custom_call" | custom-call | tf_op jit(solution)/shard_map/pallas_call | solution.py:421
  2.5 4.0 %collective-permute-start.10 = (bf16[64,2048]{1,0:T(8,128)(2,1)S(1)}, bf16[64,2048]{1,0:T(8,128)(2,1)S(1)}, u32[]{:S(2)}, u32[]{:S(2)}) collective-permute-start(bf16[64,2048]{1,0:T(8,128)(2,1)S(1)} %get-tuple-element.34), channel_id=1, source_target_pairs={{0,64},{1,65},{2,66},{3,67},{4,68},{5,69},{6,70},{7,71},{8,72},{9,... | collective-permute-start | bytes 786440 | tf_op jit(solution)/shard_map/ppermute | solution.py:446
  8.6 5.2 %collective-permute-done.10 = bf16[64,2048]{1,0:T(8,128)(2,1)S(1)} collective-permute-done((bf16[64,2048]{1,0:T(8,128)(2,1)S(1)}, bf16[64,2048]{1,0:T(8,128)(2,1)S(1)}, u32[]{:S(2)}, u32[]{:S(2)}) %collective-permute-start.10) | collective-permute-done | bytes 262176 | tf_op jit(solution)/shard_map/ppermute | solution.py:446
  13.8 1.5 collective-permute-start.11
  15.3 2.7 %collective-permute-start.12 = (bf16[1,64,2048]{2,1,0:T(8,128)(2,1)S(1)}, bf16[1,64,2048]{2,1,0:T(8,128)(2,1)S(1)}, u32[]{:S(2)}, u32[]{:S(2)}) collective-permute-start(bf16[1,64,2048]{2,1,0:T(8,128)(2,1)S(1)} %bitcast.19), channel_id=1, source_target_pairs={{0,8},{1,9},{2,10},{3,11},{4,12},{5,13},{6,14},{7,15},{8,0},{9,1},... | collective-permute-start | bytes 786440 | tf_op jit(solution)/shard_map/ppermute | solution.py:450
  18.0 1.9 %collective-permute-done.1 = bf16[64,2048]{1,0:T(8,128)(2,1)S(1)} collective-permute-done((bf16[64,2048]{1,0:T(8,128)(2,1)S(1)}, bf16[64,2048]{1,0:T(8,128)(2,1)S(1)}, u32[]{:S(2)}, u32[]{:S(2)}) %collective-permute-start.1) | collective-permute-done | bytes 262176 | tf_op jit(solution)/shard_map/ppermute | solution.py:446
  19.9 2.8 %collective-permute-start.13 = (bf16[1,64,2048]{2,1,0:T(8,128)(2,1)S(1)}, bf16[1,64,2048]{2,1,0:T(8,128)(2,1)}, u32[]{:S(2)}, u32[]{:S(2)}) collective-permute-start(bf16[1,64,2048]{2,1,0:T(8,128)(2,1)S(1)} %bitcast.20), channel_id=1, source_target_pairs={{0,12},{1,13},{2,14},{3,15},{4,0},{5,1},{6,2},{7,3},{8,4},{9,5},{1... | collective-permute-start | bytes 786440 | tf_op jit(solution)/shard_map/ppermute | solution.py:450
  22.8 2.3 %collective-permute-start.4 = (bf16[2,64,2048]{2,1,0:T(8,128)(2,1)S(1)}, bf16[2,64,2048]{2,1,0:T(8,128)(2,1)}, u32[]{:S(2)}, u32[]{:S(2)}) collective-permute-start(bf16[2,64,2048]{2,1,0:T(8,128)(2,1)S(1)} %pad_maximum_fusion.refs_1_), channel_id=1, source_target_pairs={{0,8},{1,9},{2,10},{3,11},{4,12},{5,13},{6,14},{7,15},{8,0},{9,1},... | collective-permute-start | bytes 1572872 | tf_op jit(solution)/shard_map/ppermute | solution.py:450
  28.3 10.5 %collective-permute-done.3.refs_2_ = bf16[2,64,2048]{2,1,0:T(8,128)(2,1)S(1)} collective-permute-done((bf16[2,64,2048]{2,1,0:T(8,128)(2,1)S(1)}, bf16[2,64,2048]{2,1,0:T(8,128)(2,1)S(1)}, u32[]{:S(2)}, u32[]{:S(2)}) %collective-permute-start.3) | collective-permute-done | bytes 524320 | tf_op jit(solution)/shard_map/ppermute | solution.py:450
  41.1 1.9 %collective-permute-done.17.refs_17_ = bf16[1,64,2048]{2,1,0:T(8,128)(2,1)} collective-permute-done((bf16[1,64,2048]{2,1,0:T(8,128)(2,1)}, bf16[1,64,2048]{2,1,0:T(8,128)(2,1)}, u32[]{:S(2)}, u32[]{:S(2)}) %collective-permute-start.17) | collective-permute-done | bytes 262176 | tf_op jit(solution)/shard_map/ppermute | solution.py:60
  43.0 16.6 %shard_map.95 = (f32[512,1024]{1,0:T(8,128)}, f32[512,1024]{1,0:T(8,128)}, f32[16,128]{1,0:T(8,128)S(1)}) custom-call(s32[6]{0:T(128)S(1)} %stack.36.place, bf16[64,8192]{1,0:T(8,128)(2,1)} %copy-done, bf16[2,64,2048]{2,1,0:T(8,128)(2,1)} %copy-done.2, bf16[2,64,2048]{2,1,0:T(8,128)(2,1)} %copy-done.5, bf16[2,64,2048]{2,1,0:T(8,128)(2,1)} %collective-permute-done.4.refs_3_, ...), custom_call_target="tpu_custom_call" | custom-call | flops 8589934592 | bytes 31457280 | tf_op jit(solution)/shard_map/pallas_call | solution.py:455
  60.9 22.5 %all_to_all.15 = f32[64,16,128]{2,1,0:T(8,128)S(1)} all-to-all(f32[64,16,128]{2,1,0:T(8,128)S(1)} %broadcast_in_dim.10), channel_id=1, replica_groups={{0,1,2,3,4,5,6,7,8,9,10,11,12,13,14,15,32,33,34,35,36,37,38,39,40,41,42..., dimensions={0} | all-to-all | bytes 1048576 | tf_op jit(solution)/shard_map/all_to_all | solution.py:402
  83.4 4.6 %shard_map.96 = (bf16[4,64,1024]{2,1,0:T(8,128)(2,1)S(1)}, bf16[1792,1024]{1,0:T(8,128)(2,1)S(1)}, f32[256,1792]{1,0:T(8,128)S(1)}) custom-call(s32[6]{0:T(128)S(1)} %stack.36.place, f32[512,1024]{1,0:T(8,128)} %get-tuple-element.38.teacher_in, f32[512,1024]{1,0:T(8,128)} %get-tuple-element.39.student_in, f32[16,128]{1,0:T(8,128)S(1)} %reduce_sum.9.totals, ...), custom_call_target="tpu_custom_call" | custom-call | flops 939524096 | bytes 6291456 | tf_op jit(solution)/shard_map/pallas_call | solution.py:494
  88.3 4.5 %shard_map.97 = (bf16[4,64,1024]{2,1,0:T(8,128)(2,1)S(1)}, bf16[1792,1024]{1,0:T(8,128)(2,1)S(1)}, f32[256,1792]{1,0:T(8,128)S(1)}) custom-call(s32[6]{0:T(128)S(1)} %stack.36.place, f32[512,1024]{1,0:T(8,128)} %get-tuple-element.38.teacher_in, f32[512,1024]{1,0:T(8,128)} %get-tuple-element.39.student_in, f32[16,128]{1,0:T(8,128)S(1)} %reduce_sum.9.totals, ...), custom_call_target="tpu_custom_call" | custom-call | flops 939524096 | bytes 6291456 | tf_op jit(solution)/shard_map/pallas_call | solution.py:494
  93.4 2.0 %shard_map.98 = (f32[16,4,1792]{2,1,0:T(4,128)S(1)}, f32[16,4,1792]{2,1,0:T(4,128)S(1)}, f32[16,4,1792]{2,1,0:T(4,128)S(1)}, f32[16,4,1792]{2,1,0:T(4,128)S(1)}) custom-call(s32[6]{0:T(128)S(1)} %stack.36.place, bf16[4,64,1024]{2,1,0:T(8,128)(2,1)S(1)} %get-tuple-element.41.logit_grad.refs_18_, bf16[1792,1024]{1,0:T(8,128)(2,1)S(1)} %get-tuple-element.42.head, ...), custom_call_target="tpu_custom_call" | custom-call | flops 939524096 | bytes 6291456 | tf_op jit(solution)/shard_map/pallas_call | solution.py:520
  97.3 1.5 collective-permute-start.22
  98.8 2.0 %shard_map.99 = (f32[16,4,1792]{2,1,0:T(4,128)S(1)}, f32[16,4,1792]{2,1,0:T(4,128)S(1)}, f32[16,4,1792]{2,1,0:T(4,128)S(1)}, f32[16,4,1792]{2,1,0:T(4,128)S(1)}) custom-call(s32[6]{0:T(128)S(1)} %stack.36.place, bf16[4,64,1024]{2,1,0:T(8,128)(2,1)S(1)} %get-tuple-element.41.logit_grad.refs_18_, bf16[1792,1024]{1,0:T(8,128)(2,1)S(1)} %get-tuple-element.48.head, ...), custom_call_target="tpu_custom_call" | custom-call | flops 939524096 | bytes 6291456 | tf_op jit(solution)/shard_map/pallas_call | solution.py:520
  101.6 2.2 %collective-permute-start.25 = (f32[16,4,1792]{2,1,0:T(4,128)S(1)}, f32[16,4,1792]{2,1,0:T(4,128)S(1)}, u32[]{:S(2)}, u32[]{:S(2)}) collective-permute-start(f32[16,4,1792]{2,1,0:T(4,128)S(1)} %get-tuple-element.52), channel_id=1, source_target_pairs={{0,8},{1,9},{2,10},{3,11},{4,12},{5,13},{6,14},{7,15},{8,0},{9,1},... | collective-permute-start | bytes 1376264 | tf_op jit(solution)/shard_map/ppermute | solution.py:529
  103.7 6.3 %collective-permute-done.20.refs_1_ = f32[16,4,1792]{2,1,0:T(4,128)S(1)} collective-permute-done((f32[16,4,1792]{2,1,0:T(4,128)S(1)}, f32[16,4,1792]{2,1,0:T(4,128)S(1)}, u32[]{:S(2)}, u32[]{:S(2)}) %collective-permute-start.20) | collective-permute-done | bytes 458784 | tf_op jit(solution)/shard_map/ppermute | solution.py:529
  110.0 10.6 %shard_map.100 = bf16[3584,1024]{1,0:T(8,128)(2,1)} custom-call(s32[6]{0:T(128)S(1)} %stack.36.place, bf16[64,8192]{1,0:T(8,128)(2,1)} %copy-done, bf16[2,64,2048]{2,1,0:T(8,128)(2,1)} %copy-done.2, bf16[2,64,2048]{2,1,0:T(8,128)(2,1)} %copy-done.5, bf16[2,64,2048]{2,1,0:T(8,128)(2,1)} %collective-permute-done.4.refs_3_, ...), custom_call_target="tpu_custom_call" | custom-call | flops 3758096384 | bytes 13631488 | tf_op jit(solution)/shard_map/pallas_call | solution.py:530
  121.9 3.6 %all-to-all-start.1 = ((f32[16,4,3584]{2,1,0:T(4,128)}), f32[16,4,3584]{2,1,0:T(4,128)S(1)}, u32[]{:S(2)}, u32[]{:S(2)}) async-start(f32[16,4,3584]{2,1,0:T(4,128)} %shard_map.101), calls=%async_computation.1 | async-start | bytes 1835008 | tf_op jit(solution)/shard_map/all_to_all | solution.py:559
  125.7 14.7 %all-to-all-done.1.got = f32[16,4,3584]{2,1,0:T(4,128)S(1)} async-done(((f32[16,4,3584]{2,1,0:T(4,128)}), f32[16,4,3584]{2,1,0:T(4,128)S(1)}, u32[]{:S(2)}, u32[]{:S(2)}) %all-to-all-start.1) | async-done | bytes 917536 | tf_op jit(solution)/shard_map/all_to_all | solution.py:559
  141.3 4.2 %all-to-all-start.2 = ((bf16[16,4,3584]{2,1,0:T(4,128)(2,1)}), bf16[16,4,3584]{2,1,0:T(4,128)(2,1)S(1)}, u32[]{:S(2)}, u32[]{:S(2)}) async-start(bf16[16,4,3584]{2,1,0:T(4,128)(2,1)} %shard_map.102), calls=%async_computation.2 | async-start | bytes 917504 | tf_op jit(solution)/shard_map/all_to_all | solution.py:569
  146.2 10.3 %all-to-all-done.2 = bf16[16,4,3584]{2,1,0:T(4,128)(2,1)S(1)} async-done(((bf16[16,4,3584]{2,1,0:T(4,128)(2,1)}), bf16[16,4,3584]{2,1,0:T(4,128)(2,1)S(1)}, u32[]{:S(2)}, u32[]{:S(2)}) %all-to-all-start.2) | async-done | bytes 458784 | tf_op jit(solution)/shard_map/all_to_all | solution.py:569
  (85 shorter events, 16.5 us)
Async XLA Ops:
  2.4 20.3 %collective-permute-start.2 = (bf16[64,8192]{1,0:T(8,128)(2,1)S(1)}, bf16[64,8192]{1,0:T(8,128)(2,1)S(1)}, u32[]{:S(2)}, u32[]{:S(2)}) collective-permute-start(bf16[64,8192]{1,0:T(8,128)(2,1)S(1)} %get-tuple-element.33.refs_0_), channel_id=1, source_target_pairs={{0,16},{1,17},{2,18},{3,19},{4,20},{5,21},{6,22},{7,23},{8,24},{9,... | collective-permute-start | bytes 3145736 | tf_op jit(solution)/shard_map/ppermute | solution.py:60
  2.5 11.2 %collective-permute-start.10 = (bf16[64,2048]{1,0:T(8,128)(2,1)S(1)}, bf16[64,2048]{1,0:T(8,128)(2,1)S(1)}, u32[]{:S(2)}, u32[]{:S(2)}) collective-permute-start(bf16[64,2048]{1,0:T(8,128)(2,1)S(1)} %get-tuple-element.34), channel_id=1, source_target_pairs={{0,64},{1,65},{2,66},{3,67},{4,68},{5,69},{6,70},{7,71},{8,72},{9,... | collective-permute-start | bytes 786440 | tf_op jit(solution)/shard_map/ppermute | solution.py:446
  6.6 13.3 %collective-permute-start.1 = (bf16[64,2048]{1,0:T(8,128)(2,1)S(1)}, bf16[64,2048]{1,0:T(8,128)(2,1)S(1)}, u32[]{:S(2)}, u32[]{:S(2)}) collective-permute-start(bf16[64,2048]{1,0:T(8,128)(2,1)S(1)} %get-tuple-element.34), channel_id=1, source_target_pairs={{0,96},{1,97},{2,98},{3,99},{4,100},{5,101},{6,102},{7,103},{8,104... | collective-permute-start | bytes 786440 | tf_op jit(solution)/shard_map/ppermute | solution.py:446
  7.3 15.3 %collective-permute-start = (bf16[64,2048]{1,0:T(8,128)(2,1)S(1)}, bf16[64,2048]{1,0:T(8,128)(2,1)S(1)}, u32[]{:S(2)}, u32[]{:S(2)}) collective-permute-start(bf16[64,2048]{1,0:T(8,128)(2,1)S(1)} %get-tuple-element.34), channel_id=1, source_target_pairs={{0,32},{1,33},{2,34},{3,35},{4,36},{5,37},{6,38},{7,39},{8,40},{9,... | collective-permute-start | bytes 786440 | tf_op jit(solution)/shard_map/ppermute | solution.py:446
  13.8 11.3 %collective-permute-start.11 = (bf16[1,64,2048]{2,1,0:T(8,128)(2,1)S(1)}, bf16[1,64,2048]{2,1,0:T(8,128)(2,1)S(1)}, u32[]{:S(2)}, u32[]{:S(2)}) collective-permute-start(bf16[1,64,2048]{2,1,0:T(8,128)(2,1)S(1)} %bitcast.18), channel_id=1, source_target_pairs={{0,4},{1,5},{2,6},{3,7},{4,8},{5,9},{6,10},{7,11},{8,12},{9,13},{1... | collective-permute-start | bytes 786440 | tf_op jit(solution)/shard_map/ppermute | solution.py:450
  15.3 11.0 %collective-permute-start.12 = (bf16[1,64,2048]{2,1,0:T(8,128)(2,1)S(1)}, bf16[1,64,2048]{2,1,0:T(8,128)(2,1)S(1)}, u32[]{:S(2)}, u32[]{:S(2)}) collective-permute-start(bf16[1,64,2048]{2,1,0:T(8,128)(2,1)S(1)} %bitcast.19), channel_id=1, source_target_pairs={{0,8},{1,9},{2,10},{3,11},{4,12},{5,13},{6,14},{7,15},{8,0},{9,1},... | collective-permute-start | bytes 786440 | tf_op jit(solution)/shard_map/ppermute | solution.py:450
  19.9 6.6 %collective-permute-start.13 = (bf16[1,64,2048]{2,1,0:T(8,128)(2,1)S(1)}, bf16[1,64,2048]{2,1,0:T(8,128)(2,1)}, u32[]{:S(2)}, u32[]{:S(2)}) collective-permute-start(bf16[1,64,2048]{2,1,0:T(8,128)(2,1)S(1)} %bitcast.20), channel_id=1, source_target_pairs={{0,12},{1,13},{2,14},{3,15},{4,0},{5,1},{6,2},{7,3},{8,4},{9,5},{1... | collective-permute-start | bytes 786440 | tf_op jit(solution)/shard_map/ppermute | solution.py:450
  22.7 16.1 %collective-permute-start.3 = (bf16[2,64,2048]{2,1,0:T(8,128)(2,1)S(1)}, bf16[2,64,2048]{2,1,0:T(8,128)(2,1)S(1)}, u32[]{:S(2)}, u32[]{:S(2)}) collective-permute-start(bf16[2,64,2048]{2,1,0:T(8,128)(2,1)S(1)} %pad_maximum_fusion.refs_1_), channel_id=1, source_target_pairs={{0,4},{1,5},{2,6},{3,7},{4,8},{5,9},{6,10},{7,11},{8,12},{9,13},{1... | collective-permute-start | bytes 1572872 | tf_op jit(solution)/shard_map/ppermute | solution.py:450
  22.8 16.0 %collective-permute-start.4 = (bf16[2,64,2048]{2,1,0:T(8,128)(2,1)S(1)}, bf16[2,64,2048]{2,1,0:T(8,128)(2,1)}, u32[]{:S(2)}, u32[]{:S(2)}) collective-permute-start(bf16[2,64,2048]{2,1,0:T(8,128)(2,1)S(1)} %pad_maximum_fusion.refs_1_), channel_id=1, source_target_pairs={{0,8},{1,9},{2,10},{3,11},{4,12},{5,13},{6,14},{7,15},{8,0},{9,1},... | collective-permute-start | bytes 1572872 | tf_op jit(solution)/shard_map/ppermute | solution.py:450
  25.1 14.7 %collective-permute-start.5 = (bf16[2,64,2048]{2,1,0:T(8,128)(2,1)S(1)}, bf16[2,64,2048]{2,1,0:T(8,128)(2,1)}, u32[]{:S(2)}, u32[]{:S(2)}) collective-permute-start(bf16[2,64,2048]{2,1,0:T(8,128)(2,1)S(1)} %pad_maximum_fusion.refs_1_), channel_id=1, source_target_pairs={{0,12},{1,13},{2,14},{3,15},{4,0},{5,1},{6,2},{7,3},{8,4},{9,5},{1... | collective-permute-start | bytes 1572872 | tf_op jit(solution)/shard_map/ppermute | solution.py:450
  27.8 12.0 %collective-permute-start.16 = (bf16[1,64,2048]{2,1,0:T(8,128)(2,1)S(1)}, bf16[1,64,2048]{2,1,0:T(8,128)(2,1)S(1)}, u32[]{:S(2)}, u32[]{:S(2)}) collective-permute-start(bf16[1,64,2048]{2,1,0:T(8,128)(2,1)S(1)} %collective-permute-done.12.refs_12_), channel_id=1, source_target_pairs={{0,16},{1,17},{2,18},{3,19},{4,20},{5,21},{6,22},{7,23},{8,24},{9,... | collective-permute-start | bytes 786440 | tf_op jit(solution)/shard_map/ppermute | solution.py:60
  28.1 14.8 %collective-permute-start.6 = (bf16[2,64,2048]{2,1,0:T(8,128)(2,1)S(1)}, bf16[2,64,2048]{2,1,0:T(8,128)(2,1)}, u32[]{:S(2)}, u32[]{:S(2)}) collective-permute-start(bf16[2,64,2048]{2,1,0:T(8,128)(2,1)S(1)} %pad_maximum_fusion.refs_1_), channel_id=1, source_target_pairs={{0,16},{1,17},{2,18},{3,19},{4,20},{5,21},{6,22},{7,23},{8,24},{9,... | collective-permute-start | bytes 1572872 | tf_op jit(solution)/shard_map/ppermute | solution.py:60
  38.8 4.1 %collective-permute-start.7 = (bf16[2,64,2048]{2,1,0:T(8,128)(2,1)S(1)}, bf16[2,64,2048]{2,1,0:T(8,128)(2,1)}, u32[]{:S(2)}, u32[]{:S(2)}) collective-permute-start(bf16[2,64,2048]{2,1,0:T(8,128)(2,1)S(1)} %collective-permute-done.3.refs_2_), channel_id=1, source_target_pairs={{0,16},{1,17},{2,18},{3,19},{4,20},{5,21},{6,22},{7,23},{8,24},{9,... | collective-permute-start | bytes 1572872 | tf_op jit(solution)/shard_map/ppermute | solution.py:60
  38.8 4.1 %collective-permute-start.8 = (bf16[2,64,2048]{2,1,0:T(8,128)(2,1)}, bf16[2,64,2048]{2,1,0:T(8,128)(2,1)}, u32[]{:S(2)}, u32[]{:S(2)}) collective-permute-start(bf16[2,64,2048]{2,1,0:T(8,128)(2,1)} %collective-permute-done.4.refs_3_), channel_id=1, source_target_pairs={{0,16},{1,17},{2,18},{3,19},{4,20},{5,21},{6,22},{7,23},{8,24},{9,... | collective-permute-start | bytes 1572872 | tf_op jit(solution)/shard_map/ppermute | solution.py:60
  88.0 5.4 %collective-permute-start.19 = (f32[256,1792]{1,0:T(8,128)S(1)}, f32[256,1792]{1,0:T(8,128)S(1)}, u32[]{:S(2)}, u32[]{:S(2)}) collective-permute-start(f32[256,1792]{1,0:T(8,128)S(1)} %get-tuple-element.43), channel_id=1, source_target_pairs={{0,16},{1,17},{2,18},{3,19},{4,20},{5,21},{6,22},{7,23},{8,24},{9,... | collective-permute-start | bytes 5505032 | tf_op jit(solution)/shard_map/ppermute | solution.py:60
  92.8 6.0 %collective-permute-start.23 = (f32[256,1792]{1,0:T(8,128)S(1)}, f32[256,1792]{1,0:T(8,128)S(1)}, u32[]{:S(2)}, u32[]{:S(2)}) collective-permute-start(f32[256,1792]{1,0:T(8,128)S(1)} %get-tuple-element.49), channel_id=1, source_target_pairs={{0,16},{1,17},{2,18},{3,19},{4,20},{5,21},{6,22},{7,23},{8,24},{9,... | collective-permute-start | bytes 5505032 | tf_op jit(solution)/shard_map/ppermute | solution.py:60
  95.4 14.7 %collective-permute-start.20 = (f32[16,4,1792]{2,1,0:T(4,128)S(1)}, f32[16,4,1792]{2,1,0:T(4,128)S(1)}, u32[]{:S(2)}, u32[]{:S(2)}) collective-permute-start(f32[16,4,1792]{2,1,0:T(4,128)S(1)} %get-tuple-element.45), channel_id=1, source_target_pairs={{0,4},{1,5},{2,6},{3,7},{4,8},{5,9},{6,10},{7,11},{8,12},{9,13},{1... | collective-permute-start | bytes 1376264 | tf_op jit(solution)/shard_map/ppermute | solution.py:529
  96.0 24.7 %collective-permute-start.21 = (f32[16,4,1792]{2,1,0:T(4,128)S(1)}, f32[16,4,1792]{2,1,0:T(4,128)S(1)}, u32[]{:S(2)}, u32[]{:S(2)}) collective-permute-start(f32[16,4,1792]{2,1,0:T(4,128)S(1)} %get-tuple-element.46), channel_id=1, source_target_pairs={{0,8},{1,9},{2,10},{3,11},{4,12},{5,13},{6,14},{7,15},{8,0},{9,1},... | collective-permute-start | bytes 1376264 | tf_op jit(solution)/shard_map/ppermute | solution.py:529
  97.3 23.4 %collective-permute-start.22 = (f32[16,4,1792]{2,1,0:T(4,128)S(1)}, f32[16,4,1792]{2,1,0:T(4,128)S(1)}, u32[]{:S(2)}, u32[]{:S(2)}) collective-permute-start(f32[16,4,1792]{2,1,0:T(4,128)S(1)} %get-tuple-element.47), channel_id=1, source_target_pairs={{0,12},{1,13},{2,14},{3,15},{4,0},{5,1},{6,2},{7,3},{8,4},{9,5},{1... | collective-permute-start | bytes 1376264 | tf_op jit(solution)/shard_map/ppermute | solution.py:529
  100.8 19.9 %collective-permute-start.24 = (f32[16,4,1792]{2,1,0:T(4,128)S(1)}, f32[16,4,1792]{2,1,0:T(4,128)S(1)}, u32[]{:S(2)}, u32[]{:S(2)}) collective-permute-start(f32[16,4,1792]{2,1,0:T(4,128)S(1)} %get-tuple-element.51), channel_id=1, source_target_pairs={{0,4},{1,5},{2,6},{3,7},{4,8},{5,9},{6,10},{7,11},{8,12},{9,13},{1... | collective-permute-start | bytes 1376264 | tf_op jit(solution)/shard_map/ppermute | solution.py:529
  101.6 19.1 %collective-permute-start.25 = (f32[16,4,1792]{2,1,0:T(4,128)S(1)}, f32[16,4,1792]{2,1,0:T(4,128)S(1)}, u32[]{:S(2)}, u32[]{:S(2)}) collective-permute-start(f32[16,4,1792]{2,1,0:T(4,128)S(1)} %get-tuple-element.52), channel_id=1, source_target_pairs={{0,8},{1,9},{2,10},{3,11},{4,12},{5,13},{6,14},{7,15},{8,0},{9,1},... | collective-permute-start | bytes 1376264 | tf_op jit(solution)/shard_map/ppermute | solution.py:529
  110.0 10.8 %collective-permute-start.26 = (f32[16,4,1792]{2,1,0:T(4,128)S(1)}, f32[16,4,1792]{2,1,0:T(4,128)S(1)}, u32[]{:S(2)}, u32[]{:S(2)}) collective-permute-start(f32[16,4,1792]{2,1,0:T(4,128)S(1)} %get-tuple-element.53), channel_id=1, source_target_pairs={{0,12},{1,13},{2,14},{3,15},{4,0},{5,1},{6,2},{7,3},{8,4},{9,5},{1... | collective-permute-start | bytes 1376264 | tf_op jit(solution)/shard_map/ppermute | solution.py:529
  121.9 18.5 %all-to-all-start.1 = ((f32[16,4,3584]{2,1,0:T(4,128)}), f32[16,4,3584]{2,1,0:T(4,128)S(1)}, u32[]{:S(2)}, u32[]{:S(2)}) async-start(f32[16,4,3584]{2,1,0:T(4,128)} %shard_map.101), calls=%async_computation.1 | async-start | bytes 1835008 | tf_op jit(solution)/shard_map/all_to_all | solution.py:559
  141.3 15.2 %all-to-all-start.2 = ((bf16[16,4,3584]{2,1,0:T(4,128)(2,1)}), bf16[16,4,3584]{2,1,0:T(4,128)(2,1)S(1)}, u32[]{:S(2)}, u32[]{:S(2)}) async-start(bf16[16,4,3584]{2,1,0:T(4,128)(2,1)} %shard_map.102), calls=%async_computation.2 | async-start | bytes 917504 | tf_op jit(solution)/shard_map/all_to_all | solution.py:569
  (18 other events, 239.5 us)

commit v5 on v4

--- a/solution.py
+++ b/solution.py
@@ -122,7 +122,7 @@
         copy.wait()
 
 
-CHUNK = 1024
+CHUNK = 1536
 BUFFERS = 3
 
 
@@ -472,7 +472,7 @@
             pltpu.SemaphoreType.DMA((BUFFERS,)),
             pltpu.SemaphoreType.DMA((2, 8)),
         ],
-        compiler_params=limit(32),
+        compiler_params=limit(38),
         cost_estimate=pl.CostEstimate(
             flops=2 * ROWS * D_ALL * COLS, bytes_accessed=30 * MIB, transcendentals=4 * ROWS * COLS
         ),

time: 158 us -> 158 us (level)
  no operation moved by 1% of the time
where the time goes in v5:
time: 158 us
  waiting for transfers between devices  53.7 us (34%)
  Pallas kernels  44.3 us (28%)
  starting transfers between devices  33.7 us (21%)
  blocking collectives  22.5 us (14%)
  local copies, waits for them, and re-layouts  2.27 us (1%)
    all_to_all x1, blocking collectives, sum_everywhere(): lax.all_to_all(copies, AXES, 0, 0, tiled=True, axis_index_groups=CHIPS)  22.5 us
    pallas_call x1, Pallas kernels, body(): pl.pallas_call(forward_kernel, out_shape=[pltpu.HBM((ROWS, COLS), jnp.flo...  16.8 us
    all_to_all x1, waiting for transfers between devices, body(): got = lax.all_to_all(got, AXES, 0, 0, tiled=True, axis_index_groups=WALLS)  14.7 us
    ppermute x6, waiting for transfers between devices, along_line(): lax.ppermute(value, AXES, ALONG_LINE[e])  11.3 us
    pallas_call x1, Pallas kernels, body(): pl.pallas_call(head_grad_kernel, out_shape=pltpu.HBM((D_S, COLS), jnp.bfl...  10.6 us
    ppermute x6, starting transfers between devices, along_line(): lax.ppermute(value, AXES, ALONG_LINE[e])  10.5 us
    all_to_all x1, waiting for transfers between devices, body(): lax.all_to_all(hidden_grad, AXES, 0, 0, tiled=True, axis_index_groups=PLA...  10.3 us
    pallas_call x2, Pallas kernels, body(): pl.pallas_call(functools.partial(grad_kernel, part), out_shape=[jax.Shape...  9.04 us
  transfers between devices with their start and end apart: 29, of which 13 were waited for; matrix products, arithmetic and copies ran while one was open for 1% of the time, Pallas kernels for 12%

profile of v5, /device:TPU:0, one launch (start us, length us, event | category | flops | bytes accessed | tf_op | source)
XLA Modules:
  0.0 157.6 jit_solution(4969412494622437034)
XLA Ops:
  0.6 1.8 %shard_map.94 = (bf16[64,8192]{1,0:T(8,128)(2,1)S(1)}, bf16[64,2048]{1,0:T(8,128)(2,1)S(1)}) custom-call(bf16[64,4608]{1,0:T(8,128)(2,1)} %bitcast.17, bf16[64,3584]{1,0:T(8,128)(2,1)} %bitcast.16, f32[4608]{0:T(1024)} %refs_2_.1, f32[3584]{0:T(1024)} %gain.1), custom_call_target="tpu_custom_call" | custom-call | tf_op jit(solution)/shard_map/pallas_call | solution.py:421
  2.5 4.0 %collective-permute-start.10 = (bf16[64,2048]{1,0:T(8,128)(2,1)S(1)}, bf16[64,2048]{1,0:T(8,128)(2,1)S(1)}, u32[]{:S(2)}, u32[]{:S(2)}) collective-permute-start(bf16[64,2048]{1,0:T(8,128)(2,1)S(1)} %get-tuple-element.34), channel_id=1, source_target_pairs={{0,64},{1,65},{2,66},{3,67},{4,68},{5,69},{6,70},{7,71},{8,72},{9,... | collective-permute-start | bytes 786440 | tf_op jit(solution)/shard_map/ppermute | solution.py:446
  8.6 5.2 %collective-permute-done.10 = bf16[64,2048]{1,0:T(8,128)(2,1)S(1)} collective-permute-done((bf16[64,2048]{1,0:T(8,128)(2,1)S(1)}, bf16[64,2048]{1,0:T(8,128)(2,1)S(1)}, u32[]{:S(2)}, u32[]{:S(2)}) %collective-permute-start.10) | collective-permute-done | bytes 262176 | tf_op jit(solution)/shard_map/ppermute | solution.py:446
  13.8 1.5 collective-permute-start.11
  15.3 2.7 %collective-permute-start.12 = (bf16[1,64,2048]{2,1,0:T(8,128)(2,1)S(1)}, bf16[1,64,2048]{2,1,0:T(8,128)(2,1)S(1)}, u32[]{:S(2)}, u32[]{:S(2)}) collective-permute-start(bf16[1,64,2048]{2,1,0:T(8,128)(2,1)S(1)} %bitcast.19), channel_id=1, source_target_pairs={{0,8},{1,9},{2,10},{3,11},{4,12},{5,13},{6,14},{7,15},{8,0},{9,1},... | collective-permute-start | bytes 786440 | tf_op jit(solution)/shard_map/ppermute | solution.py:450
  18.0 1.9 %collective-permute-done.1 = bf16[64,2048]{1,0:T(8,128)(2,1)S(1)} collective-permute-done((bf16[64,2048]{1,0:T(8,128)(2,1)S(1)}, bf16[64,2048]{1,0:T(8,128)(2,1)S(1)}, u32[]{:S(2)}, u32[]{:S(2)}) %collective-permute-start.1) | collective-permute-done | bytes 262176 | tf_op jit(solution)/shard_map/ppermute | solution.py:446
  19.9 2.8 %collective-permute-start.13 = (bf16[1,64,2048]{2,1,0:T(8,128)(2,1)S(1)}, bf16[1,64,2048]{2,1,0:T(8,128)(2,1)}, u32[]{:S(2)}, u32[]{:S(2)}) collective-permute-start(bf16[1,64,2048]{2,1,0:T(8,128)(2,1)S(1)} %bitcast.20), channel_id=1, source_target_pairs={{0,12},{1,13},{2,14},{3,15},{4,0},{5,1},{6,2},{7,3},{8,4},{9,5},{1... | collective-permute-start | bytes 786440 | tf_op jit(solution)/shard_map/ppermute | solution.py:450
  22.8 2.3 %collective-permute-start.4 = (bf16[2,64,2048]{2,1,0:T(8,128)(2,1)S(1)}, bf16[2,64,2048]{2,1,0:T(8,128)(2,1)}, u32[]{:S(2)}, u32[]{:S(2)}) collective-permute-start(bf16[2,64,2048]{2,1,0:T(8,128)(2,1)S(1)} %pad_maximum_fusion.refs_1_), channel_id=1, source_target_pairs={{0,8},{1,9},{2,10},{3,11},{4,12},{5,13},{6,14},{7,15},{8,0},{9,1},... | collective-permute-start | bytes 1572872 | tf_op jit(solution)/shard_map/ppermute | solution.py:450
  28.3 10.5 %collective-permute-done.3.refs_2_ = bf16[2,64,2048]{2,1,0:T(8,128)(2,1)S(1)} collective-permute-done((bf16[2,64,2048]{2,1,0:T(8,128)(2,1)S(1)}, bf16[2,64,2048]{2,1,0:T(8,128)(2,1)S(1)}, u32[]{:S(2)}, u32[]{:S(2)}) %collective-permute-start.3) | collective-permute-done | bytes 524320 | tf_op jit(solution)/shard_map/ppermute | solution.py:450
  41.1 1.9 %collective-permute-done.17.refs_17_ = bf16[1,64,2048]{2,1,0:T(8,128)(2,1)} collective-permute-done((bf16[1,64,2048]{2,1,0:T(8,128)(2,1)}, bf16[1,64,2048]{2,1,0:T(8,128)(2,1)}, u32[]{:S(2)}, u32[]{:S(2)}) %collective-permute-start.17) | collective-permute-done | bytes 262176 | tf_op jit(solution)/shard_map/ppermute | solution.py:60
  43.0 16.8 %shard_map.95 = (f32[512,1024]{1,0:T(8,128)}, f32[512,1024]{1,0:T(8,128)}, f32[16,128]{1,0:T(8,128)S(1)}) custom-call(s32[6]{0:T(128)S(1)} %stack.36.place, bf16[64,8192]{1,0:T(8,128)(2,1)} %copy-done, bf16[2,64,2048]{2,1,0:T(8,128)(2,1)} %copy-done.2, bf16[2,64,2048]{2,1,0:T(8,128)(2,1)} %copy-done.5, bf16[2,64,2048]{2,1,0:T(8,128)(2,1)} %collective-permute-done.4.refs_3_, ...), custom_call_target="tpu_custom_call" | custom-call | flops 8589934592 | bytes 31457280 | tf_op jit(solution)/shard_map/pallas_call | solution.py:455
  61.1 22.5 %all_to_all.15 = f32[64,16,128]{2,1,0:T(8,128)S(1)} all-to-all(f32[64,16,128]{2,1,0:T(8,128)S(1)} %broadcast_in_dim.10), channel_id=1, replica_groups={{0,1,2,3,4,5,6,7,8,9,10,11,12,13,14,15,32,33,34,35,36,37,38,39,40,41,42..., dimensions={0} | all-to-all | bytes 1048576 | tf_op jit(solution)/shard_map/all_to_all | solution.py:402
  83.7 4.6 %shard_map.96 = (bf16[4,64,1024]{2,1,0:T(8,128)(2,1)S(1)}, bf16[1792,1024]{1,0:T(8,128)(2,1)S(1)}, f32[256,1792]{1,0:T(8,128)S(1)}) custom-call(s32[6]{0:T(128)S(1)} %stack.36.place, f32[512,1024]{1,0:T(8,128)} %get-tuple-element.38.teacher_in, f32[512,1024]{1,0:T(8,128)} %get-tuple-element.39.student_in, f32[16,128]{1,0:T(8,128)S(1)} %reduce_sum.9.totals, ...), custom_call_target="tpu_custom_call" | custom-call | flops 939524096 | bytes 6291456 | tf_op jit(solution)/shard_map/pallas_call | solution.py:494
  88.6 4.5 %shard_map.97 = (bf16[4,64,1024]{2,1,0:T(8,128)(2,1)S(1)}, bf16[1792,1024]{1,0:T(8,128)(2,1)S(1)}, f32[256,1792]{1,0:T(8,128)S(1)}) custom-call(s32[6]{0:T(128)S(1)} %stack.36.place, f32[512,1024]{1,0:T(8,128)} %get-tuple-element.38.teacher_in, f32[512,1024]{1,0:T(8,128)} %get-tuple-element.39.student_in, f32[16,128]{1,0:T(8,128)S(1)} %reduce_sum.9.totals, ...), custom_call_target="tpu_custom_call" | custom-call | flops 939524096 | bytes 6291456 | tf_op jit(solution)/shard_map/pallas_call | solution.py:494
  93.6 2.0 %shard_map.98 = (f32[16,4,1792]{2,1,0:T(4,128)S(1)}, f32[16,4,1792]{2,1,0:T(4,128)S(1)}, f32[16,4,1792]{2,1,0:T(4,128)S(1)}, f32[16,4,1792]{2,1,0:T(4,128)S(1)}) custom-call(s32[6]{0:T(128)S(1)} %stack.36.place, bf16[4,64,1024]{2,1,0:T(8,128)(2,1)S(1)} %get-tuple-element.41.logit_grad.refs_18_, bf16[1792,1024]{1,0:T(8,128)(2,1)S(1)} %get-tuple-element.42.head, ...), custom_call_target="tpu_custom_call" | custom-call | flops 939524096 | bytes 6291456 | tf_op jit(solution)/shard_map/pallas_call | solution.py:520
  97.5 1.5 collective-permute-start.22
  99.0 2.0 %shard_map.99 = (f32[16,4,1792]{2,1,0:T(4,128)S(1)}, f32[16,4,1792]{2,1,0:T(4,128)S(1)}, f32[16,4,1792]{2,1,0:T(4,128)S(1)}, f32[16,4,1792]{2,1,0:T(4,128)S(1)}) custom-call(s32[6]{0:T(128)S(1)} %stack.36.place, bf16[4,64,1024]{2,1,0:T(8,128)(2,1)S(1)} %get-tuple-element.41.logit_grad.refs_18_, bf16[1792,1024]{1,0:T(8,128)(2,1)S(1)} %get-tuple-element.48.head, ...), custom_call_target="tpu_custom_call" | custom-call | flops 939524096 | bytes 6291456 | tf_op jit(solution)/shard_map/pallas_call | solution.py:520
  101.8 2.2 %collective-permute-start.25 = (f32[16,4,1792]{2,1,0:T(4,128)S(1)}, f32[16,4,1792]{2,1,0:T(4,128)S(1)}, u32[]{:S(2)}, u32[]{:S(2)}) collective-permute-start(f32[16,4,1792]{2,1,0:T(4,128)S(1)} %get-tuple-element.52), channel_id=1, source_target_pairs={{0,8},{1,9},{2,10},{3,11},{4,12},{5,13},{6,14},{7,15},{8,0},{9,1},... | collective-permute-start | bytes 1376264 | tf_op jit(solution)/shard_map/ppermute | solution.py:529
  104.0 6.3 %collective-permute-done.20.refs_1_ = f32[16,4,1792]{2,1,0:T(4,128)S(1)} collective-permute-done((f32[16,4,1792]{2,1,0:T(4,128)S(1)}, f32[16,4,1792]{2,1,0:T(4,128)S(1)}, u32[]{:S(2)}, u32[]{:S(2)}) %collective-permute-start.20) | collective-permute-done | bytes 458784 | tf_op jit(solution)/shard_map/ppermute | solution.py:529
  110.3 10.6 %shard_map.100 = bf16[3584,1024]{1,0:T(8,128)(2,1)} custom-call(s32[6]{0:T(128)S(1)} %stack.36.place, bf16[64,8192]{1,0:T(8,128)(2,1)} %copy-done, bf16[2,64,2048]{2,1,0:T(8,128)(2,1)} %copy-done.2, bf16[2,64,2048]{2,1,0:T(8,128)(2,1)} %copy-done.5, bf16[2,64,2048]{2,1,0:T(8,128)(2,1)} %collective-permute-done.4.refs_3_, ...), custom_call_target="tpu_custom_call" | custom-call | flops 3758096384 | bytes 13631488 | tf_op jit(solution)/shard_map/pallas_call | solution.py:530
  122.1 3.6 %all-to-all-start.1 = ((f32[16,4,3584]{2,1,0:T(4,128)}), f32[16,4,3584]{2,1,0:T(4,128)S(1)}, u32[]{:S(2)}, u32[]{:S(2)}) async-start(f32[16,4,3584]{2,1,0:T(4,128)} %shard_map.101), calls=%async_computation.1 | async-start | bytes 1835008 | tf_op jit(solution)/shard_map/all_to_all | solution.py:559
  125.9 14.7 %all-to-all-done.1.got = f32[16,4,3584]{2,1,0:T(4,128)S(1)} async-done(((f32[16,4,3584]{2,1,0:T(4,128)}), f32[16,4,3584]{2,1,0:T(4,128)S(1)}, u32[]{:S(2)}, u32[]{:S(2)}) %all-to-all-start.1) | async-done | bytes 917536 | tf_op jit(solution)/shard_map/all_to_all | solution.py:559
  141.5 4.2 %all-to-all-start.2 = ((bf16[16,4,3584]{2,1,0:T(4,128)(2,1)}), bf16[16,4,3584]{2,1,0:T(4,128)(2,1)S(1)}, u32[]{:S(2)}, u32[]{:S(2)}) async-start(bf16[16,4,3584]{2,1,0:T(4,128)(2,1)} %shard_map.102), calls=%async_computation.2 | async-start | bytes 917504 | tf_op jit(solution)/shard_map/all_to_all | solution.py:569
  146.5 10.3 %all-to-all-done.2 = bf16[16,4,3584]{2,1,0:T(4,128)(2,1)S(1)} async-done(((bf16[16,4,3584]{2,1,0:T(4,128)(2,1)}), bf16[16,4,3584]{2,1,0:T(4,128)(2,1)S(1)}, u32[]{:S(2)}, u32[]{:S(2)}) %all-to-all-start.2) | async-done | bytes 458784 | tf_op jit(solution)/shard_map/all_to_all | solution.py:569
  (85 shorter events, 16.5 us)
Async XLA Ops:
  2.4 20.3 %collective-permute-start.2 = (bf16[64,8192]{1,0:T(8,128)(2,1)S(1)}, bf16[64,8192]{1,0:T(8,128)(2,1)S(1)}, u32[]{:S(2)}, u32[]{:S(2)}) collective-permute-start(bf16[64,8192]{1,0:T(8,128)(2,1)S(1)} %get-tuple-element.33.refs_0_), channel_id=1, source_target_pairs={{0,16},{1,17},{2,18},{3,19},{4,20},{5,21},{6,22},{7,23},{8,24},{9,... | collective-permute-start | bytes 3145736 | tf_op jit(solution)/shard_map/ppermute | solution.py:60
  2.5 11.2 %collective-permute-start.10 = (bf16[64,2048]{1,0:T(8,128)(2,1)S(1)}, bf16[64,2048]{1,0:T(8,128)(2,1)S(1)}, u32[]{:S(2)}, u32[]{:S(2)}) collective-permute-start(bf16[64,2048]{1,0:T(8,128)(2,1)S(1)} %get-tuple-element.34), channel_id=1, source_target_pairs={{0,64},{1,65},{2,66},{3,67},{4,68},{5,69},{6,70},{7,71},{8,72},{9,... | collective-permute-start | bytes 786440 | tf_op jit(solution)/shard_map/ppermute | solution.py:446
  6.6 13.3 %collective-permute-start.1 = (bf16[64,2048]{1,0:T(8,128)(2,1)S(1)}, bf16[64,2048]{1,0:T(8,128)(2,1)S(1)}, u32[]{:S(2)}, u32[]{:S(2)}) collective-permute-start(bf16[64,2048]{1,0:T(8,128)(2,1)S(1)} %get-tuple-element.34), channel_id=1, source_target_pairs={{0,96},{1,97},{2,98},{3,99},{4,100},{5,101},{6,102},{7,103},{8,104... | collective-permute-start | bytes 786440 | tf_op jit(solution)/shard_map/ppermute | solution.py:446
  7.3 15.3 %collective-permute-start = (bf16[64,2048]{1,0:T(8,128)(2,1)S(1)}, bf16[64,2048]{1,0:T(8,128)(2,1)S(1)}, u32[]{:S(2)}, u32[]{:S(2)}) collective-permute-start(bf16[64,2048]{1,0:T(8,128)(2,1)S(1)} %get-tuple-element.34), channel_id=1, source_target_pairs={{0,32},{1,33},{2,34},{3,35},{4,36},{5,37},{6,38},{7,39},{8,40},{9,... | collective-permute-start | bytes 786440 | tf_op jit(solution)/shard_map/ppermute | solution.py:446
  13.8 11.3 %collective-permute-start.11 = (bf16[1,64,2048]{2,1,0:T(8,128)(2,1)S(1)}, bf16[1,64,2048]{2,1,0:T(8,128)(2,1)S(1)}, u32[]{:S(2)}, u32[]{:S(2)}) collective-permute-start(bf16[1,64,2048]{2,1,0:T(8,128)(2,1)S(1)} %bitcast.18), channel_id=1, source_target_pairs={{0,4},{1,5},{2,6},{3,7},{4,8},{5,9},{6,10},{7,11},{8,12},{9,13},{1... | collective-permute-start | bytes 786440 | tf_op jit(solution)/shard_map/ppermute | solution.py:450
  15.3 11.0 %collective-permute-start.12 = (bf16[1,64,2048]{2,1,0:T(8,128)(2,1)S(1)}, bf16[1,64,2048]{2,1,0:T(8,128)(2,1)S(1)}, u32[]{:S(2)}, u32[]{:S(2)}) collective-permute-start(bf16[1,64,2048]{2,1,0:T(8,128)(2,1)S(1)} %bitcast.19), channel_id=1, source_target_pairs={{0,8},{1,9},{2,10},{3,11},{4,12},{5,13},{6,14},{7,15},{8,0},{9,1},... | collective-permute-start | bytes 786440 | tf_op jit(solution)/shard_map/ppermute | solution.py:450
  19.9 6.6 %collective-permute-start.13 = (bf16[1,64,2048]{2,1,0:T(8,128)(2,1)S(1)}, bf16[1,64,2048]{2,1,0:T(8,128)(2,1)}, u32[]{:S(2)}, u32[]{:S(2)}) collective-permute-start(bf16[1,64,2048]{2,1,0:T(8,128)(2,1)S(1)} %bitcast.20), channel_id=1, source_target_pairs={{0,12},{1,13},{2,14},{3,15},{4,0},{5,1},{6,2},{7,3},{8,4},{9,5},{1... | collective-permute-start | bytes 786440 | tf_op jit(solution)/shard_map/ppermute | solution.py:450
  22.7 16.1 %collective-permute-start.3 = (bf16[2,64,2048]{2,1,0:T(8,128)(2,1)S(1)}, bf16[2,64,2048]{2,1,0:T(8,128)(2,1)S(1)}, u32[]{:S(2)}, u32[]{:S(2)}) collective-permute-start(bf16[2,64,2048]{2,1,0:T(8,128)(2,1)S(1)} %pad_maximum_fusion.refs_1_), channel_id=1, source_target_pairs={{0,4},{1,5},{2,6},{3,7},{4,8},{5,9},{6,10},{7,11},{8,12},{9,13},{1... | collective-permute-start | bytes 1572872 | tf_op jit(solution)/shard_map/ppermute | solution.py:450
  22.8 16.0 %collective-permute-start.4 = (bf16[2,64,2048]{2,1,0:T(8,128)(2,1)S(1)}, bf16[2,64,2048]{2,1,0:T(8,128)(2,1)}, u32[]{:S(2)}, u32[]{:S(2)}) collective-permute-start(bf16[2,64,2048]{2,1,0:T(8,128)(2,1)S(1)} %pad_maximum_fusion.refs_1_), channel_id=1, source_target_pairs={{0,8},{1,9},{2,10},{3,11},{4,12},{5,13},{6,14},{7,15},{8,0},{9,1},... | collective-permute-start | bytes 1572872 | tf_op jit(solution)/shard_map/ppermute | solution.py:450
  25.1 14.7 %collective-permute-start.5 = (bf16[2,64,2048]{2,1,0:T(8,128)(2,1)S(1)}, bf16[2,64,2048]{2,1,0:T(8,128)(2,1)}, u32[]{:S(2)}, u32[]{:S(2)}) collective-permute-start(bf16[2,64,2048]{2,1,0:T(8,128)(2,1)S(1)} %pad_maximum_fusion.refs_1_), channel_id=1, source_target_pairs={{0,12},{1,13},{2,14},{3,15},{4,0},{5,1},{6,2},{7,3},{8,4},{9,5},{1... | collective-permute-start | bytes 1572872 | tf_op jit(solution)/shard_map/ppermute | solution.py:450
  27.8 12.0 %collective-permute-start.16 = (bf16[1,64,2048]{2,1,0:T(8,128)(2,1)S(1)}, bf16[1,64,2048]{2,1,0:T(8,128)(2,1)S(1)}, u32[]{:S(2)}, u32[]{:S(2)}) collective-permute-start(bf16[1,64,2048]{2,1,0:T(8,128)(2,1)S(1)} %collective-permute-done.12.refs_12_), channel_id=1, source_target_pairs={{0,16},{1,17},{2,18},{3,19},{4,20},{5,21},{6,22},{7,23},{8,24},{9,... | collective-permute-start | bytes 786440 | tf_op jit(solution)/shard_map/ppermute | solution.py:60
  28.1 14.8 %collective-permute-start.6 = (bf16[2,64,2048]{2,1,0:T(8,128)(2,1)S(1)}, bf16[2,64,2048]{2,1,0:T(8,128)(2,1)}, u32[]{:S(2)}, u32[]{:S(2)}) collective-permute-start(bf16[2,64,2048]{2,1,0:T(8,128)(2,1)S(1)} %pad_maximum_fusion.refs_1_), channel_id=1, source_target_pairs={{0,16},{1,17},{2,18},{3,19},{4,20},{5,21},{6,22},{7,23},{8,24},{9,... | collective-permute-start | bytes 1572872 | tf_op jit(solution)/shard_map/ppermute | solution.py:60
  38.8 4.1 %collective-permute-start.7 = (bf16[2,64,2048]{2,1,0:T(8,128)(2,1)S(1)}, bf16[2,64,2048]{2,1,0:T(8,128)(2,1)}, u32[]{:S(2)}, u32[]{:S(2)}) collective-permute-start(bf16[2,64,2048]{2,1,0:T(8,128)(2,1)S(1)} %collective-permute-done.3.refs_2_), channel_id=1, source_target_pairs={{0,16},{1,17},{2,18},{3,19},{4,20},{5,21},{6,22},{7,23},{8,24},{9,... | collective-permute-start | bytes 1572872 | tf_op jit(solution)/shard_map/ppermute | solution.py:60
  38.8 4.1 %collective-permute-start.8 = (bf16[2,64,2048]{2,1,0:T(8,128)(2,1)}, bf16[2,64,2048]{2,1,0:T(8,128)(2,1)}, u32[]{:S(2)}, u32[]{:S(2)}) collective-permute-start(bf16[2,64,2048]{2,1,0:T(8,128)(2,1)} %collective-permute-done.4.refs_3_), channel_id=1, source_target_pairs={{0,16},{1,17},{2,18},{3,19},{4,20},{5,21},{6,22},{7,23},{8,24},{9,... | collective-permute-start | bytes 1572872 | tf_op jit(solution)/shard_map/ppermute | solution.py:60
  88.2 5.4 %collective-permute-start.19 = (f32[256,1792]{1,0:T(8,128)S(1)}, f32[256,1792]{1,0:T(8,128)S(1)}, u32[]{:S(2)}, u32[]{:S(2)}) collective-permute-start(f32[256,1792]{1,0:T(8,128)S(1)} %get-tuple-element.43), channel_id=1, source_target_pairs={{0,16},{1,17},{2,18},{3,19},{4,20},{5,21},{6,22},{7,23},{8,24},{9,... | collective-permute-start | bytes 5505032 | tf_op jit(solution)/shard_map/ppermute | solution.py:60
  93.0 6.0 %collective-permute-start.23 = (f32[256,1792]{1,0:T(8,128)S(1)}, f32[256,1792]{1,0:T(8,128)S(1)}, u32[]{:S(2)}, u32[]{:S(2)}) collective-permute-start(f32[256,1792]{1,0:T(8,128)S(1)} %get-tuple-element.49), channel_id=1, source_target_pairs={{0,16},{1,17},{2,18},{3,19},{4,20},{5,21},{6,22},{7,23},{8,24},{9,... | collective-permute-start | bytes 5505032 | tf_op jit(solution)/shard_map/ppermute | solution.py:60
  95.6 14.7 %collective-permute-start.20 = (f32[16,4,1792]{2,1,0:T(4,128)S(1)}, f32[16,4,1792]{2,1,0:T(4,128)S(1)}, u32[]{:S(2)}, u32[]{:S(2)}) collective-permute-start(f32[16,4,1792]{2,1,0:T(4,128)S(1)} %get-tuple-element.45), channel_id=1, source_target_pairs={{0,4},{1,5},{2,6},{3,7},{4,8},{5,9},{6,10},{7,11},{8,12},{9,13},{1... | collective-permute-start | bytes 1376264 | tf_op jit(solution)/shard_map/ppermute | solution.py:529
  96.3 24.7 %collective-permute-start.21 = (f32[16,4,1792]{2,1,0:T(4,128)S(1)}, f32[16,4,1792]{2,1,0:T(4,128)S(1)}, u32[]{:S(2)}, u32[]{:S(2)}) collective-permute-start(f32[16,4,1792]{2,1,0:T(4,128)S(1)} %get-tuple-element.46), channel_id=1, source_target_pairs={{0,8},{1,9},{2,10},{3,11},{4,12},{5,13},{6,14},{7,15},{8,0},{9,1},... | collective-permute-start | bytes 1376264 | tf_op jit(solution)/shard_map/ppermute | solution.py:529
  97.5 23.4 %collective-permute-start.22 = (f32[16,4,1792]{2,1,0:T(4,128)S(1)}, f32[16,4,1792]{2,1,0:T(4,128)S(1)}, u32[]{:S(2)}, u32[]{:S(2)}) collective-permute-start(f32[16,4,1792]{2,1,0:T(4,128)S(1)} %get-tuple-element.47), channel_id=1, source_target_pairs={{0,12},{1,13},{2,14},{3,15},{4,0},{5,1},{6,2},{7,3},{8,4},{9,5},{1... | collective-permute-start | bytes 1376264 | tf_op jit(solution)/shard_map/ppermute | solution.py:529
  101.0 19.9 %collective-permute-start.24 = (f32[16,4,1792]{2,1,0:T(4,128)S(1)}, f32[16,4,1792]{2,1,0:T(4,128)S(1)}, u32[]{:S(2)}, u32[]{:S(2)}) collective-permute-start(f32[16,4,1792]{2,1,0:T(4,128)S(1)} %get-tuple-element.51), channel_id=1, source_target_pairs={{0,4},{1,5},{2,6},{3,7},{4,8},{5,9},{6,10},{7,11},{8,12},{9,13},{1... | collective-permute-start | bytes 1376264 | tf_op jit(solution)/shard_map/ppermute | solution.py:529
  101.8 19.1 %collective-permute-start.25 = (f32[16,4,1792]{2,1,0:T(4,128)S(1)}, f32[16,4,1792]{2,1,0:T(4,128)S(1)}, u32[]{:S(2)}, u32[]{:S(2)}) collective-permute-start(f32[16,4,1792]{2,1,0:T(4,128)S(1)} %get-tuple-element.52), channel_id=1, source_target_pairs={{0,8},{1,9},{2,10},{3,11},{4,12},{5,13},{6,14},{7,15},{8,0},{9,1},... | collective-permute-start | bytes 1376264 | tf_op jit(solution)/shard_map/ppermute | solution.py:529
  110.3 10.8 %collective-permute-start.26 = (f32[16,4,1792]{2,1,0:T(4,128)S(1)}, f32[16,4,1792]{2,1,0:T(4,128)S(1)}, u32[]{:S(2)}, u32[]{:S(2)}) collective-permute-start(f32[16,4,1792]{2,1,0:T(4,128)S(1)} %get-tuple-element.53), channel_id=1, source_target_pairs={{0,12},{1,13},{2,14},{3,15},{4,0},{5,1},{6,2},{7,3},{8,4},{9,5},{1... | collective-permute-start | bytes 1376264 | tf_op jit(solution)/shard_map/ppermute | solution.py:529
  122.1 18.5 %all-to-all-start.1 = ((f32[16,4,3584]{2,1,0:T(4,128)}), f32[16,4,3584]{2,1,0:T(4,128)S(1)}, u32[]{:S(2)}, u32[]{:S(2)}) async-start(f32[16,4,3584]{2,1,0:T(4,128)} %shard_map.101), calls=%async_computation.1 | async-start | bytes 1835008 | tf_op jit(solution)/shard_map/all_to_all | solution.py:559
  141.5 15.2 %all-to-all-start.2 = ((bf16[16,4,3584]{2,1,0:T(4,128)(2,1)}), bf16[16,4,3584]{2,1,0:T(4,128)(2,1)S(1)}, u32[]{:S(2)}, u32[]{:S(2)}) async-start(bf16[16,4,3584]{2,1,0:T(4,128)(2,1)} %shard_map.102), calls=%async_computation.2 | async-start | bytes 917504 | tf_op jit(solution)/shard_map/all_to_all | solution.py:569
  (18 other events, 239.5 us)
